TPU v7x, 32 devices: a whole 2x2x4 slice. The times are simulated.
32 devices in a mesh: section: 4 (over y, x), hid: 8 (over z, core).
Axes of the slice: x: 2, y: 2, z: 4, core: 2. Of those that a mesh axis runs over, the one named last changes fastest.
Arguments:
- layer_input: bfloat16 [4, 32, 4096], P('section', 'hid'), may hold values from -6 to 6
- hidden_grad: bfloat16 [4, 16, 7168], P('section', None, 'hid'), may hold values from -3 to 3
- gate_weight: bfloat16 [4, 4096, 7168], P('section', None, 'hid'), may hold values from -0.09375 to 0.09375
- up_weight: bfloat16 [4, 4096, 7168], P('section', None, 'hid'), may hold values from -0.09375 to 0.09375
- expert_ids: int32 [4, 32, 2], replicated, may hold values from 0 to 7, as said below
Outputs:
- grad_in: bfloat16 [4, 32, 4096], P('section', 'hid')
- grad_gate_weight: bfloat16 [4, 4096, 7168], P('section', None, 'hid')
Inputs may be any that keep to these rules, and one draw needn't show every extreme that they name: `expert_ids`: each token names two different experts. In every aligned block of 4 tokens of one section, between 1 and 2 tokens name expert 0; in one section every block has exactly 2.
All inputs are finite; a program needn't handle non-finite values.
Results may differ from a plain program's by a relative error of at most 0.0049.
Values may be sent and summed in bfloat16 or wider, within the bound.
No kernel may reach another device: no remote copies, remote signals or barrier semaphores. Data moves between devices by JAX's collectives and lax.ppermute only.
A program may use at most 64 MiB of HBM per device.

v0:
```python
import jax
import jax.numpy as jnp
from jax import lax
from jax.sharding import PartitionSpec as P


def shifted(value, axis, steps):
    count = lax.axis_size(axis)
    pairs = [(source, (source + steps) % count) for source in range(count)]
    return lax.ppermute(value, axis, pairs)


def own_table(ids, hid_at, tok_dev, k_dev):
    chosen = jnp.any(ids == 0, axis=1).astype(jnp.int32)
    local = lax.dynamic_slice_in_dim(chosen, hid_at * tok_dev, tok_dev, 0)
    slot_rank = jnp.cumsum(local) - local
    slot_iota = lax.broadcasted_iota(jnp.int32, (k_dev, tok_dev), 0)
    matches = (slot_rank[None, :] == slot_iota) & (local[None, :] == 1)
    return matches.astype(jnp.bfloat16)


def contract_last(left, right):
    return lax.dot_general(
        left, right, (((1,), (1,)), ((), ())), preferred_element_type=jnp.float32
    )


def contract_first(left, right):
    return lax.dot_general(
        left, right, (((0,), (0,)), ((), ())), preferred_element_type=jnp.float32
    )


def per_device(layer_input, hidden_grad, gate_weight, up_weight, expert_ids):
    tok_dev = layer_input.shape[1]
    k_dev = tok_dev // 2
    section_at = lax.axis_index("section")
    hid_at = lax.axis_index("hid")
    section_ids = lax.dynamic_index_in_dim(expert_ids, section_at, 0, keepdims=False)
    table = own_table(section_ids, hid_at, tok_dev, k_dev)
    packed = jnp.dot(table, layer_input[0], preferred_element_type=jnp.float32).astype(jnp.bfloat16)
    slot_rows = lax.all_gather(packed, "hid", axis=0, tiled=True)
    gate_local = gate_weight[0]
    up_local = up_weight[0]
    gate_act = jnp.dot(slot_rows, gate_local, preferred_element_type=jnp.float32)
    up_act = jnp.dot(slot_rows, up_local, preferred_element_type=jnp.float32)
    sigmoid_gate = jax.nn.sigmoid(gate_act)
    hidden_float = hidden_grad[0].astype(jnp.float32)
    grad_gate_act = (
        hidden_float * up_act * sigmoid_gate * (1.0 + gate_act * (1.0 - sigmoid_gate))
    ).astype(jnp.bfloat16)
    grad_up_act = (hidden_float * gate_act * sigmoid_gate).astype(jnp.bfloat16)
    summed = lax.psum_scatter(
        contract_last(grad_gate_act, gate_local) + contract_last(grad_up_act, up_local),
        "hid",
        scatter_dimension=0,
        tiled=True,
    )
    own_grad = summed.astype(jnp.bfloat16)
    token_grad = contract_first(table, own_grad).astype(jnp.bfloat16)
    passed = shifted(token_grad, "section", -1)
    weight_grad = contract_first(slot_rows, grad_gate_act).astype(jnp.bfloat16)
    return (passed[None], weight_grad[None])


def solution(mesh):
    return jax.shard_map(
        per_device,
        mesh=mesh,
        in_specs=(
            P("section", "hid", None),
            P("section", None, "hid"),
            P("section", None, "hid"),
            P("section", None, "hid"),
            P(),
        ),
        out_specs=(P("section", "hid", None), P("section", None, "hid")),
        check_vma=False,
    )
```

profile of v0, /device:TPU:0, one launch (start us, length us, event | category | flops | bytes accessed | tf_op | source)
XLA Modules:
  0.0 71.3 jit_solution(10365282643789886680)
XLA Ops:
  0.6 0.0 copy-start
  0.6 0.0 copy-start.2
  0.7 0.7 compare_reduce_fusion
  1.4 0.1 broadcast_compare_fusion
  1.5 0.1 dynamic-slice_bitcast_fusion
  1.5 0.2 reduce-window.9
  1.7 0.1 bitcast_subtract_fusion
  1.8 0.0 copy-done
  1.8 0.1 fusion.11
  1.9 15.7 %all-gather = bf16[8,2,4096]{2,1,0:T(2,128)(2,1)S(1)} all-gather(bf16[1,2,4096]{2,1,0:T(2,128)(2,1)S(1)} %fusion.11), channel_id=1, replica_groups=mesh['section'=4,'hid'=8] {'hid'}, dimensions={0}, use_global_device_ids=true | all-gather | bytes 147456 | tf_op jit(solution)/shard_map/all_gather | solution.py:42
  17.6 0.1 reshape.41
  17.7 0.0 copy-start.1
  17.7 0.0 slice-start
  17.7 4.3 %fusion.2 = f32[16,896]{1,0:T(8,128)S(1)} fusion(bf16[16,4096]{1,0:T(8,128)(2,1)S(1)} %reshape.41, bf16[1,4096,896]{2,1,0:T(8,128)(2,1)} %param.7), kind=kOutput, calls=%fused_computation.2 | convolution fusion | flops 117440512 | bytes 7528448 | tf_op jit(solution)/shard_map/dot_general | solution.py:45
  22.0 0.0 copy-done.2
  22.0 0.9 %copy-done.1 = bf16[1,4096,896]{2,1,0:T(8,128)(2,1)S(1)} copy-done((bf16[1,4096,896]{2,1,0:T(8,128)(2,1)S(1)}, bf16[1,4096,896]{2,1,0:T(8,128)(2,1)}, u32[]{:S(2)}) %copy-start.1) | copy-done | bytes 7340056
  22.9 0.0 slice-start.1
  22.9 1.1 %fusion.21 = bf16[16,896]{1,0:T(8,128)(2,1)S(1)} fusion(bf16[16,4096]{1,0:T(8,128)(2,1)S(1)} %reshape.41, bf16[1,4096,896]{2,1,0:T(8,128)(2,1)S(1)} %copy-done.1, f32[16,896]{1,0:T(8,128)S(1)} %fusion.2, bf16[1,16,896]{2,1,0:T(8,128)(2,1)S(1)} %copy-done.2), kind=kOutput, calls=%fused_computation.16 | convolution fusion | flops 117598208 | bytes 7585792 | tf_op jit(solution)/shard_map/dot_general | solution.py:46
  23.9 0.1 slice-done
  24.1 1.3 %slice-done.1 = s8[3145728]{0:T(1024)(128)(4,1)S(1)} async-done(((s8[7340032]{0:T(1024)(128)(4,1)}), s8[3145728]{0:T(1024)(128)(4,1)S(1)}, s32[]{:S(2)}) %slice-start.1) | async-done | bytes 3145752
  25.3 0.0 copy-start.3
  25.3 2.0 %fusion = f32[16,4096]{1,0:T(8,128)S(1)} fusion(bf16[16,896]{1,0:T(8,128)(2,1)S(1)} %fusion.21, bf16[1,4096,896]{2,1,0:T(8,128)(2,1)S(1)} %bitcast.46), kind=kOutput, calls=%fused_computation | convolution fusion | flops 117440512 | bytes 7630848 | tf_op jit(solution)/shard_map/dot_general | solution.py:23
  27.3 2.0 %fusion.8 = f32[16,4096]{1,0:T(8,128)S(1)} fusion(f32[16,4096]{1,0:T(8,128)S(1)} %fusion, bf16[1,4096,896]{2,1,0:T(8,128)(2,1)S(1)} %copy-done.1, f32[16,896]{1,0:T(8,128)S(1)} %fusion.2, bf16[1,16,896]{2,1,0:T(8,128)(2,1)S(1)} %copy-done.2), kind=kOutput, calls=%fused_computation.9 | convolution fusion | flops 117606400 | bytes 7950336 | tf_op jit(solution)/shard_map/dot_general | solution.py:23
  29.3 32.2 %all-reduce.2 = bf16[16,4096]{1,0:T(8,128)(2,1)S(1)} all-reduce(f32[16,4096]{1,0:T(8,128)S(1)} %fusion.8), channel_id=2, replica_groups=mesh['section'=4,'hid'=8] {'hid'}, use_global_device_ids=true, to_apply=%region_2.3.clone | all-reduce | flops 65536 | bytes 393216
  61.6 0.0 copy-done.3
  61.6 0.6 dynamic-slice
  62.8 0.2 convolution_convert_fusion
  63.0 2.5 %collective-permute-start = (bf16[4,4096]{1,0:T(4,128)(2,1)S(1)}, bf16[4,4096]{1,0:T(4,128)(2,1)S(1)}, u32[]{:S(2)}, u32[]{:S(2)}) collective-permute-start(bf16[4,4096]{1,0:T(4,128)(2,1)S(1)} %convolution_convert_fusion), channel_id=1, source_target_pairs={{0,24},{8,0},{16,8},{24,16},{1,25},{9,1},{17,9},{25,17},{2,26},{10... | collective-permute-start | bytes 98312 | tf_op jit(solution)/shard_map/ppermute | solution.py:10
  65.5 5.2 %convert_bitcast_fusion = bf16[1,4096,896]{2,1,0:T(8,128)(2,1)} fusion(bf16[16,4096]{1,0:T(8,128)(2,1)S(1)} %reshape.41, bf16[16,896]{1,0:T(8,128)(2,1)S(1)} %fusion.21), kind=kOutput, calls=%fused_computation.8 | convolution fusion | flops 121110528 | bytes 7499776 | tf_op jit(solution)/shard_map/dot_general | solution.py:29
  70.7 0.0 collective-permute-done
  70.7 0.6 copy.10
  (2 shorter events, 0.0 us)
Async XLA Ops:
  0.6 1.2 %copy-start = (bf16[1,4,4096]{2,1,0:T(4,128)(2,1)S(1)}, bf16[1,4,4096]{2,1,0:T(4,128)(2,1)}, u32[]{:S(2)}) copy-start(bf16[1,4,4096]{2,1,0:T(4,128)(2,1)} %param.5) | copy-start | bytes 98308
  0.6 21.4 %copy-start.2 = (bf16[1,16,896]{2,1,0:T(8,128)(2,1)S(1)}, bf16[1,16,896]{2,1,0:T(8,128)(2,1)}, u32[]{:S(2)}) copy-start(bf16[1,16,896]{2,1,0:T(8,128)(2,1)} %param.6) | copy-start | bytes 86020
  17.7 5.2 %copy-start.1 = (bf16[1,4096,896]{2,1,0:T(8,128)(2,1)S(1)}, bf16[1,4096,896]{2,1,0:T(8,128)(2,1)}, u32[]{:S(2)}) copy-start(bf16[1,4096,896]{2,1,0:T(8,128)(2,1)} %param.8) | copy-start | bytes 22020100
  17.7 6.4 %slice-start = ((s8[7340032]{0:T(1024)(128)(4,1)}), s8[4194304]{0:T(1024)(128)(4,1)S(1)}, s32[]{:S(2)}) async-start(s8[7340032]{0:T(1024)(128)(4,1)} %bitcast.45), calls=%async_computation | async-start | bytes 8388608
  22.9 2.5 %slice-start.1 = ((s8[7340032]{0:T(1024)(128)(4,1)}), s8[3145728]{0:T(1024)(128)(4,1)S(1)}, s32[]{:S(2)}) async-start(s8[7340032]{0:T(1024)(128)(4,1)} %bitcast.45), calls=%async_computation.1 | async-start | bytes 6291456
  25.3 36.2 %copy-start.3 = (u32[32]{0:T(128)S(1)}, u32[32]{0:T(128)}, u32[]{:S(2)}) copy-start(u32[32]{0:T(128)} %constant.34) | copy-start | bytes 388
  63.0 7.7 %collective-permute-start = (bf16[4,4096]{1,0:T(4,128)(2,1)S(1)}, bf16[4,4096]{1,0:T(4,128)(2,1)S(1)}, u32[]{:S(2)}, u32[]{:S(2)}) collective-permute-start(bf16[4,4096]{1,0:T(4,128)(2,1)S(1)} %convolution_convert_fusion), channel_id=1, source_target_pairs={{0,24},{8,0},{16,8},{24,16},{1,25},{9,1},{17,9},{25,17},{2,26},{10... | collective-permute-start | bytes 98312 | tf_op jit(solution)/shard_map/ppermute | solution.py:10
where the time goes:
time: 71.5 us; the launch traced here: 71.3 us
  blocking collectives  47.9 us (67%)
  matrix products  14.9 us (21%)
  local copies, waits for them, and re-layouts  3.59 us (5%)
  starting transfers between devices  2.5 us (3%)
  between operations  1.38 us (2%)
  other arithmetic  1.05 us (1%)
    unnamed x1, blocking collectives  32.2 us
    all_gather x1, blocking collectives, per_device(): slot_rows = lax.all_gather(packed, 'hid', axis=0, tiled=True)  15.7 us
    dot_general x2, matrix products, contract_first(): lax.dot_general(left, right, (((0,), (0,)), ((), ())), preferred_element_...  5.38 us
    dot_general x1, matrix products, per_device(): jnp.dot(slot_rows, gate_local, preferred_element_type=jnp.float32)  4.28 us
    dot_general x2, matrix products, contract_last(): lax.dot_general(left, right, (((1,), (1,)), ((), ())), preferred_element_...  4.01 us
    unnamed x15, local copies, waits for them, and re-layouts  3.52 us
    ppermute x1, starting transfers between devices, shifted(): return lax.ppermute(value, axis, pairs)  2.5 us
  transfers between devices with their start and end apart: 1, of which 0 were waited for; matrix products, arithmetic and copies ran while one was open for 7% of the time, Pallas kernels for 0%

commit v1 on v0

v1 whole, which is shorter than its diff:
```python
import functools

import jax
import jax.numpy as jnp
from jax import lax
from jax.experimental import pallas as pl
from jax.experimental.pallas import tpu as pltpu
from jax.sharding import PartitionSpec as P

F32 = jnp.float32
BF16 = jnp.bfloat16
CORES = 2
CHIPS = 4
VMEM = pl.BlockSpec(memory_space=pltpu.VMEM)
ANY = pl.BlockSpec(memory_space=pl.ANY)


def moved(value, target):
    sections, hids = lax.axis_size("section"), lax.axis_size("hid")
    pairs = []
    for section in range(sections):
        for hid in range(hids):
            to_section, to_hid = target(section, hid)
            pairs.append((section * hids + hid, (to_section % sections) * hids + to_hid))
    return lax.ppermute(value, ("section", "hid"), pairs)


def to_other_core(value):
    return moved(value, lambda section, hid: (section, hid ^ 1))


def expert_kernel(table_ref, hidden_ref, *refs, n_blocks, chunk):
    block_refs = refs[:n_blocks]
    gate_ref, up_ref, slots_ref, grad_gate_ref, keep_ref, send_ref = refs[n_blocks:]
    rows = jnp.concatenate([ref[...].astype(F32) for ref in block_refs], axis=0).astype(BF16)
    slots = jnp.dot(table_ref[...], rows, preferred_element_type=F32).astype(BF16)
    slots_ref[...] = slots
    cap, width = slots.shape
    hidden = gate_ref.shape[1]
    gate_act = jnp.zeros((cap, hidden), F32)
    up_act = jnp.zeros((cap, hidden), F32)
    for at in range(0, width, chunk):
        part = slots[:, at : at + chunk]
        gate_act += jnp.dot(part, gate_ref[at : at + chunk, :], preferred_element_type=F32)
        up_act += jnp.dot(part, up_ref[at : at + chunk, :], preferred_element_type=F32)
    sigmoid_gate = jax.nn.sigmoid(gate_act)
    hidden_float = hidden_ref[...].astype(F32)
    grad_gate = (
        hidden_float * up_act * sigmoid_gate * (1.0 + gate_act * (1.0 - sigmoid_gate))
    ).astype(BF16)
    grad_up = (hidden_float * gate_act * sigmoid_gate).astype(BF16)
    grad_gate_ref[...] = grad_gate
    half = cap // 2
    contract_last = (((1,), (1,)), ((), ()))
    for at in range(0, width, chunk):
        total = lax.dot_general(
            grad_gate, gate_ref[at : at + chunk, :], contract_last, preferred_element_type=F32
        ) + lax.dot_general(
            grad_up, up_ref[at : at + chunk, :], contract_last, preferred_element_type=F32
        )
        keep_ref[:, at : at + chunk] = total[:half]
        send_ref[:, at : at + chunk] = total[half:].astype(send_ref.dtype)


def expert(table, hidden_grad, blocks, gate, up, send_dtype):
    cap, hidden = hidden_grad.shape
    width = gate.shape[0]
    return pl.pallas_call(
        functools.partial(expert_kernel, n_blocks=len(blocks), chunk=512),
        out_shape=(
            jax.ShapeDtypeStruct((cap, width), BF16),
            jax.ShapeDtypeStruct((cap, hidden), BF16),
            jax.ShapeDtypeStruct((cap // 2, width), F32),
            jax.ShapeDtypeStruct((cap // 2, width), send_dtype),
        ),
        in_specs=[VMEM] * (4 + len(blocks)),
        out_specs=(VMEM,) * 4,
        compiler_params=pltpu.CompilerParams(vmem_limit_bytes=44 << 20),
        cost_estimate=pl.CostEstimate(
            flops=8 * cap * width * hidden, bytes_accessed=4 * width * hidden, transcendentals=cap * hidden
        ),
        name="expert",
    )(table, hidden_grad, *blocks, gate, up)


def weight_kernel(slots_ref, grad_ref, out_ref):
    out_ref[...] = lax.dot_general(
        slots_ref[...], grad_ref[...], (((0,), (0,)), ((), ())), preferred_element_type=F32
    ).astype(out_ref.dtype)


def weight_gradient(slots, grad_gate):
    cap, width = slots.shape
    hidden = grad_gate.shape[1]
    chunk = 512
    return pl.pallas_call(
        weight_kernel,
        out_shape=jax.ShapeDtypeStruct((width, hidden), BF16),
        grid=(width // chunk,),
        in_specs=[
            pl.BlockSpec((cap, chunk), lambda i: (0, i)),
            pl.BlockSpec((cap, hidden), lambda i: (0, 0)),
        ],
        out_specs=pl.BlockSpec((chunk, hidden), lambda i: (i, 0)),
        compiler_params=pltpu.CompilerParams(vmem_limit_bytes=16 << 20),
        cost_estimate=pl.CostEstimate(
            flops=2 * cap * width * hidden, bytes_accessed=2 * width * hidden, transcendentals=0
        ),
        name="weight_gradient",
    )(slots, grad_gate)


def slot_numbers(ids, tok_dev, k_dev):
    chosen = jnp.any(ids == 0, axis=1)
    blocks = chosen.reshape(-1, tok_dev).astype(jnp.int32)
    ranks = [jnp.zeros_like(blocks[:, 0])]
    for at in range(tok_dev - 1):
        ranks.append(ranks[-1] + blocks[:, at])
    rank = jnp.stack(ranks, axis=1).reshape(-1)
    owner = lax.broadcasted_iota(jnp.int32, rank.shape, 0) // tok_dev
    return jnp.where(chosen, owner * k_dev + rank, -1)


def permuted_table(slot_of, slot_ids, token_ids):
    tokens = lax.broadcasted_iota(jnp.int32, (1, slot_of.shape[0]), 1)
    picked = jnp.sum(jnp.where(token_ids[:, None] == tokens, slot_of[None, :], 0), axis=1)
    return (slot_ids[:, None] == picked[None, :]).astype(BF16)


def own_rows(slot_of, hid_at, tok_dev, k_dev, grads):
    token = lax.broadcasted_iota(jnp.int32, (tok_dev, 1), 0) + hid_at * tok_dev
    tokens = lax.broadcasted_iota(jnp.int32, (1, slot_of.shape[0]), 1)
    slot = jnp.sum(jnp.where(token == tokens, slot_of[None, :], 0), axis=1, keepdims=True)
    rows = jnp.zeros((tok_dev, grads.shape[1]), grads.dtype)
    for rank in range(k_dev):
        rows = jnp.where(slot == hid_at * k_dev + rank, grads[rank : rank + 1], rows)
    return rows


def per_device(layer_input, hidden_grad, gate_weight, up_weight, expert_ids):
    tok_dev = layer_input.shape[1]
    k_dev = tok_dev // 2
    section_at = lax.axis_index("section")
    hid_at = lax.axis_index("hid")
    sections, hids = lax.axis_size("section"), lax.axis_size("hid")
    split = hids == CORES * CHIPS
    core_at, chip_at = hid_at % CORES, hid_at // CORES
    own = layer_input[0]

    place = lax.broadcasted_iota(jnp.int32, (hids * tok_dev,), 0)
    device, token = place // tok_dev, place % tok_dev
    if split:
        other = to_other_core(own)
        near = moved(own, lambda section, hid: (section, hid ^ 2))
        both = jnp.concatenate([own, other], axis=0)
        far = moved(both, lambda section, hid: (section, hid ^ (4 if hid % CORES else 6)))
        near_other = to_other_core(near)
        far_other = to_other_core(far)
        blocks = [own, other, near, near_other, far, far_other]
        turn = jnp.where(device < 4, device, jnp.where(device < 6, device ^ 2, device ^ 3) ^ (2 * core_at))
        device = hid_at ^ turn
    else:
        blocks = [lax.all_gather(own, "hid", axis=0, tiled=True)]
    token_ids = device * tok_dev + token

    place = lax.broadcasted_iota(jnp.int32, (hids * k_dev,), 0)
    device, rank = place // k_dev, place % k_dev
    if split:
        quarter = device // CORES
        step = jnp.where(quarter < 2, core_at, 1 - core_at) + 2 * (quarter % 2)
        device = (chip_at ^ step) * CORES + device % CORES
    slot_ids = device * k_dev + rank

    ids = lax.dynamic_index_in_dim(expert_ids, section_at, 0, keepdims=False)
    table = permuted_table(slot_numbers(ids, tok_dev, k_dev), slot_ids, token_ids)
    slots_iota = lax.broadcasted_iota(jnp.int32, (1, hids * k_dev), 1)
    order = (slot_ids[:, None] == slots_iota).astype(BF16)
    hidden_ordered = jnp.dot(order, hidden_grad[0], preferred_element_type=F32).astype(BF16)

    slots, grad_gate, keep, send = expert(
        table, hidden_ordered, blocks, gate_weight[0], up_weight[0], BF16 if split else F32
    )

    next_ids = lax.dynamic_index_in_dim(expert_ids, (section_at + 1) % sections, 0, keepdims=False)
    if split:
        rows = keep.shape[0] // 2
        keep = keep + to_other_core(send).astype(F32)
        across = moved(keep[rows:].astype(BF16), lambda section, hid: (section, hid ^ 4))
        part = (keep[:rows] + across.astype(F32)).astype(BF16)
        part = moved(part, lambda section, hid: (section - 1, hid ^ (2 * (hid % CORES))))
        total = part.astype(F32) + to_other_core(part).astype(F32)
        own_total = jnp.where(core_at == 0, total[: rows // 2], total[rows // 2 :])
    else:
        whole = jnp.concatenate([keep, send], axis=0)
        own_total = lax.psum_scatter(whole, "hid", scatter_dimension=0, tiled=True)
        own_total = moved(own_total, lambda section, hid: (section - 1, hid))
    grad_in = own_rows(slot_numbers(next_ids, tok_dev, k_dev), hid_at, tok_dev, k_dev, own_total).astype(BF16)
    weight_grad = weight_gradient(slots, grad_gate)
    return (grad_in[None], weight_grad[None])


def solution(mesh):
    return jax.shard_map(
        per_device,
        mesh=mesh,
        in_specs=(
            P("section", "hid", None),
            P("section", None, "hid"),
            P("section", None, "hid"),
            P("section", None, "hid"),
            P(),
        ),
        out_specs=(P("section", "hid", None), P("section", None, "hid")),
        check_vma=False,
    )
```

time: 71.5 us -> 43.8 us (0.61)
  blocking collectives: 47.9 us -> 0 us
  Pallas kernels: 0 us -> 14.9 us
  matrix products: 14.9 us -> 0.19 us
  starting transfers between devices: 2.5 us -> 11.5 us
  waiting for transfers between devices: 0.01 us -> 8.91 us
  other arithmetic: 1.05 us -> 3.01 us
    unnamed x1 -> x0, blocking collectives: 32.2 us -> none
    all_gather x1 -> x0, blocking collectives: 15.7 us -> none  [per_device(): slot_rows = lax.all_gather(packed, 'hid', axis=0, tiled=True)]
    pallas_call x0 -> x2, Pallas kernels: none -> 14.9 us  [the longest x1 8.98 us: expert(): pl.pallas_call(functools.partial(expert_kernel, n_blocks=len(blocks), chu...]
    dot_general x7 -> x1, matrix products: 14.9 us -> 0.19 us  [per_device(): jnp.dot(order, hidden_grad[0], preferred_element_type=F32).astype(BF16)]
    ppermute x1 -> x9, starting transfers between devices: 2.5 us -> 11.5 us  [moved(): return lax.ppermute(value, ('section', 'hid'), pairs)]
    ppermute x1 -> x9, waiting for transfers between devices: 0.01 us -> 8.91 us  [moved(): return lax.ppermute(value, ('section', 'hid'), pairs)]
    concatenate x0 -> x1, other arithmetic: none -> 0.8 us  [per_device(): both = jnp.concatenate([own, other], axis=0)]
    convert_element_type x1 -> x5, other arithmetic: 0.01 us -> 0.8 us  [the longest x1 0.7 us: per_device(): own_rows(slot_numbers(next_ids, tok_dev, k_dev), hid_at, tok_dev, k_dev,...]
  transfers between devices with their start and end apart: 1 -> 9, of which waited for: 0 -> 5; matrix products, arithmetic and copies ran while one was open for 7% -> 6% of each run, Pallas kernels for 0% -> 14%
where the time goes in v1:
time: 43.8 us; the launch traced here: 43.4 us
  Pallas kernels  14.9 us (34%)
  starting transfers between devices  11.5 us (26%)
  waiting for transfers between devices  8.91 us (20%)
  local copies, waits for them, and re-layouts  4.24 us (10%)
  other arithmetic  3.01 us (7%)
  between operations  0.74 us (2%)
    ppermute x9, starting transfers between devices, moved(): return lax.ppermute(value, ('section', 'hid'), pairs)  11.5 us
    pallas_call x1, Pallas kernels, expert(): pl.pallas_call(functools.partial(expert_kernel, n_blocks=len(blocks), chu...  8.98 us
    ppermute x9, waiting for transfers between devices, moved(): return lax.ppermute(value, ('section', 'hid'), pairs)  8.91 us
    pallas_call x1, Pallas kernels, weight_gradient(): pl.pallas_call(weight_kernel, out_shape=jax.ShapeDtypeStruct((width, hidd...  5.89 us
    unnamed x6, local copies, waits for them, and re-layouts  3.87 us
  transfers between devices with their start and end apart: 9, of which 5 were waited for; matrix products, arithmetic and copies ran while one was open for 6% of the time, Pallas kernels for 14%

profile of v1, /device:TPU:0, one launch (start us, length us, event | category | flops | bytes accessed | tf_op | source)
XLA Modules:
  0.0 43.4 jit_solution(13899967374596430638)
XLA Ops:
  0.6 0.0 copy-start
  0.6 3.1 %collective-permute-start.1 = (bf16[4,4096]{1,0:T(4,128)(2,1)}, bf16[4,4096]{1,0:T(4,128)(2,1)S(1)}, u32[]{:S(2)}, u32[]{:S(2)}) collective-permute-start(bf16[4,4096]{1,0:T(4,128)(2,1)} %bitcast.11), channel_id=1, source_target_pairs={{0,2},{1,3},{2,0},{3,1},{4,6},{5,7},{6,4},{7,5},{8,10},{9,11},{10,... | collective-permute-start | bytes 98312 | tf_op jit(solution)/shard_map/ppermute | solution.py:25
  3.7 0.0 collective-permute-start
  3.7 0.7 %compare_reduce_fusion.1 = (pred[32]{0:T(512)(128)(4,1)S(1)}, pred[32]{0:T(512)(128)(4,1)S(1)}) fusion(s32[4,32,2]{1,2,0:T(2,128)} %param.9, s32[]{:T(128)S(6)} %select_n.181, s32[]{:T(128)S(6)} %select_n.197), kind=kLoop, calls=%fused_computation.36 | loop fusion | flops 192 | bytes 584 | tf_op jit(solution)/shard_map/reduce_or | solution.py:114
  4.5 0.1 reshape.262
  4.6 0.1 reshape.261
  4.6 0.1 slice_add_fusion.3
  4.7 0.1 slice_add_fusion.1
  4.8 0.1 pad_add_fusion
  4.9 0.1 reshape.260
  5.0 0.0 copy-done
  5.0 0.2 convolution_convert_fusion.hidden_ref
  5.2 0.0 collective-permute-done.refs_1_
  5.2 0.8 %pad_maximum_fusion = bf16[8,4096]{1,0:T(8,128)(2,1)S(1)} fusion(bf16[4,4096]{1,0:T(4,128)(2,1)S(1)} %collective-permute-done.refs_1_, bf16[4,4096]{1,0:T(4,128)(2,1)} %bitcast.13), kind=kLoop, calls=%fused_computation.5 | loop fusion | flops 131072 | bytes 131072 | tf_op jit(solution)/shard_map/concatenate | solution.py:155
  6.0 2.5 %collective-permute-start.3 = (bf16[8,4096]{1,0:T(8,128)(2,1)S(1)}, bf16[8,4096]{1,0:T(8,128)(2,1)S(1)}, u32[]{:S(2)}, u32[]{:S(2)}) collective-permute-start(bf16[8,4096]{1,0:T(8,128)(2,1)S(1)} %pad_maximum_fusion), channel_id=1, source_target_pairs={{0,6},{1,5},{2,4},{3,7},{4,2},{5,1},{6,0},{7,3},{8,14},{9,13},{10,... | collective-permute-start | bytes 196616 | tf_op jit(solution)/shard_map/ppermute | solution.py:25
  8.6 0.2 select_reduce_fusion
  8.7 0.0 collective-permute-done.1.refs_2_
  8.7 0.4 collective-permute-start.2
  9.1 3.1 %collective-permute-done.3.refs_4_ = bf16[8,4096]{1,0:T(8,128)(2,1)S(1)} collective-permute-done((bf16[8,4096]{1,0:T(8,128)(2,1)S(1)}, bf16[8,4096]{1,0:T(8,128)(2,1)S(1)}, u32[]{:S(2)}, u32[]{:S(2)}) %collective-permute-start.3) | collective-permute-done | bytes 65568 | tf_op jit(solution)/shard_map/ppermute | solution.py:25
  12.2 0.3 collective-permute-start.4
  12.5 0.1 compare_convert_fusion.table_ref
  12.6 0.1 reshape.259
  12.7 0.0 collective-permute-done.2.refs_3_
  12.7 0.8 %collective-permute-done.4.refs_5_ = bf16[8,4096]{1,0:T(8,128)(2,1)S(1)} collective-permute-done((bf16[8,4096]{1,0:T(8,128)(2,1)S(1)}, bf16[8,4096]{1,0:T(8,128)(2,1)S(1)}, u32[]{:S(2)}, u32[]{:S(2)}) %collective-permute-start.4) | collective-permute-done | bytes 65568 | tf_op jit(solution)/shard_map/ppermute | solution.py:25
  13.5 0.0 copy-start.1
  13.5 3.1 %copy-done.1 = bf16[1,4096,896]{2,1,0:T(8,128)(2,1)S(1)} copy-done((bf16[1,4096,896]{2,1,0:T(8,128)(2,1)S(1)}, bf16[1,4096,896]{2,1,0:T(8,128)(2,1)}, u32[]{:S(2)}) %copy-start.1) | copy-done | bytes 7340056
  16.6 0.0 copy-start.2
  16.6 0.8 %copy-done.2 = bf16[1,4,4096]{2,1,0:T(4,128)(2,1)S(1)} copy-done((bf16[1,4,4096]{2,1,0:T(4,128)(2,1)S(1)}, bf16[1,4,4096]{2,1,0:T(4,128)(2,1)}, u32[]{:S(2)}) %copy-start.2) | copy-done | bytes 32792
  17.4 9.0 %expert.1 = (bf16[16,4096]{1,0:T(8,128)(2,1)S(1)}, bf16[16,896]{1,0:T(8,128)(2,1)S(1)}, f32[8,4096]{1,0:T(8,128)S(1)}, bf16[8,4096]{1,0:T(8,128)(2,1)S(1)}) custom-call(bf16[16,32]{1,0:T(8,128)(2,1)S(1)} %compare_convert_fusion.table_ref, bf16[16,896]{1,0:T(8,128)(2,1)S(1)} %convolution_convert_fusion.hidden_ref, bf16[4,4096]{1,0:T(4,128)(2,1)S(1)} %bitcast.14, ...), custom_call_target="tpu_custom_call" | custom-call | flops 469762048 | bytes 14680064 | tf_op jit(solution)/shard_map/expert/pallas_call | solution.py:68
  26.3 0.3 collective-permute-start.5
  26.7 1.0 %collective-permute-done.5 = bf16[8,4096]{1,0:T(8,128)(2,1)S(1)} collective-permute-done((bf16[8,4096]{1,0:T(8,128)(2,1)S(1)}, bf16[8,4096]{1,0:T(8,128)(2,1)S(1)}, u32[]{:S(2)}, u32[]{:S(2)}) %collective-permute-start.5) | collective-permute-done | bytes 65568 | tf_op jit(solution)/shard_map/ppermute | solution.py:25
  27.7 2.3 %collective-permute-start.6 = (bf16[4,4096]{1,0:T(4,128)(2,1)S(1)}, bf16[4,4096]{1,0:T(4,128)(2,1)S(1)}, u32[]{:S(2)}, u32[]{:S(2)}) collective-permute-start(bf16[4,4096]{1,0:T(4,128)(2,1)S(1)} %slice.67), channel_id=1, source_target_pairs={{0,4},{1,5},{2,6},{3,7},{4,0},{5,1},{6,2},{7,3},{8,12},{9,13},{10,... | collective-permute-start | bytes 98312 | tf_op jit(solution)/shard_map/ppermute | solution.py:25
  30.0 2.6 %collective-permute-done.6 = bf16[4,4096]{1,0:T(4,128)(2,1)S(1)} collective-permute-done((bf16[4,4096]{1,0:T(4,128)(2,1)S(1)}, bf16[4,4096]{1,0:T(4,128)(2,1)S(1)}, u32[]{:S(2)}, u32[]{:S(2)}) %collective-permute-start.6) | collective-permute-done | bytes 32800 | tf_op jit(solution)/shard_map/ppermute | solution.py:25
  32.6 2.5 %collective-permute-start.7 = (bf16[4,4096]{1,0:T(4,128)(2,1)S(1)}, bf16[4,4096]{1,0:T(4,128)(2,1)S(1)}, u32[]{:S(2)}, u32[]{:S(2)}) collective-permute-start(bf16[4,4096]{1,0:T(4,128)(2,1)S(1)} %fusion), channel_id=1, source_target_pairs={{0,24},{1,27},{2,26},{3,25},{4,28},{5,31},{6,30},{7,29},{8,0},{9,3... | collective-permute-start | bytes 98312 | tf_op jit(solution)/shard_map/ppermute | solution.py:25
  35.1 0.2 select_reduce_fusion.1
  35.3 1.4 %collective-permute-done.7 = bf16[4,4096]{1,0:T(4,128)(2,1)S(1)} collective-permute-done((bf16[4,4096]{1,0:T(4,128)(2,1)S(1)}, bf16[4,4096]{1,0:T(4,128)(2,1)S(1)}, u32[]{:S(2)}, u32[]{:S(2)}) %collective-permute-start.7) | collective-permute-done | bytes 32800 | tf_op jit(solution)/shard_map/ppermute | solution.py:25
  36.7 0.0 collective-permute-start.8
  36.7 5.9 %weight_gradient.1 = bf16[4096,896]{1,0:T(8,128)(2,1)} custom-call(bf16[16,4096]{1,0:T(8,128)(2,1)S(1)} %get-tuple-element.8.slots_ref, bf16[16,896]{1,0:T(8,128)(2,1)S(1)} %get-tuple-element.9.grad_ref), custom_call_target="tpu_custom_call" | custom-call | flops 117440512 | bytes 7340032 | tf_op jit(solution)/shard_map/weight_gradient/pallas_call | solution.py:96
  42.6 0.0 collective-permute-done.8
  42.7 0.7 %select_convert_fusion = bf16[1,4,4096]{2,1,0:T(4,128)(2,1)} fusion(f32[4096]{0:T(1024)S(1)} %bitcast.18, f32[4096]{0:T(1024)S(1)} %bitcast.17, pred[4]{0:T(512)(128)(4,1)S(1)} %get-tuple-element.21, pred[4]{0:T(512)(128)(4,1)S(1)} %get-tuple-element.20), kind=kLoop, calls=%fused_computation.6 | loop fusion | flops 32768 | bytes 65544 | tf_op jit(solution)/shard_map/convert_element_type | solution.py:197
  (14 shorter events, 0.2 us)
Async XLA Ops:
  0.6 4.4 %copy-start = (bf16[1,16,896]{2,1,0:T(8,128)(2,1)S(1)}, bf16[1,16,896]{2,1,0:T(8,128)(2,1)}, u32[]{:S(2)}) copy-start(bf16[1,16,896]{2,1,0:T(8,128)(2,1)} %param.6) | copy-start | bytes 86020
  0.6 8.1 %collective-permute-start.1 = (bf16[4,4096]{1,0:T(4,128)(2,1)}, bf16[4,4096]{1,0:T(4,128)(2,1)S(1)}, u32[]{:S(2)}, u32[]{:S(2)}) collective-permute-start(bf16[4,4096]{1,0:T(4,128)(2,1)} %bitcast.11), channel_id=1, source_target_pairs={{0,2},{1,3},{2,0},{3,1},{4,6},{5,7},{6,4},{7,5},{8,10},{9,11},{10,... | collective-permute-start | bytes 98312 | tf_op jit(solution)/shard_map/ppermute | solution.py:25
  3.7 1.5 %collective-permute-start = (bf16[4,4096]{1,0:T(4,128)(2,1)}, bf16[4,4096]{1,0:T(4,128)(2,1)S(1)}, u32[]{:S(2)}, u32[]{:S(2)}) collective-permute-start(bf16[4,4096]{1,0:T(4,128)(2,1)} %bitcast.12), channel_id=1, source_target_pairs={{0,1},{1,0},{2,3},{3,2},{4,5},{5,4},{6,7},{7,6},{8,9},{9,8},{10,11... | collective-permute-start | bytes 98312 | tf_op jit(solution)/shard_map/ppermute | solution.py:25
  6.0 6.2 %collective-permute-start.3 = (bf16[8,4096]{1,0:T(8,128)(2,1)S(1)}, bf16[8,4096]{1,0:T(8,128)(2,1)S(1)}, u32[]{:S(2)}, u32[]{:S(2)}) collective-permute-start(bf16[8,4096]{1,0:T(8,128)(2,1)S(1)} %pad_maximum_fusion), channel_id=1, source_target_pairs={{0,6},{1,5},{2,4},{3,7},{4,2},{5,1},{6,0},{7,3},{8,14},{9,13},{10,... | collective-permute-start | bytes 196616 | tf_op jit(solution)/shard_map/ppermute | solution.py:25
  8.7 3.9 %collective-permute-start.2 = (bf16[4,4096]{1,0:T(4,128)(2,1)S(1)}, bf16[4,4096]{1,0:T(4,128)(2,1)S(1)}, u32[]{:S(2)}, u32[]{:S(2)}) collective-permute-start(bf16[4,4096]{1,0:T(4,128)(2,1)S(1)} %collective-permute-done.1.refs_2_), channel_id=1, source_target_pairs={{0,1},{1,0},{2,3},{3,2},{4,5},{5,4},{6,7},{7,6},{8,9},{9,8},{10,11... | collective-permute-start | bytes 98312 | tf_op jit(solution)/shard_map/ppermute | solution.py:25
  12.2 1.3 %collective-permute-start.4 = (bf16[8,4096]{1,0:T(8,128)(2,1)S(1)}, bf16[8,4096]{1,0:T(8,128)(2,1)S(1)}, u32[]{:S(2)}, u32[]{:S(2)}) collective-permute-start(bf16[8,4096]{1,0:T(8,128)(2,1)S(1)} %collective-permute-done.3.refs_4_), channel_id=1, source_target_pairs={{0,1},{1,0},{2,3},{3,2},{4,5},{5,4},{6,7},{7,6},{8,9},{9,8},{10,11... | collective-permute-start | bytes 196616 | tf_op jit(solution)/shard_map/ppermute | solution.py:25
  13.5 3.1 %copy-start.1 = (bf16[1,4096,896]{2,1,0:T(8,128)(2,1)S(1)}, bf16[1,4096,896]{2,1,0:T(8,128)(2,1)}, u32[]{:S(2)}) copy-start(bf16[1,4096,896]{2,1,0:T(8,128)(2,1)} %param.7) | copy-start | bytes 22020100
  16.6 0.8 %copy-start.2 = (bf16[1,4,4096]{2,1,0:T(4,128)(2,1)S(1)}, bf16[1,4,4096]{2,1,0:T(4,128)(2,1)}, u32[]{:S(2)}) copy-start(bf16[1,4,4096]{2,1,0:T(4,128)(2,1)} %param.5) | copy-start | bytes 98308
  26.3 1.3 %collective-permute-start.5 = (bf16[8,4096]{1,0:T(8,128)(2,1)S(1)}, bf16[8,4096]{1,0:T(8,128)(2,1)S(1)}, u32[]{:S(2)}, u32[]{:S(2)}) collective-permute-start(bf16[8,4096]{1,0:T(8,128)(2,1)S(1)} %get-tuple-element.7), channel_id=1, source_target_pairs={{0,1},{1,0},{2,3},{3,2},{4,5},{5,4},{6,7},{7,6},{8,9},{9,8},{10,11... | collective-permute-start | bytes 196616 | tf_op jit(solution)/shard_map/ppermute | solution.py:25
  27.7 4.9 %collective-permute-start.6 = (bf16[4,4096]{1,0:T(4,128)(2,1)S(1)}, bf16[4,4096]{1,0:T(4,128)(2,1)S(1)}, u32[]{:S(2)}, u32[]{:S(2)}) collective-permute-start(bf16[4,4096]{1,0:T(4,128)(2,1)S(1)} %slice.67), channel_id=1, source_target_pairs={{0,4},{1,5},{2,6},{3,7},{4,0},{5,1},{6,2},{7,3},{8,12},{9,13},{10,... | collective-permute-start | bytes 98312 | tf_op jit(solution)/shard_map/ppermute | solution.py:25
  32.6 4.1 %collective-permute-start.7 = (bf16[4,4096]{1,0:T(4,128)(2,1)S(1)}, bf16[4,4096]{1,0:T(4,128)(2,1)S(1)}, u32[]{:S(2)}, u32[]{:S(2)}) collective-permute-start(bf16[4,4096]{1,0:T(4,128)(2,1)S(1)} %fusion), channel_id=1, source_target_pairs={{0,24},{1,27},{2,26},{3,25},{4,28},{5,31},{6,30},{7,29},{8,0},{9,3... | collective-permute-start | bytes 98312 | tf_op jit(solution)/shard_map/ppermute | solution.py:25
  36.7 5.9 %collective-permute-start.8 = (bf16[4,4096]{1,0:T(4,128)(2,1)S(1)}, bf16[4,4096]{1,0:T(4,128)(2,1)S(1)}, u32[]{:S(2)}, u32[]{:S(2)}) collective-permute-start(bf16[4,4096]{1,0:T(4,128)(2,1)S(1)} %collective-permute-done.7), channel_id=1, source_target_pairs={{0,1},{1,0},{2,3},{3,2},{4,5},{5,4},{6,7},{7,6},{8,9},{9,8},{10,11... | collective-permute-start | bytes 98312 | tf_op jit(solution)/shard_map/ppermute | solution.py:25

commit v2 on v1

v2 whole, which is shorter than its diff:
```python
import functools

import jax
import jax.numpy as jnp
from jax import lax
from jax.experimental import pallas as pl
from jax.experimental.pallas import tpu as pltpu
from jax.sharding import PartitionSpec as P

F32 = jnp.float32
BF16 = jnp.bfloat16
CORES = 2
CHIPS = 4
VMEM = pl.BlockSpec(memory_space=pltpu.VMEM)
HBM = pl.BlockSpec(memory_space=pltpu.HBM)
ANY = pl.BlockSpec(memory_space=pl.ANY)


def moved(value, target):
    sections, hids = lax.axis_size("section"), lax.axis_size("hid")
    pairs = []
    for section in range(sections):
        for hid in range(hids):
            to_section, to_hid = target(section, hid)
            pairs.append((section * hids + hid, (to_section % sections) * hids + to_hid))
    return lax.ppermute(value, ("section", "hid"), pairs)


def to_other_core(value):
    return moved(value, lambda section, hid: (section, hid ^ 1))


def lanes(shape, dimension=1):
    return lax.broadcasted_iota(jnp.int32, shape, dimension)


def slot_row(ids_ref, section, tok_dev, k_dev):
    ids = ids_ref[pl.ds(section, 1)][0]
    tokens = ids.shape[1]
    chosen = jnp.where((ids[0:1] == 0) | (ids[1:2] == 0), 1.0, 0.0)
    chosen = jnp.broadcast_to(chosen, (8, tokens))
    before, after = lanes((tokens, tokens), 0), lanes((tokens, tokens), 1)
    earlier = jnp.where((before // tok_dev == after // tok_dev) & (before < after), 1.0, 0.0)
    rank = jnp.dot(chosen.astype(BF16), earlier.astype(BF16), preferred_element_type=F32)
    owner = (lanes((8, tokens)) // tok_dev).astype(F32)
    return jnp.where(chosen > 0, owner * k_dev + rank, -1.0)


def slot_at(slot_of, token):
    tokens = slot_of.shape[1]
    place = jnp.where(lanes((tokens, token.shape[1]), 0) == token, 1.0, 0.0).astype(BF16)
    return jnp.dot(slot_of.astype(BF16), place, preferred_element_type=F32)[0:1]


def pack_kernel(ids_ref, own_ref, other_ref, after_ref, out_ref, *, tok_dev, k_dev):
    del after_ref
    hid_at = lax.axis_index("hid")
    slot_of = slot_row(ids_ref, lax.axis_index("section"), tok_dev, k_dev)
    column = lanes((1, 2 * tok_dev))
    slots = slot_at(slot_of, (hid_at ^ (column // tok_dev)) * tok_dev + column % tok_dev)
    row = lanes((2 * k_dev, 1), 0)
    wanted = (hid_at ^ (row // k_dev)) * k_dev + row % k_dev
    table = jnp.where(wanted.astype(F32) == slots, 1.0, 0.0).astype(BF16)
    rows = jnp.concatenate([own_ref[...].astype(F32), other_ref[...].astype(F32)], axis=0)
    out_ref[...] = jnp.dot(table, rows.astype(BF16), preferred_element_type=F32).astype(BF16)


def pack(ids, own, other, after, k_dev):
    tok_dev, width = own.shape
    return pl.pallas_call(
        functools.partial(pack_kernel, tok_dev=tok_dev, k_dev=k_dev),
        out_shape=jax.ShapeDtypeStruct((2 * k_dev, width), BF16),
        in_specs=[VMEM] * 3 + [ANY],
        out_specs=VMEM,
        compiler_params=pltpu.CompilerParams(vmem_limit_bytes=4 << 20),
        name="pack",
    )(ids, own, other, after)


def open_kernel(out_ref):
    out_ref[...] = jnp.zeros_like(out_ref)


def opening(weight_bytes):
    return pl.pallas_call(
        open_kernel,
        out_shape=jax.ShapeDtypeStruct((8, 128), F32),
        out_specs=VMEM,
        compiler_params=pltpu.CompilerParams(vmem_limit_bytes=1 << 20),
        cost_estimate=pl.CostEstimate(flops=1000 * weight_bytes, bytes_accessed=2 * weight_bytes, transcendentals=0),
        name="opening",
    )()


def prepare_kernel(ids_ref, hidden_ref, after_ref, table_ref, hidden_out_ref, pick_ref, *, tok_dev, k_dev, split):
    del after_ref
    section_at, hid_at = lax.axis_index("section"), lax.axis_index("hid")
    core_at, chip_at = hid_at % CORES, hid_at // CORES
    cap, columns = table_ref.shape

    row = lanes((cap, 1), 0)
    device, rank = row // k_dev, row % k_dev
    if split:
        quarter = device // CORES
        step = 2 * jnp.where(quarter < 2, core_at, 1 - core_at) + quarter % 2
        device = (chip_at ^ step) * CORES + device % CORES
    wanted = device * k_dev + rank

    slot_of = slot_row(ids_ref, section_at, tok_dev, k_dev)
    column = lanes((1, columns))
    group, place = column // tok_dev, column % tok_dev
    if split:
        slots = slot_at(slot_of, (hid_at ^ (group + 1)) * tok_dev + place)
        turn = jnp.where(group == 0, 0, jnp.where(group == 3, 6 - 2 * core_at, 5 + 2 * core_at))
        packed = (hid_at ^ turn ^ (place // k_dev)) * k_dev + place % k_dev
        slots = jnp.where((group == 1) | (group == 2), slots, packed.astype(F32))
    else:
        slots = slot_at(slot_of, column)
    table_ref[...] = jnp.where(wanted.astype(F32) == slots, 1.0, 0.0).astype(BF16)

    order = jnp.where(wanted == lanes((cap, cap)), 1.0, 0.0).astype(BF16)
    hidden_out_ref[...] = jnp.dot(order, hidden_ref[...], preferred_element_type=F32).astype(BF16)

    sections = ids_ref.shape[0]
    slot_of = slot_row(ids_ref, (section_at + 1) % sections, tok_dev, k_dev)[0:1]
    token = lanes((tok_dev, slot_of.shape[1]), 0) + hid_at * tok_dev
    mine = jnp.where(lanes(token.shape) == token, slot_of, 0.0)
    mine = jnp.sum(mine, axis=1, keepdims=True) - (hid_at * k_dev).astype(F32)
    pick_ref[...] = jnp.broadcast_to(mine, pick_ref.shape)


def prepare(ids, hidden_grad, after, columns, tok_dev, k_dev, split):
    cap, hidden = hidden_grad.shape
    return pl.pallas_call(
        functools.partial(prepare_kernel, tok_dev=tok_dev, k_dev=k_dev, split=split),
        out_shape=(
            jax.ShapeDtypeStruct((cap, columns), BF16),
            jax.ShapeDtypeStruct((cap, hidden), BF16),
            jax.ShapeDtypeStruct((tok_dev, 128), F32),
        ),
        in_specs=[VMEM, VMEM, ANY],
        out_specs=(VMEM,) * 3,
        compiler_params=pltpu.CompilerParams(vmem_limit_bytes=4 << 20),
        name="prepare",
    )(ids, hidden_grad, after)


CONTRACT_LAST = (((1,), (1,)), ((), ()))


def expert_kernel(
    table_ref, hidden_ref, gate_ref, up_ref, *refs, n_blocks, chunk
):
    block_refs = refs[:n_blocks]
    slots_ref, grad_gate_ref, keep_ref, send_ref = refs[n_blocks:]
    rows = jnp.concatenate([ref[...].astype(F32) for ref in block_refs], axis=0).astype(BF16)
    slots = jnp.dot(table_ref[...], rows, preferred_element_type=F32).astype(BF16)
    slots_ref[...] = slots
    cap, width = slots.shape
    half = cap // 2
    gate_act = jnp.zeros((cap, gate_ref.shape[1]), F32)
    up_act = jnp.zeros((cap, gate_ref.shape[1]), F32)
    for at in range(0, width, chunk):
        part = slots[:, at : at + chunk]
        gate_act += jnp.dot(part, gate_ref[at : at + chunk, :], preferred_element_type=F32)
        up_act += jnp.dot(part, up_ref[at : at + chunk, :], preferred_element_type=F32)
    sigmoid_gate = jax.nn.sigmoid(gate_act)
    hidden_float = hidden_ref[...].astype(F32)
    grad_gate = (
        hidden_float * up_act * sigmoid_gate * (1.0 + gate_act * (1.0 - sigmoid_gate))
    ).astype(BF16)
    grad_up = (hidden_float * gate_act * sigmoid_gate).astype(BF16)
    grad_gate_ref[...] = grad_gate
    for at in range(0, width, chunk):
        there = slice(at, at + chunk)
        total = lax.dot_general(grad_gate, gate_ref[there, :], CONTRACT_LAST, preferred_element_type=F32)
        total += lax.dot_general(grad_up, up_ref[there, :], CONTRACT_LAST, preferred_element_type=F32)
        keep_ref[:, there] = total[:half]
        send_ref[:, there] = total[half:].astype(send_ref.dtype)


def expert(table, hidden_grad, gate, up, blocks, send_dtype):
    cap, hidden = hidden_grad.shape
    width = gate.shape[0]
    return pl.pallas_call(
        functools.partial(expert_kernel, n_blocks=len(blocks), chunk=512),
        out_shape=(
            jax.ShapeDtypeStruct((cap, width), BF16),
            jax.ShapeDtypeStruct((cap, hidden), BF16),
            jax.ShapeDtypeStruct((cap // 2, width), F32),
            jax.ShapeDtypeStruct((cap // 2, width), send_dtype),
        ),
        in_specs=[VMEM] * (4 + len(blocks)),
        out_specs=(VMEM,) * 4,
        compiler_params=pltpu.CompilerParams(vmem_limit_bytes=24 << 20),
        cost_estimate=pl.CostEstimate(
            flops=8 * cap * width * hidden, bytes_accessed=4 * width * hidden, transcendentals=cap * hidden
        ),
        name="expert",
    )(table, hidden_grad, gate, up, *blocks)


def weight_kernel(slots_ref, grad_ref, *refs, low, high, chunk):
    out_hbm, out_ref, sems = refs[-3:]
    copies = []
    for number, at in enumerate(range(low, high, chunk)):
        there = slice(at - low, at - low + chunk)
        out_ref[there, :] = lax.dot_general(
            slots_ref[:, at : at + chunk], grad_ref[...], (((0,), (0,)), ((), ())), preferred_element_type=F32
        ).astype(out_ref.dtype)
        copies.append(pltpu.make_async_copy(out_ref.at[there, :], out_hbm.at[at : at + chunk, :], sems.at[number]))
        copies[-1].start()
    for copy in copies:
        copy.wait()


def weight_gradient(slots, grad_gate, low, high, out=None):
    cap, width = slots.shape
    hidden = grad_gate.shape[1]
    chunk = 512
    return pl.pallas_call(
        functools.partial(weight_kernel, low=low, high=high, chunk=chunk),
        out_shape=jax.ShapeDtypeStruct((width, hidden), BF16),
        in_specs=[VMEM, VMEM] + ([] if out is None else [HBM]),
        out_specs=HBM,
        scratch_shapes=[
            pltpu.VMEM((high - low, hidden), BF16),
            pltpu.SemaphoreType.DMA(((high - low) // chunk,)),
        ],
        input_output_aliases={} if out is None else {2: 0},
        compiler_params=pltpu.CompilerParams(vmem_limit_bytes=12 << 20),
        cost_estimate=pl.CostEstimate(
            flops=2 * cap * (high - low) * hidden, bytes_accessed=2 * (high - low) * hidden, transcendentals=0
        ),
        name="weight_gradient",
    )(slots, grad_gate, *([] if out is None else [out]))


def per_device(layer_input, hidden_grad, gate_weight, up_weight, expert_ids):
    tok_dev = layer_input.shape[1]
    k_dev = tok_dev // 2
    hids = lax.axis_size("hid")
    split = hids == CORES * CHIPS
    core_at = lax.axis_index("hid") % CORES
    own, gate, up = layer_input[0], gate_weight[0], up_weight[0]
    ids = jnp.swapaxes(expert_ids, 1, 2)

    if split:
        start = opening(4 * gate.size)
        own, start = lax.optimization_barrier((own, start))
        other = to_other_core(own)
        near = moved(own, lambda section, hid: (section, hid ^ 2))
        both = pack(ids, own, other, start, k_dev)
        far = moved(both, lambda section, hid: (section, hid ^ (4 if hid % CORES else 6)))
        blocks = [both, near, to_other_core(near), far, to_other_core(far)]
        after = both
    else:
        blocks = [lax.all_gather(own, "hid", axis=0, tiled=True)]
        after = own
    columns = sum(block.shape[0] for block in blocks)
    table, hidden_ordered, pick = prepare(ids, hidden_grad[0], after, columns, tok_dev, k_dev, split)
    slots, grad_gate, keep, send = expert(
        table, hidden_ordered, gate, up, blocks, BF16 if split else F32
    )
    width = gate.shape[0]

    if split:
        rows = keep.shape[0] // 2
        keep = keep + to_other_core(send).astype(F32)
        keep, slots, grad_gate = lax.optimization_barrier((keep, slots, grad_gate))
        across = moved(keep[rows:].astype(BF16), lambda section, hid: (section, hid ^ 2))
        weight_grad = weight_gradient(slots, grad_gate, 0, width)
        across, weight_grad = lax.optimization_barrier((across, weight_grad))
        part = (keep[:rows] + across.astype(F32)).astype(BF16)
        part, slots = lax.optimization_barrier((part, slots))
        part = moved(part, lambda section, hid: (section - 1, hid ^ (4 * (hid % CORES))))
        part, weight_grad = lax.optimization_barrier((part, weight_grad))
        total = part.astype(F32) + to_other_core(part).astype(F32)
        own_total = jnp.where(core_at == 0, total[:k_dev], total[k_dev:])
    else:
        weight_grad = weight_gradient(slots, grad_gate, 0, width)
        whole = jnp.concatenate([keep, send], axis=0)
        own_total = lax.psum_scatter(whole, "hid", scatter_dimension=0, tiled=True)
        own_total = moved(own_total, lambda section, hid: (section - 1, hid))
    grad_in = jnp.zeros((tok_dev, own.shape[1]), F32)
    for rank in range(k_dev):
        grad_in = jnp.where(pick[:, :1] == rank, own_total[rank : rank + 1], grad_in)
    return (grad_in.astype(BF16)[None], weight_grad[None])


def solution(mesh):
    return jax.shard_map(
        per_device,
        mesh=mesh,
        in_specs=(
            P("section", "hid", None),
            P("section", None, "hid"),
            P("section", None, "hid"),
            P("section", None, "hid"),
            P(),
        ),
        out_specs=(P("section", "hid", None), P("section", None, "hid")),
        check_vma=False,
    )
```

time: 43.8 us -> 30.8 us (0.70)
  Pallas kernels: 14.9 us -> 10.1 us
  local copies, waits for them, and re-layouts: 4.24 us -> 0.76 us
  other arithmetic: 3.01 us -> 0.92 us
  waiting for transfers between devices: 8.91 us -> 7.21 us
  starting transfers between devices: 11.5 us -> 10.9 us
    unnamed x6 -> x10, local copies, waits for them, and re-layouts: 3.87 us -> 0.72 us
    pallas_call x1, Pallas kernels: 8.98 us -> 5.91 us  [expert(): pl.pallas_call(functools.partial(expert_kernel, n_blocks=len(blocks), chu...]
    pallas_call x1 -> x4, Pallas kernels: 5.89 us -> 4.17 us  [the longest x1 3.51 us: weight_gradient(): pl.pallas_call(functools.partial(weight_kernel, low=low, high=high, chunk...]
    ppermute x9, waiting for transfers between devices: 8.91 us -> 7.21 us  [moved(): return lax.ppermute(value, ('section', 'hid'), pairs)]
    concatenate x1 -> x0, other arithmetic: 0.8 us -> none  [per_device(): both = jnp.concatenate([own, other], axis=0)]
    reduce_or x1 -> x0, other arithmetic: 0.72 us -> none  [slot_numbers(): chosen = jnp.any(ids == 0, axis=1)]
    ppermute x9, starting transfers between devices: 11.5 us -> 10.9 us  [moved(): return lax.ppermute(value, ('section', 'hid'), pairs)]
  transfers between devices with their start and end apart: 9 -> 9, of which waited for: 5 -> 6; matrix products, arithmetic and copies ran while one was open for 6% -> 0% of each run, Pallas kernels for 14% -> 14%
where the time goes in v2:
time: 30.8 us; the launch traced here: 30.7 us
  starting transfers between devices  10.9 us (35%)
  Pallas kernels  10.1 us (33%)
  waiting for transfers between devices  7.21 us (23%)
  other arithmetic  0.92 us (3%)
  local copies, waits for them, and re-layouts  0.76 us (2%)
  between operations  0.75 us (2%)
    ppermute x9, starting transfers between devices, moved(): return lax.ppermute(value, ('section', 'hid'), pairs)  10.9 us
    ppermute x9, waiting for transfers between devices, moved(): return lax.ppermute(value, ('section', 'hid'), pairs)  7.21 us
    pallas_call x1, Pallas kernels, expert(): pl.pallas_call(functools.partial(expert_kernel, n_blocks=len(blocks), chu...  5.91 us
    pallas_call x1, Pallas kernels, weight_gradient(): pl.pallas_call(functools.partial(weight_kernel, low=low, high=high, chunk...  3.51 us
    unnamed x10, local copies, waits for them, and re-layouts  0.72 us
    convert_element_type x1, other arithmetic, per_device(): return (grad_in.astype(BF16)[None], weight_grad[None])  0.7 us
  transfers between devices with their start and end apart: 9, of which 6 were waited for; matrix products, arithmetic and copies ran while one was open for 0% of the time, Pallas kernels for 14%

profile of v2, /device:TPU:0, one launch (start us, length us, event | category | flops | bytes accessed | tf_op | source)
XLA Modules:
  0.0 30.7 jit_solution(17891808082146852205)
XLA Ops:
  0.6 0.0 copy-start.2
  0.6 0.0 copy-start.4
  0.7 0.0 copy-start.3
  0.7 0.0 copy-start.1
  0.7 0.0 copy-start
  0.7 0.7 %copy-done.2 = bf16[1,4,4096]{2,1,0:T(4,128)(2,1)S(1)} copy-done((bf16[1,4,4096]{2,1,0:T(4,128)(2,1)S(1)}, bf16[1,4,4096]{2,1,0:T(4,128)(2,1)}, u32[]{:S(2)}) %copy-start.2) | copy-done | bytes 32792
  1.4 0.5 %collective-permute-start = (bf16[4,4096]{1,0:T(4,128)(2,1)S(1)}, bf16[4,4096]{1,0:T(4,128)(2,1)S(1)}, u32[]{:S(2)}, u32[]{:S(2)}) collective-permute-start(bf16[4,4096]{1,0:T(4,128)(2,1)S(1)} %bitcast.10), channel_id=1, source_target_pairs={{0,1},{1,0},{2,3},{3,2},{4,5},{5,4},{6,7},{7,6},{8,9},{9,8},{10,11... | collective-permute-start | bytes 98312 | tf_op jit(solution)/shard_map/ppermute | solution.py:26
  1.8 2.6 %collective-permute-start.1 = (bf16[4,4096]{1,0:T(4,128)(2,1)S(1)}, bf16[4,4096]{1,0:T(4,128)(2,1)S(1)}, u32[]{:S(2)}, u32[]{:S(2)}) collective-permute-start(bf16[4,4096]{1,0:T(4,128)(2,1)S(1)} %bitcast.11), channel_id=1, source_target_pairs={{0,2},{1,3},{2,0},{3,1},{4,6},{5,7},{6,4},{7,5},{8,10},{9,11},{10,... | collective-permute-start | bytes 98312 | tf_op jit(solution)/shard_map/ppermute | solution.py:26
  4.4 0.0 collective-permute-done.other_ref
  4.4 0.0 copy-done.4
  4.4 0.4 %pack.1.after_ref.refs_0_ = bf16[4,4096]{1,0:T(4,128)(2,1)S(1)} custom-call(s32[4,2,32]{2,1,0:T(2,128)S(1)} %bitcast.14, bf16[4,4096]{1,0:T(4,128)(2,1)S(1)} %bitcast.12, bf16[4,4096]{1,0:T(4,128)(2,1)S(1)} %collective-permute-done.other_ref, f32[8,128]{1,0:T(8,128)S(1)} %opening.1.after_ref), custom_call_target="tpu_custom_call" | custom-call | tf_op jit(solution)/shard_map/pack/pallas_call | solution.py:70
  4.8 3.3 %collective-permute-start.3 = (bf16[4,4096]{1,0:T(4,128)(2,1)S(1)}, bf16[4,4096]{1,0:T(4,128)(2,1)S(1)}, u32[]{:S(2)}, u32[]{:S(2)}) collective-permute-start(bf16[4,4096]{1,0:T(4,128)(2,1)S(1)} %pack.1.after_ref.refs_0_), channel_id=1, source_target_pairs={{0,6},{1,5},{2,4},{3,7},{4,2},{5,1},{6,0},{7,3},{8,14},{9,13},{10,... | collective-permute-start | bytes 98312 | tf_op jit(solution)/shard_map/ppermute | solution.py:26
  8.1 0.0 collective-permute-done.1.refs_1_
  8.1 0.0 collective-permute-start.2
  8.1 2.5 %collective-permute-done.3.refs_3_ = bf16[4,4096]{1,0:T(4,128)(2,1)S(1)} collective-permute-done((bf16[4,4096]{1,0:T(4,128)(2,1)S(1)}, bf16[4,4096]{1,0:T(4,128)(2,1)S(1)}, u32[]{:S(2)}, u32[]{:S(2)}) %collective-permute-start.3) | collective-permute-done | bytes 32800 | tf_op jit(solution)/shard_map/ppermute | solution.py:26
  10.6 0.0 collective-permute-start.4
  10.6 0.0 copy-done.3
  10.6 0.3 prepare.1
  10.9 0.0 collective-permute-done.2.refs_2_
  10.9 0.9 %collective-permute-done.4.refs_4_ = bf16[4,4096]{1,0:T(4,128)(2,1)S(1)} collective-permute-done((bf16[4,4096]{1,0:T(4,128)(2,1)S(1)}, bf16[4,4096]{1,0:T(4,128)(2,1)S(1)}, u32[]{:S(2)}, u32[]{:S(2)}) %collective-permute-start.4) | collective-permute-done | bytes 32800 | tf_op jit(solution)/shard_map/ppermute | solution.py:26
  11.8 0.0 copy-done.1
  11.8 0.0 copy-done
  11.8 5.9 %expert.1 = (bf16[16,4096]{1,0:T(8,128)(2,1)S(1)}, bf16[16,896]{1,0:T(8,128)(2,1)S(1)}, f32[8,4096]{1,0:T(8,128)S(1)}, bf16[8,4096]{1,0:T(8,128)(2,1)S(1)}) custom-call(bf16[16,20]{1,0:T(8,128)(2,1)S(1)} %get-tuple-element.22.table_ref, bf16[16,896]{1,0:T(8,128)(2,1)S(1)} %get-tuple-element.23.hidden_ref, bf16[4096,896]{1,0:T(8,128)(2,1)S(1)} %bitcast.8, ...), custom_call_target="tpu_custom_call" | custom-call | flops 469762048 | bytes 14680064 | tf_op jit(solution)/shard_map/expert/pallas_call | solution.py:185
  17.7 0.2 collective-permute-start.5
  17.9 1.1 %collective-permute-done.5 = bf16[8,4096]{1,0:T(8,128)(2,1)S(1)} collective-permute-done((bf16[8,4096]{1,0:T(8,128)(2,1)S(1)}, bf16[8,4096]{1,0:T(8,128)(2,1)S(1)}, u32[]{:S(2)}, u32[]{:S(2)}) %collective-permute-start.5) | collective-permute-done | bytes 65568 | tf_op jit(solution)/shard_map/ppermute | solution.py:26
  19.0 0.1 collective-permute-start.6
  19.1 3.5 %weight_gradient.1 = bf16[4096,896]{1,0:T(8,128)(2,1)} custom-call(bf16[16,4096]{1,0:T(8,128)(2,1)S(1)} %get-tuple-element.29.slots_ref, bf16[16,896]{1,0:T(8,128)(2,1)S(1)} %get-tuple-element.30.grad_ref), custom_call_target="tpu_custom_call" | custom-call | flops 117440512 | bytes 7340032 | tf_op jit(solution)/shard_map/weight_gradient/pallas_call | solution.py:221
  22.6 0.4 %collective-permute-done.6 = bf16[4,4096]{1,0:T(4,128)(2,1)S(1)} collective-permute-done((bf16[4,4096]{1,0:T(4,128)(2,1)S(1)}, bf16[4,4096]{1,0:T(4,128)(2,1)S(1)}, u32[]{:S(2)}, u32[]{:S(2)}) %collective-permute-start.6) | collective-permute-done | bytes 32800 | tf_op jit(solution)/shard_map/ppermute | solution.py:26
  23.1 2.5 %collective-permute-start.7 = (bf16[4,4096]{1,0:T(4,128)(2,1)S(1)}, bf16[4,4096]{1,0:T(4,128)(2,1)S(1)}, u32[]{:S(2)}, u32[]{:S(2)}) collective-permute-start(bf16[4,4096]{1,0:T(4,128)(2,1)S(1)} %add_convert_fusion), channel_id=1, source_target_pairs={{0,24},{1,29},{2,26},{3,31},{4,28},{5,25},{6,30},{7,27},{8,0},{9,5... | collective-permute-start | bytes 98312 | tf_op jit(solution)/shard_map/ppermute | solution.py:26
  25.6 1.6 %collective-permute-done.7 = bf16[4,4096]{1,0:T(4,128)(2,1)S(1)} collective-permute-done((bf16[4,4096]{1,0:T(4,128)(2,1)S(1)}, bf16[4,4096]{1,0:T(4,128)(2,1)S(1)}, u32[]{:S(2)}, u32[]{:S(2)}) %collective-permute-start.7) | collective-permute-done | bytes 32800 | tf_op jit(solution)/shard_map/ppermute | solution.py:26
  27.1 1.9 %collective-permute-start.8 = (bf16[4,4096]{1,0:T(4,128)(2,1)S(1)}, bf16[4,4096]{1,0:T(4,128)(2,1)S(1)}, u32[]{:S(2)}, u32[]{:S(2)}) collective-permute-start(bf16[4,4096]{1,0:T(4,128)(2,1)S(1)} %collective-permute-done.7), channel_id=1, source_target_pairs={{0,1},{1,0},{2,3},{3,2},{4,5},{5,4},{6,7},{7,6},{8,9},{9,8},{10,11... | collective-permute-start | bytes 98312 | tf_op jit(solution)/shard_map/ppermute | solution.py:26
  29.0 0.1 compare_reduce_fusion.1
  29.2 0.7 %collective-permute-done.8 = bf16[4,4096]{1,0:T(4,128)(2,1)S(1)} collective-permute-done((bf16[4,4096]{1,0:T(4,128)(2,1)S(1)}, bf16[4,4096]{1,0:T(4,128)(2,1)S(1)}, u32[]{:S(2)}, u32[]{:S(2)}) %collective-permute-start.8) | collective-permute-done | bytes 32800 | tf_op jit(solution)/shard_map/ppermute | solution.py:26
  30.0 0.7 %select_convert_fusion = bf16[1,4,4096]{2,1,0:T(4,128)(2,1)} fusion(f32[4096]{0:T(1024)S(1)} %bitcast.18, f32[4096]{0:T(1024)S(1)} %bitcast.17, pred[4]{0:T(512)(128)(4,1)S(1)} %get-tuple-element.37, pred[4]{0:T(512)(128)(4,1)S(1)} %get-tuple-element.36), kind=kLoop, calls=%fused_computation.2 | loop fusion | flops 32768 | bytes 65544 | tf_op jit(solution)/shard_map/convert_element_type | solution.py:288
  (7 shorter events, 0.1 us)
Async XLA Ops:
  0.6 0.8 %copy-start.2 = (bf16[1,4,4096]{2,1,0:T(4,128)(2,1)S(1)}, bf16[1,4,4096]{2,1,0:T(4,128)(2,1)}, u32[]{:S(2)}) copy-start(bf16[1,4,4096]{2,1,0:T(4,128)(2,1)} %param.5) | copy-start | bytes 98308
  0.6 3.8 %copy-start.4 = (s32[4,32,2]{1,2,0:T(2,128)S(1)}, s32[4,32,2]{1,2,0:T(2,128)}, u32[]{:S(2)}) copy-start(s32[4,32,2]{1,2,0:T(2,128)} %param.9) | copy-start | bytes 3076
  0.7 10.0 %copy-start.3 = (bf16[1,16,896]{2,1,0:T(8,128)(2,1)S(1)}, bf16[1,16,896]{2,1,0:T(8,128)(2,1)}, u32[]{:S(2)}) copy-start(bf16[1,16,896]{2,1,0:T(8,128)(2,1)} %param.6) | copy-start | bytes 86020
  0.7 11.2 %copy-start.1 = (bf16[1,4096,896]{2,1,0:T(8,128)(2,1)S(1)}, bf16[1,4096,896]{2,1,0:T(8,128)(2,1)}, u32[]{:S(2)}) copy-start(bf16[1,4096,896]{2,1,0:T(8,128)(2,1)} %param.8) | copy-start | bytes 22020100
  0.7 11.2 %copy-start = (bf16[1,4096,896]{2,1,0:T(8,128)(2,1)S(1)}, bf16[1,4096,896]{2,1,0:T(8,128)(2,1)}, u32[]{:S(2)}) copy-start(bf16[1,4096,896]{2,1,0:T(8,128)(2,1)} %param.7) | copy-start | bytes 22020100
  1.4 3.0 %collective-permute-start = (bf16[4,4096]{1,0:T(4,128)(2,1)S(1)}, bf16[4,4096]{1,0:T(4,128)(2,1)S(1)}, u32[]{:S(2)}, u32[]{:S(2)}) collective-permute-start(bf16[4,4096]{1,0:T(4,128)(2,1)S(1)} %bitcast.10), channel_id=1, source_target_pairs={{0,1},{1,0},{2,3},{3,2},{4,5},{5,4},{6,7},{7,6},{8,9},{9,8},{10,11... | collective-permute-start | bytes 98312 | tf_op jit(solution)/shard_map/ppermute | solution.py:26
  1.8 6.3 %collective-permute-start.1 = (bf16[4,4096]{1,0:T(4,128)(2,1)S(1)}, bf16[4,4096]{1,0:T(4,128)(2,1)S(1)}, u32[]{:S(2)}, u32[]{:S(2)}) collective-permute-start(bf16[4,4096]{1,0:T(4,128)(2,1)S(1)} %bitcast.11), channel_id=1, source_target_pairs={{0,2},{1,3},{2,0},{3,1},{4,6},{5,7},{6,4},{7,5},{8,10},{9,11},{10,... | collective-permute-start | bytes 98312 | tf_op jit(solution)/shard_map/ppermute | solution.py:26
  4.8 5.8 %collective-permute-start.3 = (bf16[4,4096]{1,0:T(4,128)(2,1)S(1)}, bf16[4,4096]{1,0:T(4,128)(2,1)S(1)}, u32[]{:S(2)}, u32[]{:S(2)}) collective-permute-start(bf16[4,4096]{1,0:T(4,128)(2,1)S(1)} %pack.1.after_ref.refs_0_), channel_id=1, source_target_pairs={{0,6},{1,5},{2,4},{3,7},{4,2},{5,1},{6,0},{7,3},{8,14},{9,13},{10,... | collective-permute-start | bytes 98312 | tf_op jit(solution)/shard_map/ppermute | solution.py:26
  8.1 2.7 %collective-permute-start.2 = (bf16[4,4096]{1,0:T(4,128)(2,1)S(1)}, bf16[4,4096]{1,0:T(4,128)(2,1)S(1)}, u32[]{:S(2)}, u32[]{:S(2)}) collective-permute-start(bf16[4,4096]{1,0:T(4,128)(2,1)S(1)} %collective-permute-done.1.refs_1_), channel_id=1, source_target_pairs={{0,1},{1,0},{2,3},{3,2},{4,5},{5,4},{6,7},{7,6},{8,9},{9,8},{10,11... | collective-permute-start | bytes 98312 | tf_op jit(solution)/shard_map/ppermute | solution.py:26
  10.6 1.2 %collective-permute-start.4 = (bf16[4,4096]{1,0:T(4,128)(2,1)S(1)}, bf16[4,4096]{1,0:T(4,128)(2,1)S(1)}, u32[]{:S(2)}, u32[]{:S(2)}) collective-permute-start(bf16[4,4096]{1,0:T(4,128)(2,1)S(1)} %collective-permute-done.3.refs_3_), channel_id=1, source_target_pairs={{0,1},{1,0},{2,3},{3,2},{4,5},{5,4},{6,7},{7,6},{8,9},{9,8},{10,11... | collective-permute-start | bytes 98312 | tf_op jit(solution)/shard_map/ppermute | solution.py:26
  17.7 1.3 %collective-permute-start.5 = (bf16[8,4096]{1,0:T(8,128)(2,1)S(1)}, bf16[8,4096]{1,0:T(8,128)(2,1)S(1)}, u32[]{:S(2)}, u32[]{:S(2)}) collective-permute-start(bf16[8,4096]{1,0:T(8,128)(2,1)S(1)} %get-tuple-element.25), channel_id=1, source_target_pairs={{0,1},{1,0},{2,3},{3,2},{4,5},{5,4},{6,7},{7,6},{8,9},{9,8},{10,11... | collective-permute-start | bytes 196616 | tf_op jit(solution)/shard_map/ppermute | solution.py:26
  19.0 4.0 %collective-permute-start.6 = (bf16[4,4096]{1,0:T(4,128)(2,1)S(1)}, bf16[4,4096]{1,0:T(4,128)(2,1)S(1)}, u32[]{:S(2)}, u32[]{:S(2)}) collective-permute-start(bf16[4,4096]{1,0:T(4,128)(2,1)S(1)} %slice.41), channel_id=1, source_target_pairs={{0,2},{1,3},{2,0},{3,1},{4,6},{5,7},{6,4},{7,5},{8,10},{9,11},{10,... | collective-permute-start | bytes 98312 | tf_op jit(solution)/shard_map/ppermute | solution.py:26
  23.1 4.1 %collective-permute-start.7 = (bf16[4,4096]{1,0:T(4,128)(2,1)S(1)}, bf16[4,4096]{1,0:T(4,128)(2,1)S(1)}, u32[]{:S(2)}, u32[]{:S(2)}) collective-permute-start(bf16[4,4096]{1,0:T(4,128)(2,1)S(1)} %add_convert_fusion), channel_id=1, source_target_pairs={{0,24},{1,29},{2,26},{3,31},{4,28},{5,25},{6,30},{7,27},{8,0},{9,5... | collective-permute-start | bytes 98312 | tf_op jit(solution)/shard_map/ppermute | solution.py:26
  27.1 2.7 %collective-permute-start.8 = (bf16[4,4096]{1,0:T(4,128)(2,1)S(1)}, bf16[4,4096]{1,0:T(4,128)(2,1)S(1)}, u32[]{:S(2)}, u32[]{:S(2)}) collective-permute-start(bf16[4,4096]{1,0:T(4,128)(2,1)S(1)} %collective-permute-done.7), channel_id=1, source_target_pairs={{0,1},{1,0},{2,3},{3,2},{4,5},{5,4},{6,7},{7,6},{8,9},{9,8},{10,11... | collective-permute-start | bytes 98312 | tf_op jit(solution)/shard_map/ppermute | solution.py:26

commit v3 on v2

--- a/solution.py
+++ b/solution.py
@@ -92,8 +92,13 @@
     )()
 
 
-def prepare_kernel(ids_ref, hidden_ref, after_ref, table_ref, hidden_out_ref, pick_ref, *, tok_dev, k_dev, split):
-    del after_ref
+def prepare_kernel(
+    ids_ref, hidden_ref, gate_ref, up_ref, after_ref, table_ref, hidden_out_ref, pick_ref, up_turned_ref,
+    *, tok_dev, k_dev, split, chunk,
+):
+    del gate_ref, after_ref
+    for at in range(0, up_ref.shape[0], chunk):
+        up_turned_ref[:, at : at + chunk] = up_ref[at : at + chunk, :].T
     section_at, hid_at = lax.axis_index("section"), lax.axis_index("hid")
     core_at, chip_at = hid_at % CORES, hid_at // CORES
     cap, columns = table_ref.shape
@@ -106,17 +111,14 @@
         device = (chip_at ^ step) * CORES + device % CORES
     wanted = device * k_dev + rank
 
-    slot_of = slot_row(ids_ref, section_at, tok_dev, k_dev)
     column = lanes((1, columns))
-    group, place = column // tok_dev, column % tok_dev
-    if split:
-        slots = slot_at(slot_of, (hid_at ^ (group + 1)) * tok_dev + place)
-        turn = jnp.where(group == 0, 0, jnp.where(group == 3, 6 - 2 * core_at, 5 + 2 * core_at))
-        packed = (hid_at ^ turn ^ (place // k_dev)) * k_dev + place % k_dev
-        slots = jnp.where((group == 1) | (group == 2), slots, packed.astype(F32))
+    if split:
+        group, place = column // tok_dev, column % tok_dev
+        turn = jnp.where(group < 2, 2 * group, jnp.where(group == 2, 6 - 2 * core_at, 5 + 2 * core_at))
+        slots = (hid_at ^ turn ^ (place // k_dev)) * k_dev + place % k_dev
     else:
-        slots = slot_at(slot_of, column)
-    table_ref[...] = jnp.where(wanted.astype(F32) == slots, 1.0, 0.0).astype(BF16)
+        slots = slot_at(slot_row(ids_ref, section_at, tok_dev, k_dev), column).astype(jnp.int32)
+    table_ref[...] = jnp.where(wanted == slots, 1.0, 0.0).astype(BF16)
 
     order = jnp.where(wanted == lanes((cap, cap)), 1.0, 0.0).astype(BF16)
     hidden_out_ref[...] = jnp.dot(order, hidden_ref[...], preferred_element_type=F32).astype(BF16)
@@ -129,30 +131,29 @@
     pick_ref[...] = jnp.broadcast_to(mine, pick_ref.shape)
 
 
-def prepare(ids, hidden_grad, after, columns, tok_dev, k_dev, split):
+def prepare(ids, hidden_grad, gate, up, after, columns, tok_dev, k_dev, split):
     cap, hidden = hidden_grad.shape
     return pl.pallas_call(
-        functools.partial(prepare_kernel, tok_dev=tok_dev, k_dev=k_dev, split=split),
+        functools.partial(prepare_kernel, tok_dev=tok_dev, k_dev=k_dev, split=split, chunk=512),
         out_shape=(
             jax.ShapeDtypeStruct((cap, columns), BF16),
             jax.ShapeDtypeStruct((cap, hidden), BF16),
             jax.ShapeDtypeStruct((tok_dev, 128), F32),
-        ),
-        in_specs=[VMEM, VMEM, ANY],
-        out_specs=(VMEM,) * 3,
+            jax.ShapeDtypeStruct((hidden, gate.shape[0]), BF16),
+        ),
+        in_specs=[VMEM] * 4 + [ANY],
+        out_specs=(VMEM,) * 4,
         compiler_params=pltpu.CompilerParams(vmem_limit_bytes=4 << 20),
+        cost_estimate=pl.CostEstimate(flops=0, bytes_accessed=4 * gate.size, transcendentals=0),
         name="prepare",
-    )(ids, hidden_grad, after)
-
-
-CONTRACT_LAST = (((1,), (1,)), ((), ()))
+    )(ids, hidden_grad, gate, up, after)
 
 
 def expert_kernel(
-    table_ref, hidden_ref, gate_ref, up_ref, *refs, n_blocks, chunk
+    table_ref, hidden_ref, gate_ref, up_ref, up_turned_ref, *refs, n_blocks, chunk
 ):
     block_refs = refs[:n_blocks]
-    slots_ref, grad_gate_ref, keep_ref, send_ref = refs[n_blocks:]
+    slots_ref, grad_gate_ref, keep_ref, send_ref, gate_turned_ref = refs[n_blocks:]
     rows = jnp.concatenate([ref[...].astype(F32) for ref in block_refs], axis=0).astype(BF16)
     slots = jnp.dot(table_ref[...], rows, preferred_element_type=F32).astype(BF16)
     slots_ref[...] = slots
@@ -164,6 +165,7 @@
         part = slots[:, at : at + chunk]
         gate_act += jnp.dot(part, gate_ref[at : at + chunk, :], preferred_element_type=F32)
         up_act += jnp.dot(part, up_ref[at : at + chunk, :], preferred_element_type=F32)
+        gate_turned_ref[:, at : at + chunk] = gate_ref[at : at + chunk, :].T
     sigmoid_gate = jax.nn.sigmoid(gate_act)
     hidden_float = hidden_ref[...].astype(F32)
     grad_gate = (
@@ -173,13 +175,13 @@
     grad_gate_ref[...] = grad_gate
     for at in range(0, width, chunk):
         there = slice(at, at + chunk)
-        total = lax.dot_general(grad_gate, gate_ref[there, :], CONTRACT_LAST, preferred_element_type=F32)
-        total += lax.dot_general(grad_up, up_ref[there, :], CONTRACT_LAST, preferred_element_type=F32)
+        total = jnp.dot(grad_gate, gate_turned_ref[:, there], preferred_element_type=F32)
+        total += jnp.dot(grad_up, up_turned_ref[:, there], preferred_element_type=F32)
         keep_ref[:, there] = total[:half]
         send_ref[:, there] = total[half:].astype(send_ref.dtype)
 
 
-def expert(table, hidden_grad, gate, up, blocks, send_dtype):
+def expert(table, hidden_grad, gate, up, up_turned, blocks, send_dtype):
     cap, hidden = hidden_grad.shape
     width = gate.shape[0]
     return pl.pallas_call(
@@ -190,14 +192,15 @@
             jax.ShapeDtypeStruct((cap // 2, width), F32),
             jax.ShapeDtypeStruct((cap // 2, width), send_dtype),
         ),
-        in_specs=[VMEM] * (4 + len(blocks)),
+        in_specs=[VMEM] * (5 + len(blocks)),
         out_specs=(VMEM,) * 4,
-        compiler_params=pltpu.CompilerParams(vmem_limit_bytes=24 << 20),
+        scratch_shapes=[pltpu.VMEM((hidden, width), BF16)],
+        compiler_params=pltpu.CompilerParams(vmem_limit_bytes=16 << 20),
         cost_estimate=pl.CostEstimate(
             flops=8 * cap * width * hidden, bytes_accessed=4 * width * hidden, transcendentals=cap * hidden
         ),
         name="expert",
-    )(table, hidden_grad, gate, up, *blocks)
+    )(table, hidden_grad, gate, up, up_turned, *blocks)
 
 
 def weight_kernel(slots_ref, grad_ref, *refs, low, high, chunk):
@@ -217,7 +220,7 @@
 def weight_gradient(slots, grad_gate, low, high, out=None):
     cap, width = slots.shape
     hidden = grad_gate.shape[1]
-    chunk = 512
+    chunk = 256
     return pl.pallas_call(
         functools.partial(weight_kernel, low=low, high=high, chunk=chunk),
         out_shape=jax.ShapeDtypeStruct((width, hidden), BF16),
@@ -247,35 +250,43 @@
 
     if split:
         start = opening(4 * gate.size)
-        own, start = lax.optimization_barrier((own, start))
         other = to_other_core(own)
-        near = moved(own, lambda section, hid: (section, hid ^ 2))
         both = pack(ids, own, other, start, k_dev)
         far = moved(both, lambda section, hid: (section, hid ^ (4 if hid % CORES else 6)))
-        blocks = [both, near, to_other_core(near), far, to_other_core(far)]
+        near = moved(both, lambda section, hid: (section, hid ^ 2))
         after = both
+        columns = 4 * tok_dev
+    else:
+        after = own
+        columns = hids * tok_dev
+    table, hidden_ordered, pick, up_turned = prepare(
+        ids, hidden_grad[0], gate, up, after, columns, tok_dev, k_dev, split
+    )
+    if split:
+        far, up_turned = lax.optimization_barrier((far, up_turned))
+        blocks = [both, near, far, to_other_core(far)]
     else:
         blocks = [lax.all_gather(own, "hid", axis=0, tiled=True)]
-        after = own
-    columns = sum(block.shape[0] for block in blocks)
-    table, hidden_ordered, pick = prepare(ids, hidden_grad[0], after, columns, tok_dev, k_dev, split)
     slots, grad_gate, keep, send = expert(
-        table, hidden_ordered, gate, up, blocks, BF16 if split else F32
+        table, hidden_ordered, gate, up, up_turned, blocks, BF16 if split else F32
     )
     width = gate.shape[0]
 
     if split:
-        rows = keep.shape[0] // 2
-        keep = keep + to_other_core(send).astype(F32)
+        rows, width = keep.shape[0] // 2, gate.shape[0]
+        partner = to_other_core(send)
+        keep = keep + partner.astype(F32)
         keep, slots, grad_gate = lax.optimization_barrier((keep, slots, grad_gate))
         across = moved(keep[rows:].astype(BF16), lambda section, hid: (section, hid ^ 2))
-        weight_grad = weight_gradient(slots, grad_gate, 0, width)
+        weight_grad = weight_gradient(slots, grad_gate, 0 * width // 16, 9 * width // 16)
         across, weight_grad = lax.optimization_barrier((across, weight_grad))
         part = (keep[:rows] + across.astype(F32)).astype(BF16)
         part, slots = lax.optimization_barrier((part, slots))
         part = moved(part, lambda section, hid: (section - 1, hid ^ (4 * (hid % CORES))))
+        weight_grad = weight_gradient(slots, grad_gate, 9 * width // 16, 16 * width // 16, weight_grad)
         part, weight_grad = lax.optimization_barrier((part, weight_grad))
-        total = part.astype(F32) + to_other_core(part).astype(F32)
+        other = to_other_core(part)
+        total = part.astype(F32) + other.astype(F32)
         own_total = jnp.where(core_at == 0, total[:k_dev], total[k_dev:])
     else:
         weight_grad = weight_gradient(slots, grad_gate, 0, width)

time: 30.8 us -> 28.7 us (0.932)
  waiting for transfers between devices: 7.21 us -> 4.83 us
  Pallas kernels: 10.1 us -> 11 us
  local copies, waits for them, and re-layouts: 0.76 us -> 0.08 us
    ppermute x9 -> x8, waiting for transfers between devices: 7.21 us -> 4.83 us  [moved(): return lax.ppermute(value, ('section', 'hid'), pairs)]
    pallas_call x1, Pallas kernels: 0.26 us -> 2 us  [prepare(): pl.pallas_call(functools.partial(prepare_kernel, tok_dev=tok_dev, k_dev=k...]
    pallas_call x1, Pallas kernels: 5.91 us -> 4.21 us  [expert(): pl.pallas_call(functools.partial(expert_kernel, n_blocks=len(blocks), chu...]
    pallas_call x1 -> x2, Pallas kernels: 3.51 us -> 4.42 us  [weight_gradient(): pl.pallas_call(functools.partial(weight_kernel, low=low, high=high, chunk...]
    unnamed x10 -> x14, local copies, waits for them, and re-layouts: 0.72 us -> 0.03 us
    ppermute x9 -> x8, starting transfers between devices: 10.9 us -> 10.9 us  [moved(): return lax.ppermute(value, ('section', 'hid'), pairs)]
  transfers between devices with their start and end apart: 9 -> 8, of which waited for: 6 -> 6; matrix products, arithmetic and copies ran while one was open for 0% -> 1% of each run, Pallas kernels for 14% -> 23%
where the time goes in v3:
time: 28.7 us; the launch traced here: 28.5 us
  Pallas kernels  11 us (38%)
  starting transfers between devices  10.9 us (38%)
  waiting for transfers between devices  4.83 us (17%)
  other arithmetic  0.92 us (3%)
  between operations  0.81 us (3%)
    ppermute x8, starting transfers between devices, moved(): return lax.ppermute(value, ('section', 'hid'), pairs)  10.9 us
    ppermute x8, waiting for transfers between devices, moved(): return lax.ppermute(value, ('section', 'hid'), pairs)  4.83 us
    pallas_call x2, Pallas kernels, weight_gradient(): pl.pallas_call(functools.partial(weight_kernel, low=low, high=high, chunk...  4.42 us
    pallas_call x1, Pallas kernels, expert(): pl.pallas_call(functools.partial(expert_kernel, n_blocks=len(blocks), chu...  4.21 us
    pallas_call x1, Pallas kernels, prepare(): pl.pallas_call(functools.partial(prepare_kernel, tok_dev=tok_dev, k_dev=k...  2 us
    convert_element_type x1, other arithmetic, per_device(): return (grad_in.astype(BF16)[None], weight_grad[None])  0.7 us
  transfers between devices with their start and end apart: 8, of which 6 were waited for; matrix products, arithmetic and copies ran while one was open for 1% of the time, Pallas kernels for 23%

profile of v3, /device:TPU:0, one launch (start us, length us, event | category | flops | bytes accessed | tf_op | source)
XLA Modules:
  0.0 28.5 jit_solution(3537057521122229598)
XLA Ops:
  0.6 0.0 slice-start
  0.6 0.0 slice-start.2
  0.7 0.0 copy-start
  0.7 0.0 copy-start.2
  0.7 0.0 slice-start.1
  0.7 0.0 slice-start.3
  0.7 0.0 copy-start.1
  0.7 0.5 %collective-permute-start = (bf16[4,4096]{1,0:T(4,128)(2,1)}, bf16[4,4096]{1,0:T(4,128)(2,1)S(1)}, u32[]{:S(2)}, u32[]{:S(2)}) collective-permute-start(bf16[4,4096]{1,0:T(4,128)(2,1)} %bitcast.16), channel_id=1, source_target_pairs={{0,1},{1,0},{2,3},{3,2},{4,5},{5,4},{6,7},{7,6},{8,9},{9,8},{10,11... | collective-permute-start | bytes 98312 | tf_op jit(solution)/shard_map/ppermute | solution.py:26
  1.2 1.1 %collective-permute-done.other_ref = bf16[4,4096]{1,0:T(4,128)(2,1)S(1)} collective-permute-done((bf16[4,4096]{1,0:T(4,128)(2,1)}, bf16[4,4096]{1,0:T(4,128)(2,1)S(1)}, u32[]{:S(2)}, u32[]{:S(2)}) %collective-permute-start) | collective-permute-done | bytes 32800 | tf_op jit(solution)/shard_map/ppermute | solution.py:26
  2.3 0.0 copy-done
  2.3 0.0 copy-done.2
  2.3 0.4 %pack.1.after_ref.refs_0_ = bf16[4,4096]{1,0:T(4,128)(2,1)S(1)} custom-call(s32[4,2,32]{2,1,0:T(2,128)S(1)} %bitcast.19, bf16[4,4096]{1,0:T(4,128)(2,1)S(1)} %bitcast.17, bf16[4,4096]{1,0:T(4,128)(2,1)S(1)} %collective-permute-done.other_ref, f32[8,128]{1,0:T(8,128)S(1)} %opening.1.after_ref), custom_call_target="tpu_custom_call" | custom-call | tf_op jit(solution)/shard_map/pack/pallas_call | solution.py:70
  2.7 5.0 %collective-permute-start.1 = (bf16[4,4096]{1,0:T(4,128)(2,1)S(1)}, bf16[4,4096]{1,0:T(4,128)(2,1)S(1)}, u32[]{:S(2)}, u32[]{:S(2)}) collective-permute-start(bf16[4,4096]{1,0:T(4,128)(2,1)S(1)} %pack.1.after_ref.refs_0_), channel_id=1, source_target_pairs={{0,6},{1,5},{2,4},{3,7},{4,2},{5,1},{6,0},{7,3},{8,14},{9,13},{10,... | collective-permute-start | bytes 98312 | tf_op jit(solution)/shard_map/ppermute | solution.py:26
  7.7 0.0 collective-permute-start.2
  7.7 0.0 slice-done
  7.7 0.0 slice-done.2
  7.7 0.0 slice-done.1
  7.7 0.0 slice-done.3
  7.7 0.0 copy-done.1
  7.8 2.0 %prepare.1 = (bf16[16,16]{1,0:T(8,128)(2,1)S(1)}, bf16[16,896]{1,0:T(8,128)(2,1)S(1)}, f32[4,128]{1,0:T(4,128)S(1)}, bf16[896,4096]{1,0:T(8,128)(2,1)S(1)}) custom-call(s32[4,2,32]{2,1,0:T(2,128)S(1)} %bitcast.20, bf16[16,896]{1,0:T(8,128)(2,1)S(1)} %bitcast.18, bf16[4096,896]{1,0:T(8,128)(2,1)S(1)} %bitcast.10, bf16[4096,896]{1,0:T(8,128)(2,1)S(1)} %bitcast.14, ...), custom_call_target="tpu_custom_call" | custom-call | bytes 14680064 | tf_op jit(solution)/shard_map/prepare/pallas_call | solution.py:136
  9.8 0.1 collective-permute-done.1.refs_2_
  9.8 0.2 collective-permute-start.3
  10.0 1.6 %collective-permute-done.2.refs_1_ = bf16[4,4096]{1,0:T(4,128)(2,1)S(1)} collective-permute-done((bf16[4,4096]{1,0:T(4,128)(2,1)S(1)}, bf16[4,4096]{1,0:T(4,128)(2,1)S(1)}, u32[]{:S(2)}, u32[]{:S(2)}) %collective-permute-start.2) | collective-permute-done | bytes 32800 | tf_op jit(solution)/shard_map/ppermute | solution.py:26
  11.6 0.0 collective-permute-done.3.refs_3_
  11.6 4.2 %expert.1 = (bf16[16,4096]{1,0:T(8,128)(2,1)S(1)}, bf16[16,896]{1,0:T(8,128)(2,1)S(1)}, f32[8,4096]{1,0:T(8,128)S(1)}, bf16[8,4096]{1,0:T(8,128)(2,1)S(1)}) custom-call(bf16[16,16]{1,0:T(8,128)(2,1)S(1)} %get-tuple-element.22.table_ref, bf16[16,896]{1,0:T(8,128)(2,1)S(1)} %get-tuple-element.23.hidden_ref, bf16[4096,896]{1,0:T(8,128)(2,1)S(1)} %bitcast.11, ...), custom_call_target="tpu_custom_call" | custom-call | flops 469762048 | bytes 14680064 | tf_op jit(solution)/shard_map/expert/pallas_call | solution.py:187
  15.8 0.0 collective-permute-start.4
  15.8 1.3 %collective-permute-done.4 = bf16[8,4096]{1,0:T(8,128)(2,1)S(1)} collective-permute-done((bf16[8,4096]{1,0:T(8,128)(2,1)S(1)}, bf16[8,4096]{1,0:T(8,128)(2,1)S(1)}, u32[]{:S(2)}, u32[]{:S(2)}) %collective-permute-start.4) | collective-permute-done | bytes 65568 | tf_op jit(solution)/shard_map/ppermute | solution.py:26
  17.1 1.5 %collective-permute-start.5 = (bf16[4,4096]{1,0:T(4,128)(2,1)S(1)}, bf16[4,4096]{1,0:T(4,128)(2,1)S(1)}, u32[]{:S(2)}, u32[]{:S(2)}) collective-permute-start(bf16[4,4096]{1,0:T(4,128)(2,1)S(1)} %slice.41), channel_id=1, source_target_pairs={{0,2},{1,3},{2,0},{3,1},{4,6},{5,7},{6,4},{7,5},{8,10},{9,11},{10,... | collective-permute-start | bytes 98312 | tf_op jit(solution)/shard_map/ppermute | solution.py:26
  18.7 2.4 %weight_gradient.2.refs_0_ = bf16[4096,896]{1,0:T(8,128)(2,1)} custom-call(bf16[16,4096]{1,0:T(8,128)(2,1)S(1)} %get-tuple-element.36.slots_ref, bf16[16,896]{1,0:T(8,128)(2,1)S(1)} %get-tuple-element.33.grad_ref), custom_call_target="tpu_custom_call" | custom-call | flops 66060288 | bytes 4128768 | tf_op jit(solution)/shard_map/weight_gradient/pallas_call | solution.py:224
  21.0 0.1 collective-permute-done.5
  21.2 2.5 %collective-permute-start.6 = (bf16[4,4096]{1,0:T(4,128)(2,1)S(1)}, bf16[4,4096]{1,0:T(4,128)(2,1)S(1)}, u32[]{:S(2)}, u32[]{:S(2)}) collective-permute-start(bf16[4,4096]{1,0:T(4,128)(2,1)S(1)} %add_convert_fusion), channel_id=1, source_target_pairs={{0,24},{1,29},{2,26},{3,31},{4,28},{5,25},{6,30},{7,27},{8,0},{9,5... | collective-permute-start | bytes 98312 | tf_op jit(solution)/shard_map/ppermute | solution.py:26
  23.7 2.0 %weight_gradient.3 = bf16[4096,896]{1,0:T(8,128)(2,1)} custom-call(bf16[16,4096]{1,0:T(8,128)(2,1)S(1)} %get-tuple-element.36.slots_ref, bf16[16,896]{1,0:T(8,128)(2,1)S(1)} %get-tuple-element.33.grad_ref, bf16[4096,896]{1,0:T(8,128)(2,1)} %weight_gradient.2.refs_0_), custom_call_target="tpu_custom_call", output_to_operand_aliasing={{}: (2, {})} | custom-call | flops 51380224 | bytes 3211264 | tf_op jit(solution)/shard_map/weight_gradient/pallas_call | solution.py:224
  25.7 0.0 collective-permute-done.6
  25.7 1.2 %collective-permute-start.7 = (bf16[4,4096]{1,0:T(4,128)(2,1)S(1)}, bf16[4,4096]{1,0:T(4,128)(2,1)S(1)}, u32[]{:S(2)}, u32[]{:S(2)}) collective-permute-start(bf16[4,4096]{1,0:T(4,128)(2,1)S(1)} %collective-permute-done.6), channel_id=1, source_target_pairs={{0,1},{1,0},{2,3},{3,2},{4,5},{5,4},{6,7},{7,6},{8,9},{9,8},{10,11... | collective-permute-start | bytes 98312 | tf_op jit(solution)/shard_map/ppermute | solution.py:26
  26.9 0.1 compare_reduce_fusion.1
  27.0 0.7 %collective-permute-done.7 = bf16[4,4096]{1,0:T(4,128)(2,1)S(1)} collective-permute-done((bf16[4,4096]{1,0:T(4,128)(2,1)S(1)}, bf16[4,4096]{1,0:T(4,128)(2,1)S(1)}, u32[]{:S(2)}, u32[]{:S(2)}) %collective-permute-start.7) | collective-permute-done | bytes 32800 | tf_op jit(solution)/shard_map/ppermute | solution.py:26
  27.8 0.7 %select_convert_fusion = bf16[1,4,4096]{2,1,0:T(4,128)(2,1)} fusion(f32[4096]{0:T(1024)S(1)} %bitcast.23, f32[4096]{0:T(1024)S(1)} %bitcast.22, pred[4]{0:T(512)(128)(4,1)S(1)} %get-tuple-element.41, pred[4]{0:T(512)(128)(4,1)S(1)} %get-tuple-element.40), kind=kLoop, calls=%fused_computation.2 | loop fusion | flops 32768 | bytes 65544 | tf_op jit(solution)/shard_map/convert_element_type | solution.py:299
  (9 shorter events, 0.1 us)
Async XLA Ops:
  0.6 7.1 %slice-start = ((s8[7340032]{0:T(1024)(128)(4,1)}), s8[4194304]{0:T(1024)(128)(4,1)S(1)}, s32[]{:S(2)}) async-start(s8[7340032]{0:T(1024)(128)(4,1)} %bitcast.8), calls=%async_computation | async-start | bytes 8388608
  0.6 7.1 %slice-start.2 = ((s8[7340032]{0:T(1024)(128)(4,1)}), s8[4194304]{0:T(1024)(128)(4,1)S(1)}, s32[]{:S(2)}) async-start(s8[7340032]{0:T(1024)(128)(4,1)} %bitcast.12), calls=%async_computation.2 | async-start | bytes 8388608
  0.7 1.6 %copy-start = (bf16[1,4,4096]{2,1,0:T(4,128)(2,1)S(1)}, bf16[1,4,4096]{2,1,0:T(4,128)(2,1)}, u32[]{:S(2)}) copy-start(bf16[1,4,4096]{2,1,0:T(4,128)(2,1)} %param.5) | copy-start | bytes 98308
  0.7 1.6 %copy-start.2 = (s32[4,32,2]{1,2,0:T(2,128)S(1)}, s32[4,32,2]{1,2,0:T(2,128)}, u32[]{:S(2)}) copy-start(s32[4,32,2]{1,2,0:T(2,128)} %param.9) | copy-start | bytes 3076
  0.7 7.1 %slice-start.1 = ((s8[7340032]{0:T(1024)(128)(4,1)}), s8[3145728]{0:T(1024)(128)(4,1)S(1)}, s32[]{:S(2)}) async-start(s8[7340032]{0:T(1024)(128)(4,1)} %bitcast.8), calls=%async_computation.1 | async-start | bytes 6291456
  0.7 7.1 %slice-start.3 = ((s8[7340032]{0:T(1024)(128)(4,1)}), s8[3145728]{0:T(1024)(128)(4,1)S(1)}, s32[]{:S(2)}) async-start(s8[7340032]{0:T(1024)(128)(4,1)} %bitcast.12), calls=%async_computation.3 | async-start | bytes 6291456
  0.7 7.1 %copy-start.1 = (bf16[1,16,896]{2,1,0:T(8,128)(2,1)S(1)}, bf16[1,16,896]{2,1,0:T(8,128)(2,1)}, u32[]{:S(2)}) copy-start(bf16[1,16,896]{2,1,0:T(8,128)(2,1)} %param.6) | copy-start | bytes 86020
  0.7 1.6 %collective-permute-start = (bf16[4,4096]{1,0:T(4,128)(2,1)}, bf16[4,4096]{1,0:T(4,128)(2,1)S(1)}, u32[]{:S(2)}, u32[]{:S(2)}) collective-permute-start(bf16[4,4096]{1,0:T(4,128)(2,1)} %bitcast.16), channel_id=1, source_target_pairs={{0,1},{1,0},{2,3},{3,2},{4,5},{5,4},{6,7},{7,6},{8,9},{9,8},{10,11... | collective-permute-start | bytes 98312 | tf_op jit(solution)/shard_map/ppermute | solution.py:26
  2.7 7.1 %collective-permute-start.1 = (bf16[4,4096]{1,0:T(4,128)(2,1)S(1)}, bf16[4,4096]{1,0:T(4,128)(2,1)S(1)}, u32[]{:S(2)}, u32[]{:S(2)}) collective-permute-start(bf16[4,4096]{1,0:T(4,128)(2,1)S(1)} %pack.1.after_ref.refs_0_), channel_id=1, source_target_pairs={{0,6},{1,5},{2,4},{3,7},{4,2},{5,1},{6,0},{7,3},{8,14},{9,13},{10,... | collective-permute-start | bytes 98312 | tf_op jit(solution)/shard_map/ppermute | solution.py:26
  7.7 3.9 %collective-permute-start.2 = (bf16[4,4096]{1,0:T(4,128)(2,1)S(1)}, bf16[4,4096]{1,0:T(4,128)(2,1)S(1)}, u32[]{:S(2)}, u32[]{:S(2)}) collective-permute-start(bf16[4,4096]{1,0:T(4,128)(2,1)S(1)} %pack.1.after_ref.refs_0_), channel_id=1, source_target_pairs={{0,2},{1,3},{2,0},{3,1},{4,6},{5,7},{6,4},{7,5},{8,10},{9,11},{10,... | collective-permute-start | bytes 98312 | tf_op jit(solution)/shard_map/ppermute | solution.py:26
  9.8 1.8 %collective-permute-start.3 = (bf16[4,4096]{1,0:T(4,128)(2,1)S(1)}, bf16[4,4096]{1,0:T(4,128)(2,1)S(1)}, u32[]{:S(2)}, u32[]{:S(2)}) collective-permute-start(bf16[4,4096]{1,0:T(4,128)(2,1)S(1)} %collective-permute-done.1.refs_2_), channel_id=1, source_target_pairs={{0,1},{1,0},{2,3},{3,2},{4,5},{5,4},{6,7},{7,6},{8,9},{9,8},{10,11... | collective-permute-start | bytes 98312 | tf_op jit(solution)/shard_map/ppermute | solution.py:26
  15.8 1.3 %collective-permute-start.4 = (bf16[8,4096]{1,0:T(8,128)(2,1)S(1)}, bf16[8,4096]{1,0:T(8,128)(2,1)S(1)}, u32[]{:S(2)}, u32[]{:S(2)}) collective-permute-start(bf16[8,4096]{1,0:T(8,128)(2,1)S(1)} %get-tuple-element.28), channel_id=1, source_target_pairs={{0,1},{1,0},{2,3},{3,2},{4,5},{5,4},{6,7},{7,6},{8,9},{9,8},{10,11... | collective-permute-start | bytes 196616 | tf_op jit(solution)/shard_map/ppermute | solution.py:26
  17.1 4.0 %collective-permute-start.5 = (bf16[4,4096]{1,0:T(4,128)(2,1)S(1)}, bf16[4,4096]{1,0:T(4,128)(2,1)S(1)}, u32[]{:S(2)}, u32[]{:S(2)}) collective-permute-start(bf16[4,4096]{1,0:T(4,128)(2,1)S(1)} %slice.41), channel_id=1, source_target_pairs={{0,2},{1,3},{2,0},{3,1},{4,6},{5,7},{6,4},{7,5},{8,10},{9,11},{10,... | collective-permute-start | bytes 98312 | tf_op jit(solution)/shard_map/ppermute | solution.py:26
  21.2 4.6 %collective-permute-start.6 = (bf16[4,4096]{1,0:T(4,128)(2,1)S(1)}, bf16[4,4096]{1,0:T(4,128)(2,1)S(1)}, u32[]{:S(2)}, u32[]{:S(2)}) collective-permute-start(bf16[4,4096]{1,0:T(4,128)(2,1)S(1)} %add_convert_fusion), channel_id=1, source_target_pairs={{0,24},{1,29},{2,26},{3,31},{4,28},{5,25},{6,30},{7,27},{8,0},{9,5... | collective-permute-start | bytes 98312 | tf_op jit(solution)/shard_map/ppermute | solution.py:26
  25.7 2.0 %collective-permute-start.7 = (bf16[4,4096]{1,0:T(4,128)(2,1)S(1)}, bf16[4,4096]{1,0:T(4,128)(2,1)S(1)}, u32[]{:S(2)}, u32[]{:S(2)}) collective-permute-start(bf16[4,4096]{1,0:T(4,128)(2,1)S(1)} %collective-permute-done.6), channel_id=1, source_target_pairs={{0,1},{1,0},{2,3},{3,2},{4,5},{5,4},{6,7},{7,6},{8,9},{9,8},{10,11... | collective-permute-start | bytes 98312 | tf_op jit(solution)/shard_map/ppermute | solution.py:26

commit v4 on v3

--- a/solution.py
+++ b/solution.py
@@ -97,7 +97,7 @@
     *, tok_dev, k_dev, split, chunk,
 ):
     del gate_ref, after_ref
-    for at in range(0, up_ref.shape[0], chunk):
+    for at in range(0, up_turned_ref.shape[1], chunk):
         up_turned_ref[:, at : at + chunk] = up_ref[at : at + chunk, :].T
     section_at, hid_at = lax.axis_index("section"), lax.axis_index("hid")
     core_at, chip_at = hid_at % CORES, hid_at // CORES
@@ -114,7 +114,7 @@
     column = lanes((1, columns))
     if split:
         group, place = column // tok_dev, column % tok_dev
-        turn = jnp.where(group < 2, 2 * group, jnp.where(group == 2, 6 - 2 * core_at, 5 + 2 * core_at))
+        turn = jnp.where(group < 2, 4 * group, jnp.where(group == 2, 2 + 4 * core_at, 7 - 4 * core_at))
         slots = (hid_at ^ turn ^ (place // k_dev)) * k_dev + place % k_dev
     else:
         slots = slot_at(slot_row(ids_ref, section_at, tok_dev, k_dev), column).astype(jnp.int32)
@@ -139,7 +139,7 @@
             jax.ShapeDtypeStruct((cap, columns), BF16),
             jax.ShapeDtypeStruct((cap, hidden), BF16),
             jax.ShapeDtypeStruct((tok_dev, 128), F32),
-            jax.ShapeDtypeStruct((hidden, gate.shape[0]), BF16),
+            jax.ShapeDtypeStruct((hidden, gate.shape[0] // 2), BF16),
         ),
         in_specs=[VMEM] * 4 + [ANY],
         out_specs=(VMEM,) * 4,
@@ -149,8 +149,27 @@
     )(ids, hidden_grad, gate, up, after)
 
 
+def turn_kernel(weight_ref, after_ref, out_ref, *, low, chunk):
+    del after_ref
+    for at in range(0, out_ref.shape[1], chunk):
+        out_ref[:, at : at + chunk] = weight_ref[low + at : low + at + chunk, :].T
+
+
+def turned(weight, after, low):
+    width, hidden = weight.shape
+    return pl.pallas_call(
+        functools.partial(turn_kernel, low=low, chunk=512),
+        out_shape=jax.ShapeDtypeStruct((hidden, width - low), BF16),
+        in_specs=[VMEM, ANY],
+        out_specs=VMEM,
+        compiler_params=pltpu.CompilerParams(vmem_limit_bytes=4 << 20),
+        cost_estimate=pl.CostEstimate(flops=0, bytes_accessed=4 * hidden * (width - low), transcendentals=0),
+        name="turn",
+    )(weight, after)
+
+
 def expert_kernel(
-    table_ref, hidden_ref, gate_ref, up_ref, up_turned_ref, *refs, n_blocks, chunk
+    table_ref, hidden_ref, gate_ref, up_ref, low_turned_ref, high_turned_ref, *refs, n_blocks, chunk
 ):
     block_refs = refs[:n_blocks]
     slots_ref, grad_gate_ref, keep_ref, send_ref, gate_turned_ref = refs[n_blocks:]
@@ -176,12 +195,13 @@
     for at in range(0, width, chunk):
         there = slice(at, at + chunk)
         total = jnp.dot(grad_gate, gate_turned_ref[:, there], preferred_element_type=F32)
-        total += jnp.dot(grad_up, up_turned_ref[:, there], preferred_element_type=F32)
+        turned_ref, start = (low_turned_ref, at) if at < width // 2 else (high_turned_ref, at - width // 2)
+        total += jnp.dot(grad_up, turned_ref[:, start : start + chunk], preferred_element_type=F32)
         keep_ref[:, there] = total[:half]
-        send_ref[:, there] = total[half:].astype(send_ref.dtype)
-
-
-def expert(table, hidden_grad, gate, up, up_turned, blocks, send_dtype):
+        send_ref[:, there] = total[half:]
+
+
+def expert(table, hidden_grad, gate, up, low_turned, high_turned, blocks):
     cap, hidden = hidden_grad.shape
     width = gate.shape[0]
     return pl.pallas_call(
@@ -190,9 +210,9 @@
             jax.ShapeDtypeStruct((cap, width), BF16),
             jax.ShapeDtypeStruct((cap, hidden), BF16),
             jax.ShapeDtypeStruct((cap // 2, width), F32),
-            jax.ShapeDtypeStruct((cap // 2, width), send_dtype),
-        ),
-        in_specs=[VMEM] * (5 + len(blocks)),
+            jax.ShapeDtypeStruct((cap // 2, width), F32),
+        ),
+        in_specs=[VMEM] * (6 + len(blocks)),
         out_specs=(VMEM,) * 4,
         scratch_shapes=[pltpu.VMEM((hidden, width), BF16)],
         compiler_params=pltpu.CompilerParams(vmem_limit_bytes=16 << 20),
@@ -200,7 +220,7 @@
             flops=8 * cap * width * hidden, bytes_accessed=4 * width * hidden, transcendentals=cap * hidden
         ),
         name="expert",
-    )(table, hidden_grad, gate, up, up_turned, *blocks)
+    )(table, hidden_grad, gate, up, low_turned, high_turned, *blocks)
 
 
 def weight_kernel(slots_ref, grad_ref, *refs, low, high, chunk):
@@ -242,6 +262,7 @@
 def per_device(layer_input, hidden_grad, gate_weight, up_weight, expert_ids):
     tok_dev = layer_input.shape[1]
     k_dev = tok_dev // 2
+    width = gate_weight.shape[1]
     hids = lax.axis_size("hid")
     split = hids == CORES * CHIPS
     core_at = lax.axis_index("hid") % CORES
@@ -252,38 +273,38 @@
         start = opening(4 * gate.size)
         other = to_other_core(own)
         both = pack(ids, own, other, start, k_dev)
-        far = moved(both, lambda section, hid: (section, hid ^ (4 if hid % CORES else 6)))
-        near = moved(both, lambda section, hid: (section, hid ^ 2))
+        far = moved(both, lambda section, hid: (section, hid ^ (6 if hid % CORES else 2)))
+        near = moved(both, lambda section, hid: (section, hid ^ 4))
         after = both
         columns = 4 * tok_dev
     else:
         after = own
         columns = hids * tok_dev
-    table, hidden_ordered, pick, up_turned = prepare(
+    table, hidden_ordered, pick, low_turned = prepare(
         ids, hidden_grad[0], gate, up, after, columns, tok_dev, k_dev, split
     )
     if split:
-        far, up_turned = lax.optimization_barrier((far, up_turned))
+        far, low_turned = lax.optimization_barrier((far, low_turned))
+        high_turned = turned(up, far, width // 2)
         blocks = [both, near, far, to_other_core(far)]
     else:
+        high_turned = turned(up, own, width // 2)
         blocks = [lax.all_gather(own, "hid", axis=0, tiled=True)]
-    slots, grad_gate, keep, send = expert(
-        table, hidden_ordered, gate, up, up_turned, blocks, BF16 if split else F32
-    )
-    width = gate.shape[0]
-
-    if split:
-        rows, width = keep.shape[0] // 2, gate.shape[0]
+    slots, grad_gate, keep, send = expert(table, hidden_ordered, gate, up, low_turned, high_turned, blocks)
+    if split:
+        rows = keep.shape[0] // 2
         partner = to_other_core(send)
-        keep = keep + partner.astype(F32)
+        weight_grad = weight_gradient(slots, grad_gate, 0, 2 * width // 16)
+        partner, weight_grad = lax.optimization_barrier((partner, weight_grad))
+        keep = keep + partner
         keep, slots, grad_gate = lax.optimization_barrier((keep, slots, grad_gate))
         across = moved(keep[rows:].astype(BF16), lambda section, hid: (section, hid ^ 2))
-        weight_grad = weight_gradient(slots, grad_gate, 0 * width // 16, 9 * width // 16)
+        weight_grad = weight_gradient(slots, grad_gate, 2 * width // 16, 13 * width // 16, weight_grad)
         across, weight_grad = lax.optimization_barrier((across, weight_grad))
         part = (keep[:rows] + across.astype(F32)).astype(BF16)
         part, slots = lax.optimization_barrier((part, slots))
         part = moved(part, lambda section, hid: (section - 1, hid ^ (4 * (hid % CORES))))
-        weight_grad = weight_gradient(slots, grad_gate, 9 * width // 16, 16 * width // 16, weight_grad)
+        weight_grad = weight_gradient(slots, grad_gate, 13 * width // 16, 16 * width // 16, weight_grad)
         part, weight_grad = lax.optimization_barrier((part, weight_grad))
         other = to_other_core(part)
         total = part.astype(F32) + other.astype(F32)

time: 28.7 us -> 27.4 us (0.955)
  waiting for transfers between devices: 4.83 us -> 3.58 us
  starting transfers between devices: 10.9 us -> 9.99 us
  Pallas kernels: 11 us -> 11.9 us
    ppermute x8, waiting for transfers between devices: 4.83 us -> 3.58 us  [moved(): return lax.ppermute(value, ('section', 'hid'), pairs)]
    pallas_call x0 -> x1, Pallas kernels: none -> 1.07 us  [turned(): pl.pallas_call(functools.partial(turn_kernel, low=low, chunk=512), out_sh...]
    pallas_call x1, Pallas kernels: 2 us -> 1.04 us  [prepare(): pl.pallas_call(functools.partial(prepare_kernel, tok_dev=tok_dev, k_dev=k...]
    pallas_call x2 -> x3, Pallas kernels: 4.42 us -> 5.35 us  [weight_gradient(): pl.pallas_call(functools.partial(weight_kernel, low=low, high=high, chunk...]
    ppermute x8, starting transfers between devices: 10.9 us -> 9.99 us  [moved(): return lax.ppermute(value, ('section', 'hid'), pairs)]
  transfers between devices with their start and end apart: 8 -> 8, of which waited for: 6 -> 5; matrix products, arithmetic and copies ran while one was open for 1% -> 1% of each run, Pallas kernels for 23% -> 27%
where the time goes in v4:
time: 27.4 us; the launch traced here: 27.3 us
  Pallas kernels  11.9 us (43%)
  starting transfers between devices  9.99 us (36%)
  waiting for transfers between devices  3.58 us (13%)
  other arithmetic  0.92 us (3%)
  between operations  0.83 us (3%)
    ppermute x8, starting transfers between devices, moved(): return lax.ppermute(value, ('section', 'hid'), pairs)  9.99 us
    pallas_call x3, Pallas kernels, weight_gradient(): pl.pallas_call(functools.partial(weight_kernel, low=low, high=high, chunk...  5.35 us
    pallas_call x1, Pallas kernels, expert(): pl.pallas_call(functools.partial(expert_kernel, n_blocks=len(blocks), chu...  4.03 us
    ppermute x8, waiting for transfers between devices, moved(): return lax.ppermute(value, ('section', 'hid'), pairs)  3.58 us
    pallas_call x1, Pallas kernels, turned(): pl.pallas_call(functools.partial(turn_kernel, low=low, chunk=512), out_sh...  1.07 us
    pallas_call x1, Pallas kernels, prepare(): pl.pallas_call(functools.partial(prepare_kernel, tok_dev=tok_dev, k_dev=k...  1.04 us
    convert_element_type x1, other arithmetic, per_device(): return (grad_in.astype(BF16)[None], weight_grad[None])  0.7 us
  transfers between devices with their start and end apart: 8, of which 5 were waited for; matrix products, arithmetic and copies ran while one was open for 1% of the time, Pallas kernels for 27%

profile of v4, /device:TPU:0, one launch (start us, length us, event | category | flops | bytes accessed | tf_op | source)
XLA Modules:
  0.0 27.3 jit_solution(6816191654189495062)
XLA Ops:
  0.6 0.0 slice-start
  0.6 0.0 slice-start.2
  0.7 0.0 copy-start
  0.7 0.0 copy-start.2
  0.7 0.0 slice-start.1
  0.7 0.0 slice-start.3
  0.7 0.0 copy-start.1
  0.7 0.5 %collective-permute-start = (bf16[4,4096]{1,0:T(4,128)(2,1)}, bf16[4,4096]{1,0:T(4,128)(2,1)S(1)}, u32[]{:S(2)}, u32[]{:S(2)}) collective-permute-start(bf16[4,4096]{1,0:T(4,128)(2,1)} %bitcast.17), channel_id=1, source_target_pairs={{0,1},{1,0},{2,3},{3,2},{4,5},{5,4},{6,7},{7,6},{8,9},{9,8},{10,11... | collective-permute-start | bytes 98312 | tf_op jit(solution)/shard_map/ppermute | solution.py:26
  1.2 1.1 %collective-permute-done.other_ref = bf16[4,4096]{1,0:T(4,128)(2,1)S(1)} collective-permute-done((bf16[4,4096]{1,0:T(4,128)(2,1)}, bf16[4,4096]{1,0:T(4,128)(2,1)S(1)}, u32[]{:S(2)}, u32[]{:S(2)}) %collective-permute-start) | collective-permute-done | bytes 32800 | tf_op jit(solution)/shard_map/ppermute | solution.py:26
  2.3 0.0 copy-done
  2.3 0.0 copy-done.2
  2.3 0.4 %pack.1.after_ref.refs_0_ = bf16[4,4096]{1,0:T(4,128)(2,1)S(1)} custom-call(s32[4,2,32]{2,1,0:T(2,128)S(1)} %bitcast.20, bf16[4,4096]{1,0:T(4,128)(2,1)S(1)} %bitcast.18, bf16[4,4096]{1,0:T(4,128)(2,1)S(1)} %collective-permute-done.other_ref, f32[8,128]{1,0:T(8,128)S(1)} %opening.1.after_ref), custom_call_target="tpu_custom_call" | custom-call | tf_op jit(solution)/shard_map/pack/pallas_call | solution.py:70
  2.7 3.0 %collective-permute-start.1 = (bf16[4,4096]{1,0:T(4,128)(2,1)S(1)}, bf16[4,4096]{1,0:T(4,128)(2,1)S(1)}, u32[]{:S(2)}, u32[]{:S(2)}) collective-permute-start(bf16[4,4096]{1,0:T(4,128)(2,1)S(1)} %pack.1.after_ref.refs_0_), channel_id=1, source_target_pairs={{0,2},{1,7},{2,0},{3,5},{4,6},{5,3},{6,4},{7,1},{8,10},{9,15},{10,... | collective-permute-start | bytes 98312 | tf_op jit(solution)/shard_map/ppermute | solution.py:26
  5.7 2.6 %collective-permute-start.2 = (bf16[4,4096]{1,0:T(4,128)(2,1)S(1)}, bf16[4,4096]{1,0:T(4,128)(2,1)S(1)}, u32[]{:S(2)}, u32[]{:S(2)}) collective-permute-start(bf16[4,4096]{1,0:T(4,128)(2,1)S(1)} %pack.1.after_ref.refs_0_), channel_id=1, source_target_pairs={{0,4},{1,5},{2,6},{3,7},{4,0},{5,1},{6,2},{7,3},{8,12},{9,13},{10,... | collective-permute-start | bytes 98312 | tf_op jit(solution)/shard_map/ppermute | solution.py:26
  8.3 0.0 slice-done
  8.3 0.0 slice-done.2
  8.3 0.0 slice-done.1
  8.3 0.0 slice-done.3
  8.3 0.0 copy-done.1
  8.3 1.0 %prepare.1 = (bf16[16,16]{1,0:T(8,128)(2,1)S(1)}, bf16[16,896]{1,0:T(8,128)(2,1)S(1)}, f32[4,128]{1,0:T(4,128)S(1)}, bf16[896,2048]{1,0:T(8,128)(2,1)S(1)}) custom-call(s32[4,2,32]{2,1,0:T(2,128)S(1)} %bitcast.21, bf16[16,896]{1,0:T(8,128)(2,1)S(1)} %bitcast.19, bf16[4096,896]{1,0:T(8,128)(2,1)S(1)} %bitcast.15, bf16[4096,896]{1,0:T(8,128)(2,1)S(1)} %bitcast.10, ...), custom_call_target="tpu_custom_call" | custom-call | bytes 14680064 | tf_op jit(solution)/shard_map/prepare/pallas_call | solution.py:136
  9.4 0.0 collective-permute-done.1.after_ref.refs_2_
  9.4 0.1 collective-permute-start.3
  9.5 1.1 %turn.1.high_turned_ref = bf16[896,2048]{1,0:T(8,128)(2,1)S(1)} custom-call(bf16[4096,896]{1,0:T(8,128)(2,1)S(1)} %bitcast.11, bf16[4,4096]{1,0:T(4,128)(2,1)S(1)} %collective-permute-done.1.after_ref.refs_2_), custom_call_target="tpu_custom_call" | custom-call | bytes 7340032 | tf_op jit(solution)/shard_map/turn/pallas_call | solution.py:160
  10.5 0.6 %collective-permute-done.2.refs_1_ = bf16[4,4096]{1,0:T(4,128)(2,1)S(1)} collective-permute-done((bf16[4,4096]{1,0:T(4,128)(2,1)S(1)}, bf16[4,4096]{1,0:T(4,128)(2,1)S(1)}, u32[]{:S(2)}, u32[]{:S(2)}) %collective-permute-start.2) | collective-permute-done | bytes 32800 | tf_op jit(solution)/shard_map/ppermute | solution.py:26
  11.1 0.0 collective-permute-done.3.refs_3_
  11.1 4.0 %expert.1 = (bf16[16,4096]{1,0:T(8,128)(2,1)S(1)}, bf16[16,896]{1,0:T(8,128)(2,1)S(1)}, f32[8,4096]{1,0:T(8,128)S(1)}, f32[8,4096]{1,0:T(8,128)S(1)}) custom-call(bf16[16,16]{1,0:T(8,128)(2,1)S(1)} %get-tuple-element.24.table_ref, bf16[16,896]{1,0:T(8,128)(2,1)S(1)} %get-tuple-element.25.hidden_ref, bf16[4096,896]{1,0:T(8,128)(2,1)S(1)} %bitcast.16, ...), custom_call_target="tpu_custom_call" | custom-call | flops 469762048 | bytes 14680064 | tf_op jit(solution)/shard_map/expert/pallas_call | solution.py:207
  15.2 0.2 collective-permute-start.4
  15.3 1.3 %weight_gradient.3.refs_0_ = bf16[4096,896]{1,0:T(8,128)(2,1)} custom-call(bf16[16,4096]{1,0:T(8,128)(2,1)S(1)} %get-tuple-element.40.slots_ref, bf16[16,896]{1,0:T(8,128)(2,1)S(1)} %get-tuple-element.36.grad_ref), custom_call_target="tpu_custom_call" | custom-call | flops 14680064 | bytes 917504 | tf_op jit(solution)/shard_map/weight_gradient/pallas_call | solution.py:244
  16.6 0.0 collective-permute-done.4
  16.6 0.5 %collective-permute-start.5 = (bf16[4,4096]{1,0:T(4,128)(2,1)S(1)}, bf16[4,4096]{1,0:T(4,128)(2,1)S(1)}, u32[]{:S(2)}, u32[]{:S(2)}) collective-permute-start(bf16[4,4096]{1,0:T(4,128)(2,1)S(1)} %slice.41), channel_id=1, source_target_pairs={{0,2},{1,3},{2,0},{3,1},{4,6},{5,7},{6,4},{7,5},{8,10},{9,11},{10,... | collective-permute-start | bytes 98312 | tf_op jit(solution)/shard_map/ppermute | solution.py:26
  17.1 2.7 %weight_gradient.4.refs_0_ = bf16[4096,896]{1,0:T(8,128)(2,1)} custom-call(bf16[16,4096]{1,0:T(8,128)(2,1)S(1)} %get-tuple-element.40.slots_ref, bf16[16,896]{1,0:T(8,128)(2,1)S(1)} %get-tuple-element.36.grad_ref, bf16[4096,896]{1,0:T(8,128)(2,1)} %weight_gradient.3.refs_0_), custom_call_target="tpu_custom_call", output_to_operand_aliasing={{}: (2, {})} | custom-call | flops 80740352 | bytes 5046272 | tf_op jit(solution)/shard_map/weight_gradient/pallas_call | solution.py:244
  19.8 0.8 %collective-permute-done.5 = bf16[4,4096]{1,0:T(4,128)(2,1)S(1)} collective-permute-done((bf16[4,4096]{1,0:T(4,128)(2,1)S(1)}, bf16[4,4096]{1,0:T(4,128)(2,1)S(1)}, u32[]{:S(2)}, u32[]{:S(2)}) %collective-permute-start.5) | collective-permute-done | bytes 32800 | tf_op jit(solution)/shard_map/ppermute | solution.py:26
  20.6 2.5 %collective-permute-start.6 = (bf16[4,4096]{1,0:T(4,128)(2,1)S(1)}, bf16[4,4096]{1,0:T(4,128)(2,1)S(1)}, u32[]{:S(2)}, u32[]{:S(2)}) collective-permute-start(bf16[4,4096]{1,0:T(4,128)(2,1)S(1)} %add_convert_fusion), channel_id=1, source_target_pairs={{0,24},{1,29},{2,26},{3,31},{4,28},{5,25},{6,30},{7,27},{8,0},{9,5... | collective-permute-start | bytes 98312 | tf_op jit(solution)/shard_map/ppermute | solution.py:26
  23.2 1.4 %weight_gradient.5 = bf16[4096,896]{1,0:T(8,128)(2,1)} custom-call(bf16[16,4096]{1,0:T(8,128)(2,1)S(1)} %get-tuple-element.40.slots_ref, bf16[16,896]{1,0:T(8,128)(2,1)S(1)} %get-tuple-element.36.grad_ref, bf16[4096,896]{1,0:T(8,128)(2,1)} %weight_gradient.4.refs_0_), custom_call_target="tpu_custom_call", output_to_operand_aliasing={{}: (2, {})} | custom-call | flops 22020096 | bytes 1376256 | tf_op jit(solution)/shard_map/weight_gradient/pallas_call | solution.py:244
  24.6 0.4 %collective-permute-done.6 = bf16[4,4096]{1,0:T(4,128)(2,1)S(1)} collective-permute-done((bf16[4,4096]{1,0:T(4,128)(2,1)S(1)}, bf16[4,4096]{1,0:T(4,128)(2,1)S(1)}, u32[]{:S(2)}, u32[]{:S(2)}) %collective-permute-start.6) | collective-permute-done | bytes 32800 | tf_op jit(solution)/shard_map/ppermute | solution.py:26
  25.0 0.7 %collective-permute-start.7 = (bf16[4,4096]{1,0:T(4,128)(2,1)S(1)}, bf16[4,4096]{1,0:T(4,128)(2,1)S(1)}, u32[]{:S(2)}, u32[]{:S(2)}) collective-permute-start(bf16[4,4096]{1,0:T(4,128)(2,1)S(1)} %collective-permute-done.6), channel_id=1, source_target_pairs={{0,1},{1,0},{2,3},{3,2},{4,5},{5,4},{6,7},{7,6},{8,9},{9,8},{10,11... | collective-permute-start | bytes 98312 | tf_op jit(solution)/shard_map/ppermute | solution.py:26
  25.6 0.1 compare_reduce_fusion.1
  25.8 0.7 %collective-permute-done.7 = bf16[4,4096]{1,0:T(4,128)(2,1)S(1)} collective-permute-done((bf16[4,4096]{1,0:T(4,128)(2,1)S(1)}, bf16[4,4096]{1,0:T(4,128)(2,1)S(1)}, u32[]{:S(2)}, u32[]{:S(2)}) %collective-permute-start.7) | collective-permute-done | bytes 32800 | tf_op jit(solution)/shard_map/ppermute | solution.py:26
  26.6 0.7 %select_convert_fusion = bf16[1,4,4096]{2,1,0:T(4,128)(2,1)} fusion(f32[4096]{0:T(1024)S(1)} %bitcast.24, f32[4096]{0:T(1024)S(1)} %bitcast.23, pred[4]{0:T(512)(128)(4,1)S(1)} %get-tuple-element.45, pred[4]{0:T(512)(128)(4,1)S(1)} %get-tuple-element.44), kind=kLoop, calls=%fused_computation.1 | loop fusion | flops 32768 | bytes 65544 | tf_op jit(solution)/shard_map/convert_element_type | solution.py:320
  (9 shorter events, 0.1 us)
Async XLA Ops:
  0.6 7.7 %slice-start = ((s8[7340032]{0:T(1024)(128)(4,1)}), s8[4194304]{0:T(1024)(128)(4,1)S(1)}, s32[]{:S(2)}) async-start(s8[7340032]{0:T(1024)(128)(4,1)} %bitcast.8), calls=%async_computation | async-start | bytes 8388608
  0.6 7.6 %slice-start.2 = ((s8[7340032]{0:T(1024)(128)(4,1)}), s8[4194304]{0:T(1024)(128)(4,1)S(1)}, s32[]{:S(2)}) async-start(s8[7340032]{0:T(1024)(128)(4,1)} %bitcast.13), calls=%async_computation.2 | async-start | bytes 8388608
  0.7 1.6 %copy-start = (bf16[1,4,4096]{2,1,0:T(4,128)(2,1)S(1)}, bf16[1,4,4096]{2,1,0:T(4,128)(2,1)}, u32[]{:S(2)}) copy-start(bf16[1,4,4096]{2,1,0:T(4,128)(2,1)} %param.5) | copy-start | bytes 98308
  0.7 1.6 %copy-start.2 = (s32[4,32,2]{1,2,0:T(2,128)S(1)}, s32[4,32,2]{1,2,0:T(2,128)}, u32[]{:S(2)}) copy-start(s32[4,32,2]{1,2,0:T(2,128)} %param.9) | copy-start | bytes 3076
  0.7 7.6 %slice-start.1 = ((s8[7340032]{0:T(1024)(128)(4,1)}), s8[3145728]{0:T(1024)(128)(4,1)S(1)}, s32[]{:S(2)}) async-start(s8[7340032]{0:T(1024)(128)(4,1)} %bitcast.8), calls=%async_computation.1 | async-start | bytes 6291456
  0.7 7.6 %slice-start.3 = ((s8[7340032]{0:T(1024)(128)(4,1)}), s8[3145728]{0:T(1024)(128)(4,1)S(1)}, s32[]{:S(2)}) async-start(s8[7340032]{0:T(1024)(128)(4,1)} %bitcast.13), calls=%async_computation.3 | async-start | bytes 6291456
  0.7 7.6 %copy-start.1 = (bf16[1,16,896]{2,1,0:T(8,128)(2,1)S(1)}, bf16[1,16,896]{2,1,0:T(8,128)(2,1)}, u32[]{:S(2)}) copy-start(bf16[1,16,896]{2,1,0:T(8,128)(2,1)} %param.6) | copy-start | bytes 86020
  0.7 1.6 %collective-permute-start = (bf16[4,4096]{1,0:T(4,128)(2,1)}, bf16[4,4096]{1,0:T(4,128)(2,1)S(1)}, u32[]{:S(2)}, u32[]{:S(2)}) collective-permute-start(bf16[4,4096]{1,0:T(4,128)(2,1)} %bitcast.17), channel_id=1, source_target_pairs={{0,1},{1,0},{2,3},{3,2},{4,5},{5,4},{6,7},{7,6},{8,9},{9,8},{10,11... | collective-permute-start | bytes 98312 | tf_op jit(solution)/shard_map/ppermute | solution.py:26
  2.7 6.7 %collective-permute-start.1 = (bf16[4,4096]{1,0:T(4,128)(2,1)S(1)}, bf16[4,4096]{1,0:T(4,128)(2,1)S(1)}, u32[]{:S(2)}, u32[]{:S(2)}) collective-permute-start(bf16[4,4096]{1,0:T(4,128)(2,1)S(1)} %pack.1.after_ref.refs_0_), channel_id=1, source_target_pairs={{0,2},{1,7},{2,0},{3,5},{4,6},{5,3},{6,4},{7,1},{8,10},{9,15},{10,... | collective-permute-start | bytes 98312 | tf_op jit(solution)/shard_map/ppermute | solution.py:26
  5.7 5.4 %collective-permute-start.2 = (bf16[4,4096]{1,0:T(4,128)(2,1)S(1)}, bf16[4,4096]{1,0:T(4,128)(2,1)S(1)}, u32[]{:S(2)}, u32[]{:S(2)}) collective-permute-start(bf16[4,4096]{1,0:T(4,128)(2,1)S(1)} %pack.1.after_ref.refs_0_), channel_id=1, source_target_pairs={{0,4},{1,5},{2,6},{3,7},{4,0},{5,1},{6,2},{7,3},{8,12},{9,13},{10,... | collective-permute-start | bytes 98312 | tf_op jit(solution)/shard_map/ppermute | solution.py:26
  9.4 1.7 %collective-permute-start.3 = (bf16[4,4096]{1,0:T(4,128)(2,1)S(1)}, bf16[4,4096]{1,0:T(4,128)(2,1)S(1)}, u32[]{:S(2)}, u32[]{:S(2)}) collective-permute-start(bf16[4,4096]{1,0:T(4,128)(2,1)S(1)} %collective-permute-done.1.after_ref.refs_2_), channel_id=1, source_target_pairs={{0,1},{1,0},{2,3},{3,2},{4,5},{5,4},{6,7},{7,6},{8,9},{9,8},{10,11... | collective-permute-start | bytes 98312 | tf_op jit(solution)/shard_map/ppermute | solution.py:26
  15.2 1.4 %collective-permute-start.4 = (f32[8,4096]{1,0:T(8,128)S(1)}, f32[8,4096]{1,0:T(8,128)S(1)}, u32[]{:S(2)}, u32[]{:S(2)}) collective-permute-start(f32[8,4096]{1,0:T(8,128)S(1)} %get-tuple-element.30), channel_id=1, source_target_pairs={{0,1},{1,0},{2,3},{3,2},{4,5},{5,4},{6,7},{7,6},{8,9},{9,8},{10,11... | collective-permute-start | bytes 393224 | tf_op jit(solution)/shard_map/ppermute | solution.py:26
  16.6 4.0 %collective-permute-start.5 = (bf16[4,4096]{1,0:T(4,128)(2,1)S(1)}, bf16[4,4096]{1,0:T(4,128)(2,1)S(1)}, u32[]{:S(2)}, u32[]{:S(2)}) collective-permute-start(bf16[4,4096]{1,0:T(4,128)(2,1)S(1)} %slice.41), channel_id=1, source_target_pairs={{0,2},{1,3},{2,0},{3,1},{4,6},{5,7},{6,4},{7,5},{8,10},{9,11},{10,... | collective-permute-start | bytes 98312 | tf_op jit(solution)/shard_map/ppermute | solution.py:26
  20.6 4.3 %collective-permute-start.6 = (bf16[4,4096]{1,0:T(4,128)(2,1)S(1)}, bf16[4,4096]{1,0:T(4,128)(2,1)S(1)}, u32[]{:S(2)}, u32[]{:S(2)}) collective-permute-start(bf16[4,4096]{1,0:T(4,128)(2,1)S(1)} %add_convert_fusion), channel_id=1, source_target_pairs={{0,24},{1,29},{2,26},{3,31},{4,28},{5,25},{6,30},{7,27},{8,0},{9,5... | collective-permute-start | bytes 98312 | tf_op jit(solution)/shard_map/ppermute | solution.py:26
  25.0 1.5 %collective-permute-start.7 = (bf16[4,4096]{1,0:T(4,128)(2,1)S(1)}, bf16[4,4096]{1,0:T(4,128)(2,1)S(1)}, u32[]{:S(2)}, u32[]{:S(2)}) collective-permute-start(bf16[4,4096]{1,0:T(4,128)(2,1)S(1)} %collective-permute-done.6), channel_id=1, source_target_pairs={{0,1},{1,0},{2,3},{3,2},{4,5},{5,4},{6,7},{7,6},{8,9},{9,8},{10,11... | collective-permute-start | bytes 98312 | tf_op jit(solution)/shard_map/ppermute | solution.py:26

commit v5 on v4

--- a/solution.py
+++ b/solution.py
@@ -52,7 +52,7 @@
     return jnp.dot(slot_of.astype(BF16), place, preferred_element_type=F32)[0:1]
 
 
-def pack_kernel(ids_ref, own_ref, other_ref, after_ref, out_ref, *, tok_dev, k_dev):
+def pack_table_kernel(ids_ref, after_ref, table_ref, *, tok_dev, k_dev):
     del after_ref
     hid_at = lax.axis_index("hid")
     slot_of = slot_row(ids_ref, lax.axis_index("section"), tok_dev, k_dev)
@@ -60,21 +60,34 @@
     slots = slot_at(slot_of, (hid_at ^ (column // tok_dev)) * tok_dev + column % tok_dev)
     row = lanes((2 * k_dev, 1), 0)
     wanted = (hid_at ^ (row // k_dev)) * k_dev + row % k_dev
-    table = jnp.where(wanted.astype(F32) == slots, 1.0, 0.0).astype(BF16)
+    table_ref[...] = jnp.where(wanted.astype(F32) == slots, 1.0, 0.0).astype(BF16)
+
+
+def pack_table(ids, after, tok_dev, k_dev):
+    return pl.pallas_call(
+        functools.partial(pack_table_kernel, tok_dev=tok_dev, k_dev=k_dev),
+        out_shape=jax.ShapeDtypeStruct((2 * k_dev, 2 * tok_dev), BF16),
+        in_specs=[VMEM, ANY],
+        out_specs=VMEM,
+        compiler_params=pltpu.CompilerParams(vmem_limit_bytes=4 << 20),
+        name="pack_table",
+    )(ids, after)
+
+
+def pack_kernel(table_ref, own_ref, other_ref, out_ref):
     rows = jnp.concatenate([own_ref[...].astype(F32), other_ref[...].astype(F32)], axis=0)
-    out_ref[...] = jnp.dot(table, rows.astype(BF16), preferred_element_type=F32).astype(BF16)
-
-
-def pack(ids, own, other, after, k_dev):
-    tok_dev, width = own.shape
-    return pl.pallas_call(
-        functools.partial(pack_kernel, tok_dev=tok_dev, k_dev=k_dev),
-        out_shape=jax.ShapeDtypeStruct((2 * k_dev, width), BF16),
-        in_specs=[VMEM] * 3 + [ANY],
+    out_ref[...] = jnp.dot(table_ref[...], rows.astype(BF16), preferred_element_type=F32).astype(BF16)
+
+
+def pack(table, own, other):
+    return pl.pallas_call(
+        pack_kernel,
+        out_shape=jax.ShapeDtypeStruct((table.shape[0], own.shape[1]), BF16),
+        in_specs=[VMEM] * 3,
         out_specs=VMEM,
         compiler_params=pltpu.CompilerParams(vmem_limit_bytes=4 << 20),
         name="pack",
-    )(ids, own, other, after)
+    )(table, own, other)
 
 
 def open_kernel(out_ref):
@@ -272,7 +285,7 @@
     if split:
         start = opening(4 * gate.size)
         other = to_other_core(own)
-        both = pack(ids, own, other, start, k_dev)
+        both = pack(pack_table(ids, start, tok_dev, k_dev), own, other)
         far = moved(both, lambda section, hid: (section, hid ^ (6 if hid % CORES else 2)))
         near = moved(both, lambda section, hid: (section, hid ^ 4))
         after = both
@@ -306,9 +319,10 @@
         part = moved(part, lambda section, hid: (section - 1, hid ^ (4 * (hid % CORES))))
         weight_grad = weight_gradient(slots, grad_gate, 13 * width // 16, 16 * width // 16, weight_grad)
         part, weight_grad = lax.optimization_barrier((part, weight_grad))
-        other = to_other_core(part)
-        total = part.astype(F32) + other.astype(F32)
-        own_total = jnp.where(core_at == 0, total[:k_dev], total[k_dev:])
+        sent = jnp.where(core_at == 0, part[k_dev:], part[:k_dev])
+        mine = jnp.where(core_at == 0, part[:k_dev], part[k_dev:])
+        other = to_other_core(sent)
+        own_total = mine.astype(F32) + other.astype(F32)
     else:
         weight_grad = weight_gradient(slots, grad_gate, 0, width)
         whole = jnp.concatenate([keep, send], axis=0)

time: 27.4 us -> 27.2 us (level)
  waiting for transfers between devices: 3.58 us -> 2.79 us
  starting transfers between devices: 9.99 us -> 10.3 us
    ppermute x8, waiting for transfers between devices: 3.58 us -> 2.79 us  [moved(): return lax.ppermute(value, ('section', 'hid'), pairs)]
  transfers between devices with their start and end apart: 8 -> 8, of which waited for: 5 -> 5; matrix products, arithmetic and copies ran while one was open for 1% -> 1% of each run, Pallas kernels for 27% -> 28%
where the time goes in v5:
time: 27.2 us; the launch traced here: 27.1 us
  Pallas kernels  11.9 us (44%)
  starting transfers between devices  10.3 us (38%)
  waiting for transfers between devices  2.79 us (10%)
  other arithmetic  0.95 us (3%)
  between operations  0.83 us (3%)
  local copies, waits for them, and re-layouts  0.34 us (1%)
    ppermute x8, starting transfers between devices, moved(): return lax.ppermute(value, ('section', 'hid'), pairs)  10.3 us
    pallas_call x3, Pallas kernels, weight_gradient(): pl.pallas_call(functools.partial(weight_kernel, low=low, high=high, chunk...  5.35 us
    pallas_call x1, Pallas kernels, expert(): pl.pallas_call(functools.partial(expert_kernel, n_blocks=len(blocks), chu...  4.03 us
    ppermute x8, waiting for transfers between devices, moved(): return lax.ppermute(value, ('section', 'hid'), pairs)  2.79 us
    pallas_call x1, Pallas kernels, turned(): pl.pallas_call(functools.partial(turn_kernel, low=low, chunk=512), out_sh...  1.07 us
    pallas_call x1, Pallas kernels, prepare(): pl.pallas_call(functools.partial(prepare_kernel, tok_dev=tok_dev, k_dev=k...  1.04 us
    convert_element_type x1, other arithmetic, per_device(): return (grad_in.astype(BF16)[None], weight_grad[None])  0.7 us
  transfers between devices with their start and end apart: 8, of which 5 were waited for; matrix products, arithmetic and copies ran while one was open for 1% of the time, Pallas kernels for 28%

profile of v5, /device:TPU:0, one launch (start us, length us, event | category | flops | bytes accessed | tf_op | source)
XLA Modules:
  0.0 27.1 jit_solution(11329510435538232325)
XLA Ops:
  0.6 0.0 slice-start
  0.6 0.0 slice-start.2
  0.7 0.0 copy-start.2
  0.7 0.0 copy-start
  0.7 0.0 slice-start.1
  0.7 0.0 slice-start.3
  0.7 0.0 copy-start.1
  0.7 0.5 %collective-permute-start = (bf16[4,4096]{1,0:T(4,128)(2,1)}, bf16[4,4096]{1,0:T(4,128)(2,1)S(1)}, u32[]{:S(2)}, u32[]{:S(2)}) collective-permute-start(bf16[4,4096]{1,0:T(4,128)(2,1)} %bitcast.17), channel_id=1, source_target_pairs={{0,1},{1,0},{2,3},{3,2},{4,5},{5,4},{6,7},{7,6},{8,9},{9,8},{10,11... | collective-permute-start | bytes 98312 | tf_op jit(solution)/shard_map/ppermute | solution.py:26
  1.2 0.3 copy-done.2
  1.5 0.2 pack_table.1.table_ref
  1.7 0.6 %collective-permute-done.other_ref = bf16[4,4096]{1,0:T(4,128)(2,1)S(1)} collective-permute-done((bf16[4,4096]{1,0:T(4,128)(2,1)}, bf16[4,4096]{1,0:T(4,128)(2,1)S(1)}, u32[]{:S(2)}, u32[]{:S(2)}) %collective-permute-start) | collective-permute-done | bytes 32800 | tf_op jit(solution)/shard_map/ppermute | solution.py:26
  2.3 0.0 copy-done
  2.3 0.2 pack.1.after_ref.refs_0_
  2.5 3.0 %collective-permute-start.1 = (bf16[4,4096]{1,0:T(4,128)(2,1)S(1)}, bf16[4,4096]{1,0:T(4,128)(2,1)S(1)}, u32[]{:S(2)}, u32[]{:S(2)}) collective-permute-start(bf16[4,4096]{1,0:T(4,128)(2,1)S(1)} %pack.1.after_ref.refs_0_), channel_id=1, source_target_pairs={{0,2},{1,7},{2,0},{3,5},{4,6},{5,3},{6,4},{7,1},{8,10},{9,15},{10,... | collective-permute-start | bytes 98312 | tf_op jit(solution)/shard_map/ppermute | solution.py:26
  5.4 2.6 %collective-permute-start.2 = (bf16[4,4096]{1,0:T(4,128)(2,1)S(1)}, bf16[4,4096]{1,0:T(4,128)(2,1)S(1)}, u32[]{:S(2)}, u32[]{:S(2)}) collective-permute-start(bf16[4,4096]{1,0:T(4,128)(2,1)S(1)} %pack.1.after_ref.refs_0_), channel_id=1, source_target_pairs={{0,4},{1,5},{2,6},{3,7},{4,0},{5,1},{6,2},{7,3},{8,12},{9,13},{10,... | collective-permute-start | bytes 98312 | tf_op jit(solution)/shard_map/ppermute | solution.py:26
  8.0 0.0 slice-done
  8.0 0.0 slice-done.2
  8.0 0.0 slice-done.1
  8.0 0.0 slice-done.3
  8.0 0.0 copy-done.1
  8.1 1.0 %prepare.1 = (bf16[16,16]{1,0:T(8,128)(2,1)S(1)}, bf16[16,896]{1,0:T(8,128)(2,1)S(1)}, f32[4,128]{1,0:T(4,128)S(1)}, bf16[896,2048]{1,0:T(8,128)(2,1)S(1)}) custom-call(s32[4,2,32]{2,1,0:T(2,128)S(1)} %bitcast.21, bf16[16,896]{1,0:T(8,128)(2,1)S(1)} %bitcast.19, bf16[4096,896]{1,0:T(8,128)(2,1)S(1)} %bitcast.15, bf16[4096,896]{1,0:T(8,128)(2,1)S(1)} %bitcast.10, ...), custom_call_target="tpu_custom_call" | custom-call | bytes 14680064 | tf_op jit(solution)/shard_map/prepare/pallas_call | solution.py:149
  9.1 0.0 collective-permute-done.1.after_ref.refs_2_
  9.1 0.1 collective-permute-start.3
  9.2 1.1 %turn.1.high_turned_ref = bf16[896,2048]{1,0:T(8,128)(2,1)S(1)} custom-call(bf16[4096,896]{1,0:T(8,128)(2,1)S(1)} %bitcast.11, bf16[4,4096]{1,0:T(4,128)(2,1)S(1)} %collective-permute-done.1.after_ref.refs_2_), custom_call_target="tpu_custom_call" | custom-call | bytes 7340032 | tf_op jit(solution)/shard_map/turn/pallas_call | solution.py:173
  10.3 0.6 %collective-permute-done.2.refs_1_ = bf16[4,4096]{1,0:T(4,128)(2,1)S(1)} collective-permute-done((bf16[4,4096]{1,0:T(4,128)(2,1)S(1)}, bf16[4,4096]{1,0:T(4,128)(2,1)S(1)}, u32[]{:S(2)}, u32[]{:S(2)}) %collective-permute-start.2) | collective-permute-done | bytes 32800 | tf_op jit(solution)/shard_map/ppermute | solution.py:26
  10.9 0.0 collective-permute-done.3.refs_3_
  10.9 4.0 %expert.1 = (bf16[16,4096]{1,0:T(8,128)(2,1)S(1)}, bf16[16,896]{1,0:T(8,128)(2,1)S(1)}, f32[8,4096]{1,0:T(8,128)S(1)}, f32[8,4096]{1,0:T(8,128)S(1)}) custom-call(bf16[16,16]{1,0:T(8,128)(2,1)S(1)} %get-tuple-element.24.table_ref, bf16[16,896]{1,0:T(8,128)(2,1)S(1)} %get-tuple-element.25.hidden_ref, bf16[4096,896]{1,0:T(8,128)(2,1)S(1)} %bitcast.16, ...), custom_call_target="tpu_custom_call" | custom-call | flops 469762048 | bytes 14680064 | tf_op jit(solution)/shard_map/expert/pallas_call | solution.py:220
  14.9 0.2 collective-permute-start.4
  15.1 1.3 %weight_gradient.3.refs_0_ = bf16[4096,896]{1,0:T(8,128)(2,1)} custom-call(bf16[16,4096]{1,0:T(8,128)(2,1)S(1)} %get-tuple-element.40.slots_ref, bf16[16,896]{1,0:T(8,128)(2,1)S(1)} %get-tuple-element.36.grad_ref), custom_call_target="tpu_custom_call" | custom-call | flops 14680064 | bytes 917504 | tf_op jit(solution)/shard_map/weight_gradient/pallas_call | solution.py:257
  16.3 0.0 collective-permute-done.4
  16.4 0.7 %collective-permute-start.5 = (bf16[4,4096]{1,0:T(4,128)(2,1)S(1)}, bf16[4,4096]{1,0:T(4,128)(2,1)S(1)}, u32[]{:S(2)}, u32[]{:S(2)}) collective-permute-start(bf16[4,4096]{1,0:T(4,128)(2,1)S(1)} %slice.43), channel_id=1, source_target_pairs={{0,2},{1,3},{2,0},{3,1},{4,6},{5,7},{6,4},{7,5},{8,10},{9,11},{10,... | collective-permute-start | bytes 98312 | tf_op jit(solution)/shard_map/ppermute | solution.py:26
  17.1 2.7 %weight_gradient.4.refs_0_ = bf16[4096,896]{1,0:T(8,128)(2,1)} custom-call(bf16[16,4096]{1,0:T(8,128)(2,1)S(1)} %get-tuple-element.40.slots_ref, bf16[16,896]{1,0:T(8,128)(2,1)S(1)} %get-tuple-element.36.grad_ref, bf16[4096,896]{1,0:T(8,128)(2,1)} %weight_gradient.3.refs_0_), custom_call_target="tpu_custom_call", output_to_operand_aliasing={{}: (2, {})} | custom-call | flops 80740352 | bytes 5046272 | tf_op jit(solution)/shard_map/weight_gradient/pallas_call | solution.py:257
  19.8 0.6 %collective-permute-done.5 = bf16[4,4096]{1,0:T(4,128)(2,1)S(1)} collective-permute-done((bf16[4,4096]{1,0:T(4,128)(2,1)S(1)}, bf16[4,4096]{1,0:T(4,128)(2,1)S(1)}, u32[]{:S(2)}, u32[]{:S(2)}) %collective-permute-start.5) | collective-permute-done | bytes 32800 | tf_op jit(solution)/shard_map/ppermute | solution.py:26
  20.4 2.5 %collective-permute-start.6 = (bf16[4,4096]{1,0:T(4,128)(2,1)S(1)}, bf16[4,4096]{1,0:T(4,128)(2,1)S(1)}, u32[]{:S(2)}, u32[]{:S(2)}) collective-permute-start(bf16[4,4096]{1,0:T(4,128)(2,1)S(1)} %add_convert_fusion), channel_id=1, source_target_pairs={{0,24},{1,29},{2,26},{3,31},{4,28},{5,25},{6,30},{7,27},{8,0},{9,5... | collective-permute-start | bytes 98312 | tf_op jit(solution)/shard_map/ppermute | solution.py:26
  22.9 1.4 %weight_gradient.5 = bf16[4096,896]{1,0:T(8,128)(2,1)} custom-call(bf16[16,4096]{1,0:T(8,128)(2,1)S(1)} %get-tuple-element.40.slots_ref, bf16[16,896]{1,0:T(8,128)(2,1)S(1)} %get-tuple-element.36.grad_ref, bf16[4096,896]{1,0:T(8,128)(2,1)} %weight_gradient.4.refs_0_), custom_call_target="tpu_custom_call", output_to_operand_aliasing={{}: (2, {})} | custom-call | flops 22020096 | bytes 1376256 | tf_op jit(solution)/shard_map/weight_gradient/pallas_call | solution.py:257
  24.3 0.4 %collective-permute-done.6 = bf16[4,4096]{1,0:T(4,128)(2,1)S(1)} collective-permute-done((bf16[4,4096]{1,0:T(4,128)(2,1)S(1)}, bf16[4,4096]{1,0:T(4,128)(2,1)S(1)}, u32[]{:S(2)}, u32[]{:S(2)}) %collective-permute-start.6) | collective-permute-done | bytes 32800 | tf_op jit(solution)/shard_map/ppermute | solution.py:26
  24.8 0.7 %collective-permute-start.7 = (bf16[2,4096]{1,0:T(2,128)(2,1)S(1)}, bf16[2,4096]{1,0:T(2,128)(2,1)S(1)}, u32[]{:S(2)}, u32[]{:S(2)}) collective-permute-start(bf16[2,4096]{1,0:T(2,128)(2,1)S(1)} %broadcast_select_fusion), channel_id=1, source_target_pairs={{0,1},{1,0},{2,3},{3,2},{4,5},{5,4},{6,7},{7,6},{8,9},{9,8},{10,11... | collective-permute-start | bytes 49160 | tf_op jit(solution)/shard_map/ppermute | solution.py:26
  25.5 0.1 compare_reduce_fusion.1
  25.6 0.7 %collective-permute-done.7 = bf16[2,4096]{1,0:T(2,128)(2,1)S(1)} collective-permute-done((bf16[2,4096]{1,0:T(2,128)(2,1)S(1)}, bf16[2,4096]{1,0:T(2,128)(2,1)S(1)}, u32[]{:S(2)}, u32[]{:S(2)}) %collective-permute-start.7) | collective-permute-done | bytes 16416 | tf_op jit(solution)/shard_map/ppermute | solution.py:26
  26.4 0.7 %select_convert_fusion = bf16[1,4,4096]{2,1,0:T(4,128)(2,1)} fusion(f32[4096]{0:T(1024)S(1)} %bitcast.24, f32[4096]{0:T(1024)S(1)} %bitcast.23, pred[4]{0:T(512)(128)(4,1)S(1)} %get-tuple-element.45, pred[4]{0:T(512)(128)(4,1)S(1)} %get-tuple-element.44), kind=kLoop, calls=%fused_computation.1 | loop fusion | flops 32768 | bytes 65544 | tf_op jit(solution)/shard_map/convert_element_type | solution.py:334
  (9 shorter events, 0.1 us)
Async XLA Ops:
  0.6 7.4 %slice-start = ((s8[7340032]{0:T(1024)(128)(4,1)}), s8[4194304]{0:T(1024)(128)(4,1)S(1)}, s32[]{:S(2)}) async-start(s8[7340032]{0:T(1024)(128)(4,1)} %bitcast.8), calls=%async_computation | async-start | bytes 8388608
  0.6 7.4 %slice-start.2 = ((s8[7340032]{0:T(1024)(128)(4,1)}), s8[4194304]{0:T(1024)(128)(4,1)S(1)}, s32[]{:S(2)}) async-start(s8[7340032]{0:T(1024)(128)(4,1)} %bitcast.13), calls=%async_computation.2 | async-start | bytes 8388608
  0.7 0.8 %copy-start.2 = (s32[4,32,2]{1,2,0:T(2,128)S(1)}, s32[4,32,2]{1,2,0:T(2,128)}, u32[]{:S(2)}) copy-start(s32[4,32,2]{1,2,0:T(2,128)} %param.9) | copy-start | bytes 3076
  0.7 1.6 %copy-start = (bf16[1,4,4096]{2,1,0:T(4,128)(2,1)S(1)}, bf16[1,4,4096]{2,1,0:T(4,128)(2,1)}, u32[]{:S(2)}) copy-start(bf16[1,4,4096]{2,1,0:T(4,128)(2,1)} %param.5) | copy-start | bytes 98308
  0.7 7.4 %slice-start.1 = ((s8[7340032]{0:T(1024)(128)(4,1)}), s8[3145728]{0:T(1024)(128)(4,1)S(1)}, s32[]{:S(2)}) async-start(s8[7340032]{0:T(1024)(128)(4,1)} %bitcast.8), calls=%async_computation.1 | async-start | bytes 6291456
  0.7 7.4 %slice-start.3 = ((s8[7340032]{0:T(1024)(128)(4,1)}), s8[3145728]{0:T(1024)(128)(4,1)S(1)}, s32[]{:S(2)}) async-start(s8[7340032]{0:T(1024)(128)(4,1)} %bitcast.13), calls=%async_computation.3 | async-start | bytes 6291456
  0.7 7.4 %copy-start.1 = (bf16[1,16,896]{2,1,0:T(8,128)(2,1)S(1)}, bf16[1,16,896]{2,1,0:T(8,128)(2,1)}, u32[]{:S(2)}) copy-start(bf16[1,16,896]{2,1,0:T(8,128)(2,1)} %param.6) | copy-start | bytes 86020
  0.7 1.6 %collective-permute-start = (bf16[4,4096]{1,0:T(4,128)(2,1)}, bf16[4,4096]{1,0:T(4,128)(2,1)S(1)}, u32[]{:S(2)}, u32[]{:S(2)}) collective-permute-start(bf16[4,4096]{1,0:T(4,128)(2,1)} %bitcast.17), channel_id=1, source_target_pairs={{0,1},{1,0},{2,3},{3,2},{4,5},{5,4},{6,7},{7,6},{8,9},{9,8},{10,11... | collective-permute-start | bytes 98312 | tf_op jit(solution)/shard_map/ppermute | solution.py:26
  2.5 6.7 %collective-permute-start.1 = (bf16[4,4096]{1,0:T(4,128)(2,1)S(1)}, bf16[4,4096]{1,0:T(4,128)(2,1)S(1)}, u32[]{:S(2)}, u32[]{:S(2)}) collective-permute-start(bf16[4,4096]{1,0:T(4,128)(2,1)S(1)} %pack.1.after_ref.refs_0_), channel_id=1, source_target_pairs={{0,2},{1,7},{2,0},{3,5},{4,6},{5,3},{6,4},{7,1},{8,10},{9,15},{10,... | collective-permute-start | bytes 98312 | tf_op jit(solution)/shard_map/ppermute | solution.py:26
  5.4 5.4 %collective-permute-start.2 = (bf16[4,4096]{1,0:T(4,128)(2,1)S(1)}, bf16[4,4096]{1,0:T(4,128)(2,1)S(1)}, u32[]{:S(2)}, u32[]{:S(2)}) collective-permute-start(bf16[4,4096]{1,0:T(4,128)(2,1)S(1)} %pack.1.after_ref.refs_0_), channel_id=1, source_target_pairs={{0,4},{1,5},{2,6},{3,7},{4,0},{5,1},{6,2},{7,3},{8,12},{9,13},{10,... | collective-permute-start | bytes 98312 | tf_op jit(solution)/shard_map/ppermute | solution.py:26
  9.1 1.7 %collective-permute-start.3 = (bf16[4,4096]{1,0:T(4,128)(2,1)S(1)}, bf16[4,4096]{1,0:T(4,128)(2,1)S(1)}, u32[]{:S(2)}, u32[]{:S(2)}) collective-permute-start(bf16[4,4096]{1,0:T(4,128)(2,1)S(1)} %collective-permute-done.1.after_ref.refs_2_), channel_id=1, source_target_pairs={{0,1},{1,0},{2,3},{3,2},{4,5},{5,4},{6,7},{7,6},{8,9},{9,8},{10,11... | collective-permute-start | bytes 98312 | tf_op jit(solution)/shard_map/ppermute | solution.py:26
  14.9 1.4 %collective-permute-start.4 = (f32[8,4096]{1,0:T(8,128)S(1)}, f32[8,4096]{1,0:T(8,128)S(1)}, u32[]{:S(2)}, u32[]{:S(2)}) collective-permute-start(f32[8,4096]{1,0:T(8,128)S(1)} %get-tuple-element.30), channel_id=1, source_target_pairs={{0,1},{1,0},{2,3},{3,2},{4,5},{5,4},{6,7},{7,6},{8,9},{9,8},{10,11... | collective-permute-start | bytes 393224 | tf_op jit(solution)/shard_map/ppermute | solution.py:26
  16.4 4.0 %collective-permute-start.5 = (bf16[4,4096]{1,0:T(4,128)(2,1)S(1)}, bf16[4,4096]{1,0:T(4,128)(2,1)S(1)}, u32[]{:S(2)}, u32[]{:S(2)}) collective-permute-start(bf16[4,4096]{1,0:T(4,128)(2,1)S(1)} %slice.43), channel_id=1, source_target_pairs={{0,2},{1,3},{2,0},{3,1},{4,6},{5,7},{6,4},{7,5},{8,10},{9,11},{10,... | collective-permute-start | bytes 98312 | tf_op jit(solution)/shard_map/ppermute | solution.py:26
  20.4 4.3 %collective-permute-start.6 = (bf16[4,4096]{1,0:T(4,128)(2,1)S(1)}, bf16[4,4096]{1,0:T(4,128)(2,1)S(1)}, u32[]{:S(2)}, u32[]{:S(2)}) collective-permute-start(bf16[4,4096]{1,0:T(4,128)(2,1)S(1)} %add_convert_fusion), channel_id=1, source_target_pairs={{0,24},{1,29},{2,26},{3,31},{4,28},{5,25},{6,30},{7,27},{8,0},{9,5... | collective-permute-start | bytes 98312 | tf_op jit(solution)/shard_map/ppermute | solution.py:26
  24.8 1.5 %collective-permute-start.7 = (bf16[2,4096]{1,0:T(2,128)(2,1)S(1)}, bf16[2,4096]{1,0:T(2,128)(2,1)S(1)}, u32[]{:S(2)}, u32[]{:S(2)}) collective-permute-start(bf16[2,4096]{1,0:T(2,128)(2,1)S(1)} %broadcast_select_fusion), channel_id=1, source_target_pairs={{0,1},{1,0},{2,3},{3,2},{4,5},{5,4},{6,7},{7,6},{8,9},{9,8},{10,11... | collective-permute-start | bytes 49160 | tf_op jit(solution)/shard_map/ppermute | solution.py:26

commit v6 on v5

--- a/solution.py
+++ b/solution.py
@@ -59,7 +59,7 @@
     column = lanes((1, 2 * tok_dev))
     slots = slot_at(slot_of, (hid_at ^ (column // tok_dev)) * tok_dev + column % tok_dev)
     row = lanes((2 * k_dev, 1), 0)
-    wanted = (hid_at ^ (row // k_dev)) * k_dev + row % k_dev
+    wanted = (hid_at // CORES * CORES + row // k_dev) * k_dev + row % k_dev
     table_ref[...] = jnp.where(wanted.astype(F32) == slots, 1.0, 0.0).astype(BF16)
 
 
@@ -124,14 +124,11 @@
         device = (chip_at ^ step) * CORES + device % CORES
     wanted = device * k_dev + rank
 
-    column = lanes((1, columns))
-    if split:
-        group, place = column // tok_dev, column % tok_dev
-        turn = jnp.where(group < 2, 4 * group, jnp.where(group == 2, 2 + 4 * core_at, 7 - 4 * core_at))
-        slots = (hid_at ^ turn ^ (place // k_dev)) * k_dev + place % k_dev
-    else:
-        slots = slot_at(slot_row(ids_ref, section_at, tok_dev, k_dev), column).astype(jnp.int32)
-    table_ref[...] = jnp.where(wanted == slots, 1.0, 0.0).astype(BF16)
+    if not split:
+        slots = slot_at(slot_row(ids_ref, section_at, tok_dev, k_dev), lanes((1, columns)))
+        table_ref[...] = jnp.where(wanted.astype(F32) == slots, 1.0, 0.0).astype(BF16)
+    else:
+        table_ref[...] = jnp.zeros_like(table_ref)
 
     order = jnp.where(wanted == lanes((cap, cap)), 1.0, 0.0).astype(BF16)
     hidden_out_ref[...] = jnp.dot(order, hidden_ref[...], preferred_element_type=F32).astype(BF16)
@@ -182,12 +179,20 @@
 
 
 def expert_kernel(
-    table_ref, hidden_ref, gate_ref, up_ref, low_turned_ref, high_turned_ref, *refs, n_blocks, chunk
+    table_ref, hidden_ref, gate_ref, up_ref, low_turned_ref, high_turned_ref, *refs, n_blocks, chunk, split
 ):
     block_refs = refs[:n_blocks]
     slots_ref, grad_gate_ref, keep_ref, send_ref, gate_turned_ref = refs[n_blocks:]
-    rows = jnp.concatenate([ref[...].astype(F32) for ref in block_refs], axis=0).astype(BF16)
-    slots = jnp.dot(table_ref[...], rows, preferred_element_type=F32).astype(BF16)
+    blocks = [ref[...].astype(F32) for ref in block_refs]
+    if split:
+        this_chip, second, far, far_other = blocks
+        first_core = lax.axis_index("hid") % CORES == 0
+        low = jnp.where(first_core, this_chip, second)
+        high = jnp.where(first_core, second, this_chip)
+        slots = jnp.concatenate([low, far, high, far_other], axis=0).astype(BF16)
+    else:
+        rows = jnp.concatenate(blocks, axis=0).astype(BF16)
+        slots = jnp.dot(table_ref[...], rows, preferred_element_type=F32).astype(BF16)
     slots_ref[...] = slots
     cap, width = slots.shape
     half = cap // 2
@@ -214,11 +219,11 @@
         send_ref[:, there] = total[half:]
 
 
-def expert(table, hidden_grad, gate, up, low_turned, high_turned, blocks):
+def expert(table, hidden_grad, gate, up, low_turned, high_turned, blocks, split):
     cap, hidden = hidden_grad.shape
     width = gate.shape[0]
     return pl.pallas_call(
-        functools.partial(expert_kernel, n_blocks=len(blocks), chunk=512),
+        functools.partial(expert_kernel, n_blocks=len(blocks), chunk=512, split=split),
         out_shape=(
             jax.ShapeDtypeStruct((cap, width), BF16),
             jax.ShapeDtypeStruct((cap, hidden), BF16),
@@ -303,7 +308,7 @@
     else:
         high_turned = turned(up, own, width // 2)
         blocks = [lax.all_gather(own, "hid", axis=0, tiled=True)]
-    slots, grad_gate, keep, send = expert(table, hidden_ordered, gate, up, low_turned, high_turned, blocks)
+    slots, grad_gate, keep, send = expert(table, hidden_ordered, gate, up, low_turned, high_turned, blocks, split)
     if split:
         rows = keep.shape[0] // 2
         partner = to_other_core(send)

time: 27.2 us -> 27.1 us (level)
  transfers between devices with their start and end apart: 8 -> 8, of which waited for: 5 -> 5; matrix products, arithmetic and copies ran while one was open for 1% -> 1% of each run, Pallas kernels for 28% -> 29%
where the time goes in v6:
time: 27.1 us; the launch traced here: 27 us
  Pallas kernels  11.8 us (44%)
  starting transfers between devices  10.3 us (38%)
  waiting for transfers between devices  2.79 us (10%)
  other arithmetic  0.95 us (4%)
  between operations  0.83 us (3%)
  local copies, waits for them, and re-layouts  0.34 us (1%)
    ppermute x8, starting transfers between devices, moved(): return lax.ppermute(value, ('section', 'hid'), pairs)  10.3 us
    pallas_call x3, Pallas kernels, weight_gradient(): pl.pallas_call(functools.partial(weight_kernel, low=low, high=high, chunk...  5.35 us
    pallas_call x1, Pallas kernels, expert(): pl.pallas_call(functools.partial(expert_kernel, n_blocks=len(blocks), chu...  3.93 us
    ppermute x8, waiting for transfers between devices, moved(): return lax.ppermute(value, ('section', 'hid'), pairs)  2.79 us
    pallas_call x1, Pallas kernels, turned(): pl.pallas_call(functools.partial(turn_kernel, low=low, chunk=512), out_sh...  1.07 us
    pallas_call x1, Pallas kernels, prepare(): pl.pallas_call(functools.partial(prepare_kernel, tok_dev=tok_dev, k_dev=k...  1.04 us
    convert_element_type x1, other arithmetic, per_device(): return (grad_in.astype(BF16)[None], weight_grad[None])  0.7 us
  transfers between devices with their start and end apart: 8, of which 5 were waited for; matrix products, arithmetic and copies ran while one was open for 1% of the time, Pallas kernels for 29%

profile of v6, /device:TPU:0, one launch (start us, length us, event | category | flops | bytes accessed | tf_op | source)
XLA Modules:
  0.0 27.0 jit_solution(16627656434589579511)
XLA Ops:
  0.6 0.0 slice-start
  0.6 0.0 slice-start.2
  0.7 0.0 copy-start.2
  0.7 0.0 copy-start
  0.7 0.0 slice-start.1
  0.7 0.0 slice-start.3
  0.7 0.0 copy-start.1
  0.7 0.5 %collective-permute-start = (bf16[4,4096]{1,0:T(4,128)(2,1)}, bf16[4,4096]{1,0:T(4,128)(2,1)S(1)}, u32[]{:S(2)}, u32[]{:S(2)}) collective-permute-start(bf16[4,4096]{1,0:T(4,128)(2,1)} %bitcast.17), channel_id=1, source_target_pairs={{0,1},{1,0},{2,3},{3,2},{4,5},{5,4},{6,7},{7,6},{8,9},{9,8},{10,11... | collective-permute-start | bytes 98312 | tf_op jit(solution)/shard_map/ppermute | solution.py:26
  1.2 0.3 copy-done.2
  1.5 0.2 pack_table.1.table_ref
  1.7 0.6 %collective-permute-done.other_ref = bf16[4,4096]{1,0:T(4,128)(2,1)S(1)} collective-permute-done((bf16[4,4096]{1,0:T(4,128)(2,1)}, bf16[4,4096]{1,0:T(4,128)(2,1)S(1)}, u32[]{:S(2)}, u32[]{:S(2)}) %collective-permute-start) | collective-permute-done | bytes 32800 | tf_op jit(solution)/shard_map/ppermute | solution.py:26
  2.3 0.0 copy-done
  2.3 0.2 pack.1.after_ref.refs_0_
  2.5 3.0 %collective-permute-start.1 = (bf16[4,4096]{1,0:T(4,128)(2,1)S(1)}, bf16[4,4096]{1,0:T(4,128)(2,1)S(1)}, u32[]{:S(2)}, u32[]{:S(2)}) collective-permute-start(bf16[4,4096]{1,0:T(4,128)(2,1)S(1)} %pack.1.after_ref.refs_0_), channel_id=1, source_target_pairs={{0,2},{1,7},{2,0},{3,5},{4,6},{5,3},{6,4},{7,1},{8,10},{9,15},{10,... | collective-permute-start | bytes 98312 | tf_op jit(solution)/shard_map/ppermute | solution.py:26
  5.4 2.6 %collective-permute-start.2 = (bf16[4,4096]{1,0:T(4,128)(2,1)S(1)}, bf16[4,4096]{1,0:T(4,128)(2,1)S(1)}, u32[]{:S(2)}, u32[]{:S(2)}) collective-permute-start(bf16[4,4096]{1,0:T(4,128)(2,1)S(1)} %pack.1.after_ref.refs_0_), channel_id=1, source_target_pairs={{0,4},{1,5},{2,6},{3,7},{4,0},{5,1},{6,2},{7,3},{8,12},{9,13},{10,... | collective-permute-start | bytes 98312 | tf_op jit(solution)/shard_map/ppermute | solution.py:26
  8.0 0.0 slice-done
  8.0 0.0 slice-done.2
  8.0 0.0 slice-done.1
  8.0 0.0 slice-done.3
  8.0 0.0 copy-done.1
  8.1 1.0 %prepare.1 = (bf16[16,16]{1,0:T(8,128)(2,1)S(1)}, bf16[16,896]{1,0:T(8,128)(2,1)S(1)}, f32[4,128]{1,0:T(4,128)S(1)}, bf16[896,2048]{1,0:T(8,128)(2,1)S(1)}) custom-call(s32[4,2,32]{2,1,0:T(2,128)S(1)} %bitcast.21, bf16[16,896]{1,0:T(8,128)(2,1)S(1)} %bitcast.19, bf16[4096,896]{1,0:T(8,128)(2,1)S(1)} %bitcast.15, bf16[4096,896]{1,0:T(8,128)(2,1)S(1)} %bitcast.10, ...), custom_call_target="tpu_custom_call" | custom-call | bytes 14680064 | tf_op jit(solution)/shard_map/prepare/pallas_call | solution.py:146
  9.1 0.0 collective-permute-done.1.after_ref.refs_2_
  9.1 0.1 collective-permute-start.3
  9.2 1.1 %turn.1.high_turned_ref = bf16[896,2048]{1,0:T(8,128)(2,1)S(1)} custom-call(bf16[4096,896]{1,0:T(8,128)(2,1)S(1)} %bitcast.11, bf16[4,4096]{1,0:T(4,128)(2,1)S(1)} %collective-permute-done.1.after_ref.refs_2_), custom_call_target="tpu_custom_call" | custom-call | bytes 7340032 | tf_op jit(solution)/shard_map/turn/pallas_call | solution.py:170
  10.3 0.6 %collective-permute-done.2.refs_1_ = bf16[4,4096]{1,0:T(4,128)(2,1)S(1)} collective-permute-done((bf16[4,4096]{1,0:T(4,128)(2,1)S(1)}, bf16[4,4096]{1,0:T(4,128)(2,1)S(1)}, u32[]{:S(2)}, u32[]{:S(2)}) %collective-permute-start.2) | collective-permute-done | bytes 32800 | tf_op jit(solution)/shard_map/ppermute | solution.py:26
  10.9 0.0 collective-permute-done.3.refs_3_
  10.9 3.9 %expert.1 = (bf16[16,4096]{1,0:T(8,128)(2,1)S(1)}, bf16[16,896]{1,0:T(8,128)(2,1)S(1)}, f32[8,4096]{1,0:T(8,128)S(1)}, f32[8,4096]{1,0:T(8,128)S(1)}) custom-call(bf16[16,16]{1,0:T(8,128)(2,1)S(1)} %get-tuple-element.24.table_ref, bf16[16,896]{1,0:T(8,128)(2,1)S(1)} %get-tuple-element.25.hidden_ref, bf16[4096,896]{1,0:T(8,128)(2,1)S(1)} %bitcast.16, ...), custom_call_target="tpu_custom_call" | custom-call | flops 469762048 | bytes 14680064 | tf_op jit(solution)/shard_map/expert/pallas_call | solution.py:225
  14.8 0.2 collective-permute-start.4
  15.0 1.3 %weight_gradient.3.refs_0_ = bf16[4096,896]{1,0:T(8,128)(2,1)} custom-call(bf16[16,4096]{1,0:T(8,128)(2,1)S(1)} %get-tuple-element.40.slots_ref, bf16[16,896]{1,0:T(8,128)(2,1)S(1)} %get-tuple-element.36.grad_ref), custom_call_target="tpu_custom_call" | custom-call | flops 14680064 | bytes 917504 | tf_op jit(solution)/shard_map/weight_gradient/pallas_call | solution.py:262
  16.2 0.0 collective-permute-done.4
  16.3 0.7 %collective-permute-start.5 = (bf16[4,4096]{1,0:T(4,128)(2,1)S(1)}, bf16[4,4096]{1,0:T(4,128)(2,1)S(1)}, u32[]{:S(2)}, u32[]{:S(2)}) collective-permute-start(bf16[4,4096]{1,0:T(4,128)(2,1)S(1)} %slice.43), channel_id=1, source_target_pairs={{0,2},{1,3},{2,0},{3,1},{4,6},{5,7},{6,4},{7,5},{8,10},{9,11},{10,... | collective-permute-start | bytes 98312 | tf_op jit(solution)/shard_map/ppermute | solution.py:26
  17.0 2.7 %weight_gradient.4.refs_0_ = bf16[4096,896]{1,0:T(8,128)(2,1)} custom-call(bf16[16,4096]{1,0:T(8,128)(2,1)S(1)} %get-tuple-element.40.slots_ref, bf16[16,896]{1,0:T(8,128)(2,1)S(1)} %get-tuple-element.36.grad_ref, bf16[4096,896]{1,0:T(8,128)(2,1)} %weight_gradient.3.refs_0_), custom_call_target="tpu_custom_call", output_to_operand_aliasing={{}: (2, {})} | custom-call | flops 80740352 | bytes 5046272 | tf_op jit(solution)/shard_map/weight_gradient/pallas_call | solution.py:262
  19.7 0.6 %collective-permute-done.5 = bf16[4,4096]{1,0:T(4,128)(2,1)S(1)} collective-permute-done((bf16[4,4096]{1,0:T(4,128)(2,1)S(1)}, bf16[4,4096]{1,0:T(4,128)(2,1)S(1)}, u32[]{:S(2)}, u32[]{:S(2)}) %collective-permute-start.5) | collective-permute-done | bytes 32800 | tf_op jit(solution)/shard_map/ppermute | solution.py:26
  20.3 2.5 %collective-permute-start.6 = (bf16[4,4096]{1,0:T(4,128)(2,1)S(1)}, bf16[4,4096]{1,0:T(4,128)(2,1)S(1)}, u32[]{:S(2)}, u32[]{:S(2)}) collective-permute-start(bf16[4,4096]{1,0:T(4,128)(2,1)S(1)} %add_convert_fusion), channel_id=1, source_target_pairs={{0,24},{1,29},{2,26},{3,31},{4,28},{5,25},{6,30},{7,27},{8,0},{9,5... | collective-permute-start | bytes 98312 | tf_op jit(solution)/shard_map/ppermute | solution.py:26
  22.8 1.4 %weight_gradient.5 = bf16[4096,896]{1,0:T(8,128)(2,1)} custom-call(bf16[16,4096]{1,0:T(8,128)(2,1)S(1)} %get-tuple-element.40.slots_ref, bf16[16,896]{1,0:T(8,128)(2,1)S(1)} %get-tuple-element.36.grad_ref, bf16[4096,896]{1,0:T(8,128)(2,1)} %weight_gradient.4.refs_0_), custom_call_target="tpu_custom_call", output_to_operand_aliasing={{}: (2, {})} | custom-call | flops 22020096 | bytes 1376256 | tf_op jit(solution)/shard_map/weight_gradient/pallas_call | solution.py:262
  24.2 0.4 %collective-permute-done.6 = bf16[4,4096]{1,0:T(4,128)(2,1)S(1)} collective-permute-done((bf16[4,4096]{1,0:T(4,128)(2,1)S(1)}, bf16[4,4096]{1,0:T(4,128)(2,1)S(1)}, u32[]{:S(2)}, u32[]{:S(2)}) %collective-permute-start.6) | collective-permute-done | bytes 32800 | tf_op jit(solution)/shard_map/ppermute | solution.py:26
  24.7 0.7 %collective-permute-start.7 = (bf16[2,4096]{1,0:T(2,128)(2,1)S(1)}, bf16[2,4096]{1,0:T(2,128)(2,1)S(1)}, u32[]{:S(2)}, u32[]{:S(2)}) collective-permute-start(bf16[2,4096]{1,0:T(2,128)(2,1)S(1)} %broadcast_select_fusion), channel_id=1, source_target_pairs={{0,1},{1,0},{2,3},{3,2},{4,5},{5,4},{6,7},{7,6},{8,9},{9,8},{10,11... | collective-permute-start | bytes 49160 | tf_op jit(solution)/shard_map/ppermute | solution.py:26
  25.4 0.1 compare_reduce_fusion.1
  25.5 0.7 %collective-permute-done.7 = bf16[2,4096]{1,0:T(2,128)(2,1)S(1)} collective-permute-done((bf16[2,4096]{1,0:T(2,128)(2,1)S(1)}, bf16[2,4096]{1,0:T(2,128)(2,1)S(1)}, u32[]{:S(2)}, u32[]{:S(2)}) %collective-permute-start.7) | collective-permute-done | bytes 16416 | tf_op jit(solution)/shard_map/ppermute | solution.py:26
  26.3 0.7 %select_convert_fusion = bf16[1,4,4096]{2,1,0:T(4,128)(2,1)} fusion(f32[4096]{0:T(1024)S(1)} %bitcast.24, f32[4096]{0:T(1024)S(1)} %bitcast.23, pred[4]{0:T(512)(128)(4,1)S(1)} %get-tuple-element.45, pred[4]{0:T(512)(128)(4,1)S(1)} %get-tuple-element.44), kind=kLoop, calls=%fused_computation.1 | loop fusion | flops 32768 | bytes 65544 | tf_op jit(solution)/shard_map/convert_element_type | solution.py:339
  (9 shorter events, 0.1 us)
Async XLA Ops:
  0.6 7.4 %slice-start = ((s8[7340032]{0:T(1024)(128)(4,1)}), s8[4194304]{0:T(1024)(128)(4,1)S(1)}, s32[]{:S(2)}) async-start(s8[7340032]{0:T(1024)(128)(4,1)} %bitcast.8), calls=%async_computation | async-start | bytes 8388608
  0.6 7.4 %slice-start.2 = ((s8[7340032]{0:T(1024)(128)(4,1)}), s8[4194304]{0:T(1024)(128)(4,1)S(1)}, s32[]{:S(2)}) async-start(s8[7340032]{0:T(1024)(128)(4,1)} %bitcast.13), calls=%async_computation.2 | async-start | bytes 8388608
  0.7 0.8 %copy-start.2 = (s32[4,32,2]{1,2,0:T(2,128)S(1)}, s32[4,32,2]{1,2,0:T(2,128)}, u32[]{:S(2)}) copy-start(s32[4,32,2]{1,2,0:T(2,128)} %param.9) | copy-start | bytes 3076
  0.7 1.6 %copy-start = (bf16[1,4,4096]{2,1,0:T(4,128)(2,1)S(1)}, bf16[1,4,4096]{2,1,0:T(4,128)(2,1)}, u32[]{:S(2)}) copy-start(bf16[1,4,4096]{2,1,0:T(4,128)(2,1)} %param.5) | copy-start | bytes 98308
  0.7 7.4 %slice-start.1 = ((s8[7340032]{0:T(1024)(128)(4,1)}), s8[3145728]{0:T(1024)(128)(4,1)S(1)}, s32[]{:S(2)}) async-start(s8[7340032]{0:T(1024)(128)(4,1)} %bitcast.8), calls=%async_computation.1 | async-start | bytes 6291456
  0.7 7.4 %slice-start.3 = ((s8[7340032]{0:T(1024)(128)(4,1)}), s8[3145728]{0:T(1024)(128)(4,1)S(1)}, s32[]{:S(2)}) async-start(s8[7340032]{0:T(1024)(128)(4,1)} %bitcast.13), calls=%async_computation.3 | async-start | bytes 6291456
  0.7 7.4 %copy-start.1 = (bf16[1,16,896]{2,1,0:T(8,128)(2,1)S(1)}, bf16[1,16,896]{2,1,0:T(8,128)(2,1)}, u32[]{:S(2)}) copy-start(bf16[1,16,896]{2,1,0:T(8,128)(2,1)} %param.6) | copy-start | bytes 86020
  0.7 1.6 %collective-permute-start = (bf16[4,4096]{1,0:T(4,128)(2,1)}, bf16[4,4096]{1,0:T(4,128)(2,1)S(1)}, u32[]{:S(2)}, u32[]{:S(2)}) collective-permute-start(bf16[4,4096]{1,0:T(4,128)(2,1)} %bitcast.17), channel_id=1, source_target_pairs={{0,1},{1,0},{2,3},{3,2},{4,5},{5,4},{6,7},{7,6},{8,9},{9,8},{10,11... | collective-permute-start | bytes 98312 | tf_op jit(solution)/shard_map/ppermute | solution.py:26
  2.5 6.7 %collective-permute-start.1 = (bf16[4,4096]{1,0:T(4,128)(2,1)S(1)}, bf16[4,4096]{1,0:T(4,128)(2,1)S(1)}, u32[]{:S(2)}, u32[]{:S(2)}) collective-permute-start(bf16[4,4096]{1,0:T(4,128)(2,1)S(1)} %pack.1.after_ref.refs_0_), channel_id=1, source_target_pairs={{0,2},{1,7},{2,0},{3,5},{4,6},{5,3},{6,4},{7,1},{8,10},{9,15},{10,... | collective-permute-start | bytes 98312 | tf_op jit(solution)/shard_map/ppermute | solution.py:26
  5.4 5.4 %collective-permute-start.2 = (bf16[4,4096]{1,0:T(4,128)(2,1)S(1)}, bf16[4,4096]{1,0:T(4,128)(2,1)S(1)}, u32[]{:S(2)}, u32[]{:S(2)}) collective-permute-start(bf16[4,4096]{1,0:T(4,128)(2,1)S(1)} %pack.1.after_ref.refs_0_), channel_id=1, source_target_pairs={{0,4},{1,5},{2,6},{3,7},{4,0},{5,1},{6,2},{7,3},{8,12},{9,13},{10,... | collective-permute-start | bytes 98312 | tf_op jit(solution)/shard_map/ppermute | solution.py:26
  9.1 1.7 %collective-permute-start.3 = (bf16[4,4096]{1,0:T(4,128)(2,1)S(1)}, bf16[4,4096]{1,0:T(4,128)(2,1)S(1)}, u32[]{:S(2)}, u32[]{:S(2)}) collective-permute-start(bf16[4,4096]{1,0:T(4,128)(2,1)S(1)} %collective-permute-done.1.after_ref.refs_2_), channel_id=1, source_target_pairs={{0,1},{1,0},{2,3},{3,2},{4,5},{5,4},{6,7},{7,6},{8,9},{9,8},{10,11... | collective-permute-start | bytes 98312 | tf_op jit(solution)/shard_map/ppermute | solution.py:26
  14.8 1.4 %collective-permute-start.4 = (f32[8,4096]{1,0:T(8,128)S(1)}, f32[8,4096]{1,0:T(8,128)S(1)}, u32[]{:S(2)}, u32[]{:S(2)}) collective-permute-start(f32[8,4096]{1,0:T(8,128)S(1)} %get-tuple-element.30), channel_id=1, source_target_pairs={{0,1},{1,0},{2,3},{3,2},{4,5},{5,4},{6,7},{7,6},{8,9},{9,8},{10,11... | collective-permute-start | bytes 393224 | tf_op jit(solution)/shard_map/ppermute | solution.py:26
  16.3 4.0 %collective-permute-start.5 = (bf16[4,4096]{1,0:T(4,128)(2,1)S(1)}, bf16[4,4096]{1,0:T(4,128)(2,1)S(1)}, u32[]{:S(2)}, u32[]{:S(2)}) collective-permute-start(bf16[4,4096]{1,0:T(4,128)(2,1)S(1)} %slice.43), channel_id=1, source_target_pairs={{0,2},{1,3},{2,0},{3,1},{4,6},{5,7},{6,4},{7,5},{8,10},{9,11},{10,... | collective-permute-start | bytes 98312 | tf_op jit(solution)/shard_map/ppermute | solution.py:26
  20.3 4.3 %collective-permute-start.6 = (bf16[4,4096]{1,0:T(4,128)(2,1)S(1)}, bf16[4,4096]{1,0:T(4,128)(2,1)S(1)}, u32[]{:S(2)}, u32[]{:S(2)}) collective-permute-start(bf16[4,4096]{1,0:T(4,128)(2,1)S(1)} %add_convert_fusion), channel_id=1, source_target_pairs={{0,24},{1,29},{2,26},{3,31},{4,28},{5,25},{6,30},{7,27},{8,0},{9,5... | collective-permute-start | bytes 98312 | tf_op jit(solution)/shard_map/ppermute | solution.py:26
  24.7 1.5 %collective-permute-start.7 = (bf16[2,4096]{1,0:T(2,128)(2,1)S(1)}, bf16[2,4096]{1,0:T(2,128)(2,1)S(1)}, u32[]{:S(2)}, u32[]{:S(2)}) collective-permute-start(bf16[2,4096]{1,0:T(2,128)(2,1)S(1)} %broadcast_select_fusion), channel_id=1, source_target_pairs={{0,1},{1,0},{2,3},{3,2},{4,5},{5,4},{6,7},{7,6},{8,9},{9,8},{10,11... | collective-permute-start | bytes 49160 | tf_op jit(solution)/shard_map/ppermute | solution.py:26

commit v7 on v6

--- a/solution.py
+++ b/solution.py
@@ -277,6 +277,28 @@
     )(slots, grad_gate, *([] if out is None else [out]))
 
 
+def close_kernel(part_ref, other_ref, pick_ref, out_ref, *, k_dev):
+    part = part_ref[...].astype(F32)
+    first_core = lax.axis_index("hid") % CORES == 0
+    total = jnp.where(first_core, part[:k_dev], part[k_dev:]) + other_ref[...].astype(F32)
+    pick = pick_ref[:, :1]
+    rows = jnp.zeros(out_ref.shape, F32)
+    for rank in range(k_dev):
+        rows = jnp.where(pick == rank, total[rank : rank + 1], rows)
+    out_ref[...] = rows.astype(out_ref.dtype)
+
+
+def close(part, other, pick, k_dev):
+    return pl.pallas_call(
+        functools.partial(close_kernel, k_dev=k_dev),
+        out_shape=jax.ShapeDtypeStruct((pick.shape[0], part.shape[1]), BF16),
+        in_specs=[VMEM] * 3,
+        out_specs=VMEM,
+        compiler_params=pltpu.CompilerParams(vmem_limit_bytes=4 << 20),
+        name="close",
+    )(part, other, pick)
+
+
 def per_device(layer_input, hidden_grad, gate_weight, up_weight, expert_ids):
     tok_dev = layer_input.shape[1]
     k_dev = tok_dev // 2
@@ -325,18 +347,18 @@
         weight_grad = weight_gradient(slots, grad_gate, 13 * width // 16, 16 * width // 16, weight_grad)
         part, weight_grad = lax.optimization_barrier((part, weight_grad))
         sent = jnp.where(core_at == 0, part[k_dev:], part[:k_dev])
-        mine = jnp.where(core_at == 0, part[:k_dev], part[k_dev:])
         other = to_other_core(sent)
-        own_total = mine.astype(F32) + other.astype(F32)
+        grad_in = close(part, other, pick, k_dev)
     else:
         weight_grad = weight_gradient(slots, grad_gate, 0, width)
         whole = jnp.concatenate([keep, send], axis=0)
         own_total = lax.psum_scatter(whole, "hid", scatter_dimension=0, tiled=True)
         own_total = moved(own_total, lambda section, hid: (section - 1, hid))
-    grad_in = jnp.zeros((tok_dev, own.shape[1]), F32)
-    for rank in range(k_dev):
-        grad_in = jnp.where(pick[:, :1] == rank, own_total[rank : rank + 1], grad_in)
-    return (grad_in.astype(BF16)[None], weight_grad[None])
+        rows = jnp.zeros((tok_dev, own.shape[1]), F32)
+        for rank in range(k_dev):
+            rows = jnp.where(pick[:, :1] == rank, own_total[rank : rank + 1], rows)
+        grad_in = rows.astype(BF16)
+    return (grad_in[None], weight_grad[None])
 
 
 def solution(mesh):

time: 27.1 us -> 27 us (level)
  other arithmetic: 0.95 us -> 0.07 us
  Pallas kernels: 11.8 us -> 12.5 us
    convert_element_type x1 -> x0, other arithmetic: 0.7 us -> none  [per_device(): return (grad_in.astype(BF16)[None], weight_grad[None])]
    pallas_call x0 -> x1, Pallas kernels: none -> 0.7 us  [close(): pl.pallas_call(functools.partial(close_kernel, k_dev=k_dev), out_shape=ja...]
  transfers between devices with their start and end apart: 8 -> 8, of which waited for: 5 -> 5; matrix products, arithmetic and copies ran while one was open for 1% -> 0% of each run, Pallas kernels for 29% -> 29%
where the time goes in v7:
time: 27 us; the launch traced here: 26.9 us
  Pallas kernels  12.5 us (46%)
  starting transfers between devices  10.3 us (38%)
  waiting for transfers between devices  2.93 us (11%)
  between operations  0.82 us (3%)
  local copies, waits for them, and re-layouts  0.31 us (1%)
    ppermute x8, starting transfers between devices, moved(): return lax.ppermute(value, ('section', 'hid'), pairs)  10.3 us
    pallas_call x3, Pallas kernels, weight_gradient(): pl.pallas_call(functools.partial(weight_kernel, low=low, high=high, chunk...  5.35 us
    pallas_call x1, Pallas kernels, expert(): pl.pallas_call(functools.partial(expert_kernel, n_blocks=len(blocks), chu...  3.93 us
    ppermute x8, waiting for transfers between devices, moved(): return lax.ppermute(value, ('section', 'hid'), pairs)  2.93 us
    pallas_call x1, Pallas kernels, turned(): pl.pallas_call(functools.partial(turn_kernel, low=low, chunk=512), out_sh...  1.07 us
    pallas_call x1, Pallas kernels, prepare(): pl.pallas_call(functools.partial(prepare_kernel, tok_dev=tok_dev, k_dev=k...  1.04 us
    pallas_call x1, Pallas kernels, close(): pl.pallas_call(functools.partial(close_kernel, k_dev=k_dev), out_shape=ja...  0.7 us
  transfers between devices with their start and end apart: 8, of which 5 were waited for; matrix products, arithmetic and copies ran while one was open for 0% of the time, Pallas kernels for 29%

profile of v7, /device:TPU:0, one launch (start us, length us, event | category | flops | bytes accessed | tf_op | source)
XLA Modules:
  0.0 26.9 jit_solution(5255173654737814361)
XLA Ops:
  0.6 0.0 slice-start
  0.6 0.0 slice-start.2
  0.7 0.0 copy-start.2
  0.7 0.0 copy-start
  0.7 0.0 slice-start.1
  0.7 0.0 slice-start.3
  0.7 0.0 copy-start.1
  0.7 0.5 %collective-permute-start = (bf16[4,4096]{1,0:T(4,128)(2,1)}, bf16[4,4096]{1,0:T(4,128)(2,1)S(1)}, u32[]{:S(2)}, u32[]{:S(2)}) collective-permute-start(bf16[4,4096]{1,0:T(4,128)(2,1)} %bitcast.16), channel_id=1, source_target_pairs={{0,1},{1,0},{2,3},{3,2},{4,5},{5,4},{6,7},{7,6},{8,9},{9,8},{10,11... | collective-permute-start | bytes 98312 | tf_op jit(solution)/shard_map/ppermute | solution.py:26
  1.2 0.3 copy-done.2
  1.5 0.2 pack_table.1.table_ref
  1.7 0.6 %collective-permute-done.other_ref = bf16[4,4096]{1,0:T(4,128)(2,1)S(1)} collective-permute-done((bf16[4,4096]{1,0:T(4,128)(2,1)}, bf16[4,4096]{1,0:T(4,128)(2,1)S(1)}, u32[]{:S(2)}, u32[]{:S(2)}) %collective-permute-start) | collective-permute-done | bytes 32800 | tf_op jit(solution)/shard_map/ppermute | solution.py:26
  2.3 0.0 copy-done
  2.3 0.2 pack.1.after_ref.refs_0_
  2.5 3.0 %collective-permute-start.1 = (bf16[4,4096]{1,0:T(4,128)(2,1)S(1)}, bf16[4,4096]{1,0:T(4,128)(2,1)S(1)}, u32[]{:S(2)}, u32[]{:S(2)}) collective-permute-start(bf16[4,4096]{1,0:T(4,128)(2,1)S(1)} %pack.1.after_ref.refs_0_), channel_id=1, source_target_pairs={{0,2},{1,7},{2,0},{3,5},{4,6},{5,3},{6,4},{7,1},{8,10},{9,15},{10,... | collective-permute-start | bytes 98312 | tf_op jit(solution)/shard_map/ppermute | solution.py:26
  5.4 2.6 %collective-permute-start.2 = (bf16[4,4096]{1,0:T(4,128)(2,1)S(1)}, bf16[4,4096]{1,0:T(4,128)(2,1)S(1)}, u32[]{:S(2)}, u32[]{:S(2)}) collective-permute-start(bf16[4,4096]{1,0:T(4,128)(2,1)S(1)} %pack.1.after_ref.refs_0_), channel_id=1, source_target_pairs={{0,4},{1,5},{2,6},{3,7},{4,0},{5,1},{6,2},{7,3},{8,12},{9,13},{10,... | collective-permute-start | bytes 98312 | tf_op jit(solution)/shard_map/ppermute | solution.py:26
  8.0 0.0 slice-done
  8.0 0.0 slice-done.2
  8.0 0.0 slice-done.1
  8.0 0.0 slice-done.3
  8.0 0.0 copy-done.1
  8.1 1.0 %prepare.1 = (bf16[16,16]{1,0:T(8,128)(2,1)S(1)}, bf16[16,896]{1,0:T(8,128)(2,1)S(1)}, f32[4,128]{1,0:T(4,128)S(1)}, bf16[896,2048]{1,0:T(8,128)(2,1)S(1)}) custom-call(s32[4,2,32]{2,1,0:T(2,128)S(1)} %bitcast.20, bf16[16,896]{1,0:T(8,128)(2,1)S(1)} %bitcast.18, bf16[4096,896]{1,0:T(8,128)(2,1)S(1)} %bitcast.14, bf16[4096,896]{1,0:T(8,128)(2,1)S(1)} %bitcast.9, ...), custom_call_target="tpu_custom_call" | custom-call | bytes 14680064 | tf_op jit(solution)/shard_map/prepare/pallas_call | solution.py:146
  9.1 0.0 collective-permute-done.1.after_ref.refs_2_
  9.1 0.1 collective-permute-start.3
  9.2 1.1 %turn.1.high_turned_ref = bf16[896,2048]{1,0:T(8,128)(2,1)S(1)} custom-call(bf16[4096,896]{1,0:T(8,128)(2,1)S(1)} %bitcast.10, bf16[4,4096]{1,0:T(4,128)(2,1)S(1)} %collective-permute-done.1.after_ref.refs_2_), custom_call_target="tpu_custom_call" | custom-call | bytes 7340032 | tf_op jit(solution)/shard_map/turn/pallas_call | solution.py:170
  10.3 0.6 %collective-permute-done.2.refs_1_ = bf16[4,4096]{1,0:T(4,128)(2,1)S(1)} collective-permute-done((bf16[4,4096]{1,0:T(4,128)(2,1)S(1)}, bf16[4,4096]{1,0:T(4,128)(2,1)S(1)}, u32[]{:S(2)}, u32[]{:S(2)}) %collective-permute-start.2) | collective-permute-done | bytes 32800 | tf_op jit(solution)/shard_map/ppermute | solution.py:26
  10.9 0.0 collective-permute-done.3.refs_3_
  10.9 3.9 %expert.1 = (bf16[16,4096]{1,0:T(8,128)(2,1)S(1)}, bf16[16,896]{1,0:T(8,128)(2,1)S(1)}, f32[8,4096]{1,0:T(8,128)S(1)}, f32[8,4096]{1,0:T(8,128)S(1)}) custom-call(bf16[16,16]{1,0:T(8,128)(2,1)S(1)} %get-tuple-element.23.table_ref, bf16[16,896]{1,0:T(8,128)(2,1)S(1)} %get-tuple-element.24.hidden_ref, bf16[4096,896]{1,0:T(8,128)(2,1)S(1)} %bitcast.15, ...), custom_call_target="tpu_custom_call" | custom-call | flops 469762048 | bytes 14680064 | tf_op jit(solution)/shard_map/expert/pallas_call | solution.py:225
  14.8 0.2 collective-permute-start.4
  15.0 1.3 %weight_gradient.3.refs_0_ = bf16[4096,896]{1,0:T(8,128)(2,1)} custom-call(bf16[16,4096]{1,0:T(8,128)(2,1)S(1)} %get-tuple-element.39.slots_ref, bf16[16,896]{1,0:T(8,128)(2,1)S(1)} %get-tuple-element.35.grad_ref), custom_call_target="tpu_custom_call" | custom-call | flops 14680064 | bytes 917504 | tf_op jit(solution)/shard_map/weight_gradient/pallas_call | solution.py:262
  16.2 0.0 collective-permute-done.4
  16.3 0.7 %collective-permute-start.5 = (bf16[4,4096]{1,0:T(4,128)(2,1)S(1)}, bf16[4,4096]{1,0:T(4,128)(2,1)S(1)}, u32[]{:S(2)}, u32[]{:S(2)}) collective-permute-start(bf16[4,4096]{1,0:T(4,128)(2,1)S(1)} %slice.22), channel_id=1, source_target_pairs={{0,2},{1,3},{2,0},{3,1},{4,6},{5,7},{6,4},{7,5},{8,10},{9,11},{10,... | collective-permute-start | bytes 98312 | tf_op jit(solution)/shard_map/ppermute | solution.py:26
  17.0 2.7 %weight_gradient.4.refs_0_ = bf16[4096,896]{1,0:T(8,128)(2,1)} custom-call(bf16[16,4096]{1,0:T(8,128)(2,1)S(1)} %get-tuple-element.39.slots_ref, bf16[16,896]{1,0:T(8,128)(2,1)S(1)} %get-tuple-element.35.grad_ref, bf16[4096,896]{1,0:T(8,128)(2,1)} %weight_gradient.3.refs_0_), custom_call_target="tpu_custom_call", output_to_operand_aliasing={{}: (2, {})} | custom-call | flops 80740352 | bytes 5046272 | tf_op jit(solution)/shard_map/weight_gradient/pallas_call | solution.py:262
  19.7 0.6 %collective-permute-done.5 = bf16[4,4096]{1,0:T(4,128)(2,1)S(1)} collective-permute-done((bf16[4,4096]{1,0:T(4,128)(2,1)S(1)}, bf16[4,4096]{1,0:T(4,128)(2,1)S(1)}, u32[]{:S(2)}, u32[]{:S(2)}) %collective-permute-start.5) | collective-permute-done | bytes 32800 | tf_op jit(solution)/shard_map/ppermute | solution.py:26
  20.3 2.5 %collective-permute-start.6 = (bf16[4,4096]{1,0:T(4,128)(2,1)S(1)}, bf16[4,4096]{1,0:T(4,128)(2,1)S(1)}, u32[]{:S(2)}, u32[]{:S(2)}) collective-permute-start(bf16[4,4096]{1,0:T(4,128)(2,1)S(1)} %add_convert_fusion), channel_id=1, source_target_pairs={{0,24},{1,29},{2,26},{3,31},{4,28},{5,25},{6,30},{7,27},{8,0},{9,5... | collective-permute-start | bytes 98312 | tf_op jit(solution)/shard_map/ppermute | solution.py:26
  22.8 1.4 %weight_gradient.5 = bf16[4096,896]{1,0:T(8,128)(2,1)} custom-call(bf16[16,4096]{1,0:T(8,128)(2,1)S(1)} %get-tuple-element.39.slots_ref, bf16[16,896]{1,0:T(8,128)(2,1)S(1)} %get-tuple-element.35.grad_ref, bf16[4096,896]{1,0:T(8,128)(2,1)} %weight_gradient.4.refs_0_), custom_call_target="tpu_custom_call", output_to_operand_aliasing={{}: (2, {})} | custom-call | flops 22020096 | bytes 1376256 | tf_op jit(solution)/shard_map/weight_gradient/pallas_call | solution.py:262
  24.2 0.4 %collective-permute-done.6.part_ref = bf16[4,4096]{1,0:T(4,128)(2,1)S(1)} collective-permute-done((bf16[4,4096]{1,0:T(4,128)(2,1)S(1)}, bf16[4,4096]{1,0:T(4,128)(2,1)S(1)}, u32[]{:S(2)}, u32[]{:S(2)}) %collective-permute-start.6) | collective-permute-done | bytes 32800 | tf_op jit(solution)/shard_map/ppermute | solution.py:26
  24.7 0.7 %collective-permute-start.7 = (bf16[2,4096]{1,0:T(2,128)(2,1)S(1)}, bf16[2,4096]{1,0:T(2,128)(2,1)S(1)}, u32[]{:S(2)}, u32[]{:S(2)}) collective-permute-start(bf16[2,4096]{1,0:T(2,128)(2,1)S(1)} %broadcast_select_fusion), channel_id=1, source_target_pairs={{0,1},{1,0},{2,3},{3,2},{4,5},{5,4},{6,7},{7,6},{8,9},{9,8},{10,11... | collective-permute-start | bytes 49160 | tf_op jit(solution)/shard_map/ppermute | solution.py:26
  25.4 0.8 %collective-permute-done.7.other_ref = bf16[2,4096]{1,0:T(2,128)(2,1)S(1)} collective-permute-done((bf16[2,4096]{1,0:T(2,128)(2,1)S(1)}, bf16[2,4096]{1,0:T(2,128)(2,1)S(1)}, u32[]{:S(2)}, u32[]{:S(2)}) %collective-permute-start.7) | collective-permute-done | bytes 16416 | tf_op jit(solution)/shard_map/ppermute | solution.py:26
  26.2 0.7 %close.1 = bf16[4,4096]{1,0:T(4,128)(2,1)} custom-call(bf16[4,4096]{1,0:T(4,128)(2,1)S(1)} %collective-permute-done.6.part_ref, bf16[2,4096]{1,0:T(2,128)(2,1)S(1)} %collective-permute-done.7.other_ref, f32[4,128]{1,0:T(4,128)S(1)} %get-tuple-element.42.pick_ref), custom_call_target="tpu_custom_call" | custom-call | tf_op jit(solution)/shard_map/close/pallas_call | solution.py:292
  (7 shorter events, 0.1 us)
Async XLA Ops:
  0.6 7.4 %slice-start = ((s8[7340032]{0:T(1024)(128)(4,1)}), s8[4194304]{0:T(1024)(128)(4,1)S(1)}, s32[]{:S(2)}) async-start(s8[7340032]{0:T(1024)(128)(4,1)} %bitcast.7), calls=%async_computation | async-start | bytes 8388608
  0.6 7.4 %slice-start.2 = ((s8[7340032]{0:T(1024)(128)(4,1)}), s8[4194304]{0:T(1024)(128)(4,1)S(1)}, s32[]{:S(2)}) async-start(s8[7340032]{0:T(1024)(128)(4,1)} %bitcast.12), calls=%async_computation.2 | async-start | bytes 8388608
  0.7 0.8 %copy-start.2 = (s32[4,32,2]{1,2,0:T(2,128)S(1)}, s32[4,32,2]{1,2,0:T(2,128)}, u32[]{:S(2)}) copy-start(s32[4,32,2]{1,2,0:T(2,128)} %param.9) | copy-start | bytes 3076
  0.7 1.6 %copy-start = (bf16[1,4,4096]{2,1,0:T(4,128)(2,1)S(1)}, bf16[1,4,4096]{2,1,0:T(4,128)(2,1)}, u32[]{:S(2)}) copy-start(bf16[1,4,4096]{2,1,0:T(4,128)(2,1)} %param.5) | copy-start | bytes 98308
  0.7 7.4 %slice-start.1 = ((s8[7340032]{0:T(1024)(128)(4,1)}), s8[3145728]{0:T(1024)(128)(4,1)S(1)}, s32[]{:S(2)}) async-start(s8[7340032]{0:T(1024)(128)(4,1)} %bitcast.7), calls=%async_computation.1 | async-start | bytes 6291456
  0.7 7.4 %slice-start.3 = ((s8[7340032]{0:T(1024)(128)(4,1)}), s8[3145728]{0:T(1024)(128)(4,1)S(1)}, s32[]{:S(2)}) async-start(s8[7340032]{0:T(1024)(128)(4,1)} %bitcast.12), calls=%async_computation.3 | async-start | bytes 6291456
  0.7 7.4 %copy-start.1 = (bf16[1,16,896]{2,1,0:T(8,128)(2,1)S(1)}, bf16[1,16,896]{2,1,0:T(8,128)(2,1)}, u32[]{:S(2)}) copy-start(bf16[1,16,896]{2,1,0:T(8,128)(2,1)} %param.6) | copy-start | bytes 86020
  0.7 1.6 %collective-permute-start = (bf16[4,4096]{1,0:T(4,128)(2,1)}, bf16[4,4096]{1,0:T(4,128)(2,1)S(1)}, u32[]{:S(2)}, u32[]{:S(2)}) collective-permute-start(bf16[4,4096]{1,0:T(4,128)(2,1)} %bitcast.16), channel_id=1, source_target_pairs={{0,1},{1,0},{2,3},{3,2},{4,5},{5,4},{6,7},{7,6},{8,9},{9,8},{10,11... | collective-permute-start | bytes 98312 | tf_op jit(solution)/shard_map/ppermute | solution.py:26
  2.5 6.7 %collective-permute-start.1 = (bf16[4,4096]{1,0:T(4,128)(2,1)S(1)}, bf16[4,4096]{1,0:T(4,128)(2,1)S(1)}, u32[]{:S(2)}, u32[]{:S(2)}) collective-permute-start(bf16[4,4096]{1,0:T(4,128)(2,1)S(1)} %pack.1.after_ref.refs_0_), channel_id=1, source_target_pairs={{0,2},{1,7},{2,0},{3,5},{4,6},{5,3},{6,4},{7,1},{8,10},{9,15},{10,... | collective-permute-start | bytes 98312 | tf_op jit(solution)/shard_map/ppermute | solution.py:26
  5.4 5.4 %collective-permute-start.2 = (bf16[4,4096]{1,0:T(4,128)(2,1)S(1)}, bf16[4,4096]{1,0:T(4,128)(2,1)S(1)}, u32[]{:S(2)}, u32[]{:S(2)}) collective-permute-start(bf16[4,4096]{1,0:T(4,128)(2,1)S(1)} %pack.1.after_ref.refs_0_), channel_id=1, source_target_pairs={{0,4},{1,5},{2,6},{3,7},{4,0},{5,1},{6,2},{7,3},{8,12},{9,13},{10,... | collective-permute-start | bytes 98312 | tf_op jit(solution)/shard_map/ppermute | solution.py:26
  9.1 1.7 %collective-permute-start.3 = (bf16[4,4096]{1,0:T(4,128)(2,1)S(1)}, bf16[4,4096]{1,0:T(4,128)(2,1)S(1)}, u32[]{:S(2)}, u32[]{:S(2)}) collective-permute-start(bf16[4,4096]{1,0:T(4,128)(2,1)S(1)} %collective-permute-done.1.after_ref.refs_2_), channel_id=1, source_target_pairs={{0,1},{1,0},{2,3},{3,2},{4,5},{5,4},{6,7},{7,6},{8,9},{9,8},{10,11... | collective-permute-start | bytes 98312 | tf_op jit(solution)/shard_map/ppermute | solution.py:26
  14.8 1.4 %collective-permute-start.4 = (f32[8,4096]{1,0:T(8,128)S(1)}, f32[8,4096]{1,0:T(8,128)S(1)}, u32[]{:S(2)}, u32[]{:S(2)}) collective-permute-start(f32[8,4096]{1,0:T(8,128)S(1)} %get-tuple-element.29), channel_id=1, source_target_pairs={{0,1},{1,0},{2,3},{3,2},{4,5},{5,4},{6,7},{7,6},{8,9},{9,8},{10,11... | collective-permute-start | bytes 393224 | tf_op jit(solution)/shard_map/ppermute | solution.py:26
  16.3 4.0 %collective-permute-start.5 = (bf16[4,4096]{1,0:T(4,128)(2,1)S(1)}, bf16[4,4096]{1,0:T(4,128)(2,1)S(1)}, u32[]{:S(2)}, u32[]{:S(2)}) collective-permute-start(bf16[4,4096]{1,0:T(4,128)(2,1)S(1)} %slice.22), channel_id=1, source_target_pairs={{0,2},{1,3},{2,0},{3,1},{4,6},{5,7},{6,4},{7,5},{8,10},{9,11},{10,... | collective-permute-start | bytes 98312 | tf_op jit(solution)/shard_map/ppermute | solution.py:26
  20.3 4.3 %collective-permute-start.6 = (bf16[4,4096]{1,0:T(4,128)(2,1)S(1)}, bf16[4,4096]{1,0:T(4,128)(2,1)S(1)}, u32[]{:S(2)}, u32[]{:S(2)}) collective-permute-start(bf16[4,4096]{1,0:T(4,128)(2,1)S(1)} %add_convert_fusion), channel_id=1, source_target_pairs={{0,24},{1,29},{2,26},{3,31},{4,28},{5,25},{6,30},{7,27},{8,0},{9,5... | collective-permute-start | bytes 98312 | tf_op jit(solution)/shard_map/ppermute | solution.py:26
  24.7 1.5 %collective-permute-start.7 = (bf16[2,4096]{1,0:T(2,128)(2,1)S(1)}, bf16[2,4096]{1,0:T(2,128)(2,1)S(1)}, u32[]{:S(2)}, u32[]{:S(2)}) collective-permute-start(bf16[2,4096]{1,0:T(2,128)(2,1)S(1)} %broadcast_select_fusion), channel_id=1, source_target_pairs={{0,1},{1,0},{2,3},{3,2},{4,5},{5,4},{6,7},{7,6},{8,9},{9,8},{10,11... | collective-permute-start | bytes 49160 | tf_op jit(solution)/shard_map/ppermute | solution.py:26
